TPU v7x, 32 devices: a whole 2x2x4 slice. The times are simulated.
32 devices in a mesh: img: 8 (over z, y), cls: 4 (over x, core).
Axes of the slice: x: 2, y: 2, z: 4, core: 2. Of those that a mesh axis runs over, the one named last changes fastest.
Arguments:
- patches: bfloat16 [16, 64, 18432], P('img', 'cls'), may hold values from -6 to 6
- boxes: int32 [16, 3, 4], P('img'), may hold values from 0 to 96, as said below
- match: int32 [16, 9, 6144], P('img'), may hold values from -2 to 15, as said below
- gt_labels: int32 [16, 16], P('img'), may hold values from 0 to 79
- gt_deltas: float32 [16, 16, 4], P('img'), may hold values from -4 to 4
- ema_old: float32 [], replicated, may hold values from 9830.4 to 39321.6
- shared_params: float32 [1378304], P(('img', 'cls'))
- shared_m: float32 [1378304], P(('img', 'cls')), may hold values from -0.0048828125 to 0.0048828125
- shared_v: float32 [1378304], P(('img', 'cls')), may hold values from 5.086263e-08 to 8.138021e-07
- class_params: float32 [2304, 720], P('img', 'cls'), may hold values from -0.125 to 0.125
- class_m: float32 [2304, 720], P('img', 'cls'), may hold values from -0.00048828125 to 0.00048828125
- class_v: float32 [2304, 720], P('img', 'cls'), may hold values from 5.086263e-10 to 8.138021e-09
Outputs:
- loss: float32 [], replicated
- ema: float32 [], replicated
- shared_new: float32 [1378304], P(('img', 'cls'))
- shared_m_new: float32 [1378304], P(('img', 'cls'))
- shared_v_new: float32 [1378304], P(('img', 'cls'))
- class_new: float32 [2304, 720], P('img', 'cls')
- class_m_new: float32 [2304, 720], P('img', 'cls')
- class_v_new: float32 [2304, 720], P('img', 'cls')
Inputs may be any that keep to these rules, and one draw needn't show every extreme that they name: `boxes`: crops of a canvas are disjoint; crop 0 covers every row of its canvas. `match`: -1 marks background, -2 an ignored anchor, other values the index of the matched ground-truth box.
All inputs are finite; a program needn't handle non-finite values.
Results may differ from a plain program's by a relative error of at most 0.011.
The roundings to bfloat16 on the way count: a program that leaves them out, or rounds other values in their place, can miss the bound.
Values may be sent and summed in bfloat16 or wider, within the bound.
A program may use at most 320 MiB of HBM per device.

v0:
```python
import jax
import jax.numpy as jnp
from jax import lax
from jax.sharding import PartitionSpec as P

C = 256
CLASSES = 80
ANCH = 9
PATCH = 192
BOX_OUT = 36
STEP = 5


PRIOR = -4.59511985013459
ALPHA = 0.25
HUBER = 1.0 / 9.0
EMA_KEEP = 0.9
RATE = 0.01
MOMENT_ONE = 0.5
MOMENT_TWO = 0.5
DECAY = 0.05
EPSILON = 1e-08


def padded_2(cells, sides, width):
    for axis, dim in sides:
        count = lax.axis_size(axis)
        ends = count - 1
        head = lax.slice_in_dim(cells, 0, width, axis=dim)
        tail = lax.slice_in_dim(cells, cells.shape[dim] - width, cells.shape[dim], axis=dim)
        cells = jnp.concatenate(
            [
                lax.ppermute(tail, axis, [(i, (i + 1) % count) for i in range(ends)]),
                cells,
                lax.ppermute(head, axis, [((i + 1) % count, i) for i in range(ends)]),
            ],
            axis=dim,
        )
    return cells


def crop_map(boxes, row_count, col_count):
    row_index = jnp.arange(row_count, dtype=jnp.int32)[:, None, None]
    col_index = jnp.arange(col_count, dtype=jnp.int32)[None, :, None]
    edges = boxes[..., None, None, :, :]
    inside = (
        (row_index >= edges[..., 0])
        & (row_index < edges[..., 2])
        & (col_index >= edges[..., 1])
        & (col_index < edges[..., 3])
    )
    number = jnp.arange(boxes.shape[-2], dtype=jnp.int32)
    return jnp.max(jnp.where(inside, number, -1), axis=-1)


def unpack(flat_values):
    lengths = [PATCH * C, C, C * C, C, 18 * C * C, 2 * C, 9 * C * BOX_OUT]
    pieces = []
    offset = 0
    for length in lengths:
        pieces.append(flat_values[offset : offset + length])
        offset = offset + length
    return (
        pieces[0].reshape(PATCH, C),
        pieces[1],
        pieces[2].reshape(C, C),
        pieces[3],
        pieces[4].reshape(2, 9, C, C),
        pieces[5].reshape(2, C),
        pieces[6].reshape(9, C, BOX_OUT),
    )


def pick_label(table, index):
    return table[index]


def pick_delta(table, index):
    return table[index]


def targets(crop_ids, match, labels, deltas):
    valid = (crop_ids >= 0)[..., None]
    positive = (match >= 0) & valid
    counted = (match != -2) & valid
    safe_index = jnp.maximum(match, 0)
    matched_label = jax.vmap(pick_label)(labels, safe_index)
    matched_label = jnp.where(positive, matched_label, -1)
    box_target = jax.vmap(pick_delta)(deltas, safe_index)
    box_target = jnp.where((match >= 0)[..., None], box_target, jnp.zeros((), jnp.float32))
    return (
        positive,
        counted,
        matched_label,
        box_target.reshape(box_target.shape[:-2] + (4 * ANCH,)),
    )


def focal_sum(logit_in, target, weighting):
    prob = jax.nn.sigmoid(logit_in)
    cross = jax.nn.softplus(logit_in) - target * logit_in
    miss = prob + target - 2.0 * prob * target
    balance = ALPHA * target + (1.0 - ALPHA) * (1.0 - target)
    return jnp.sum(weighting * balance * miss * miss * cross)


def huber_sum(differ, weighting):
    magnitude = jnp.abs(differ)
    return jnp.sum(
        weighting
        * jnp.where(magnitude < HUBER, 0.5 * differ * differ / HUBER, magnitude - 0.5 * HUBER)
    )


def pad_cols(values):
    return jnp.pad(values, ((0, 0), (0, 0), (1, 1), (0, 0)))


def masked_slice(padded, ids_pad, row_count, col_count, row_start, col_start):
    center = ids_pad[:, 1 : row_count + 1, 1 : col_count + 1]
    same = (
        ids_pad[:, row_start : row_start + row_count, col_start : col_start + col_count] == center
    ) & (center >= 0)
    return jnp.where(
        same[..., None],
        padded[:, row_start : row_start + row_count, col_start : col_start + col_count],
        jnp.zeros((), padded.dtype),
    )


def conv_apply(padded, taps, ids_pad, row_count, flip):
    col_count = padded.shape[2] - 2
    summed = None
    for row_tap in range(3):
        for col_tap in range(3):
            weight = taps[row_tap * 3 + col_tap]
            if flip:
                masked_in = masked_slice(
                    padded, ids_pad, row_count, col_count, 2 - row_tap, 2 - col_tap
                )
                term = lax.dot_general(
                    masked_in, weight, (((3,), (1,)), ((), ())), preferred_element_type=jnp.float32
                )
            else:
                masked_in = masked_slice(padded, ids_pad, row_count, col_count, row_tap, col_tap)
                term = lax.dot_general(
                    masked_in, weight, (((3,), (0,)), ((), ())), preferred_element_type=jnp.float32
                )
            summed = term if summed is None else summed + term
    return summed


def conv_grad(padded, grad_out, ids_pad, row_count):
    col_count = padded.shape[2] - 2
    terms = []
    for row_tap in range(3):
        for col_tap in range(3):
            masked_in = masked_slice(padded, ids_pad, row_count, col_count, row_tap, col_tap)
            terms.append(
                lax.dot_general(
                    masked_in,
                    grad_out,
                    (((0, 1, 2), (0, 1, 2)), ((), ())),
                    preferred_element_type=jnp.float32,
                )
            )
    return jnp.stack(terms)


def gelu_back(pre_values, grad):
    return jax.vjp(jax.nn.gelu, pre_values)[1](grad)[0]


def adamw_update(weight, first, second, grad):
    first_new = MOMENT_ONE * first + (1.0 - MOMENT_ONE) * grad
    second_new = MOMENT_TWO * second + (1.0 - MOMENT_TWO) * grad * grad
    first_hat = first_new / (1.0 - MOMENT_ONE**STEP)
    second_hat = second_new / (1.0 - MOMENT_TWO**STEP)
    weight_new = weight - RATE * (first_hat / (jnp.sqrt(second_hat) + EPSILON) + DECAY * weight)
    return (weight_new, first_new, second_new)


def local(
    patches,
    boxes,
    match,
    gt_labels,
    gt_deltas,
    ema_old,
    shared_params,
    shared_m,
    shared_v,
    class_params,
    class_m,
    class_v,
):
    cls_parts = lax.axis_size("cls")
    cls_rank = lax.axis_index("cls")
    all_weights = lax.all_gather(
        shared_params.astype(jnp.bfloat16), ("img", "cls"), axis=0, tiled=True
    )
    class_rows = lax.all_gather(class_params.astype(jnp.bfloat16), "img", axis=0, tiled=True)
    stem_w, stem_b, lat_w, lat_b, tower_w, tower_b, box_w = unpack(all_weights)
    canvas_count, row_count, merged_width = patches.shape
    patch_width = PATCH
    col_count = merged_width // patch_width
    full_rows = row_count * cls_parts
    first_row = cls_rank * row_count
    match_cells = jnp.transpose(
        match.reshape(canvas_count, match.shape[1], full_rows, col_count), (0, 2, 3, 1)
    )
    crop_ids = crop_map(boxes, full_rows, col_count)
    ids_wide = jnp.pad(crop_ids, ((0, 0), (2, 2), (1, 1)), constant_values=-1)
    ids_near = lax.dynamic_slice_in_dim(ids_wide, first_row, row_count + 4, 1)
    ids_mid = ids_near[:, 1 : row_count + 3]
    ids_all = ids_wide[:, 1 : full_rows + 3]
    patch_rows = patches.reshape(-1, patch_width)
    stem_pre = jnp.dot(patch_rows, stem_w, preferred_element_type=jnp.float32) + stem_b
    stem_out = jax.nn.gelu(stem_pre).astype(jnp.bfloat16)
    feature = (jnp.dot(stem_out, lat_w, preferred_element_type=jnp.float32) + lat_b).astype(
        jnp.bfloat16
    )
    feature = feature.reshape(canvas_count, row_count, col_count, C)
    feature_pad = pad_cols(padded_2(feature, (("cls", 1),), 2))
    feature_mid = feature_pad[:, 1 : row_count + 3]
    class_pre = conv_apply(feature_mid, tower_w[0], ids_mid, row_count, False) + tower_b[0]
    box_pre = conv_apply(feature_pad, tower_w[1], ids_near, row_count + 2, False) + tower_b[1]
    class_tower = jax.nn.gelu(class_pre).astype(jnp.bfloat16)
    box_tower = pad_cols(jax.nn.gelu(box_pre).astype(jnp.bfloat16))
    predicted = conv_apply(box_tower, box_w, ids_mid, row_count, False)
    positive, counted, matched_label, box_target = targets(
        crop_ids, match_cells, gt_labels, gt_deltas
    )
    class_taps = class_rows.reshape(9, C, class_rows.shape[-1])
    class_full = lax.all_gather(class_tower, "cls", axis=1, tiled=True)
    tower_pad = jnp.pad(class_full, ((0, 0), (1, 1), (1, 1), (0, 0)))
    logits = conv_apply(tower_pad, class_taps, ids_all, full_rows, False) + PRIOR
    column = cls_rank * logits.shape[-1] + jnp.arange(logits.shape[-1], dtype=jnp.int32)
    anchor_pick = (column // CLASSES == jnp.arange(ANCH, dtype=jnp.int32)[:, None]).astype(
        jnp.bfloat16
    )
    label_column = jnp.einsum(
        "brwa,ac->brwc",
        matched_label.astype(jnp.bfloat16),
        anchor_pick,
        preferred_element_type=jnp.float32,
    )
    class_target = (label_column == (column % CLASSES).astype(jnp.float32)).astype(jnp.float32)
    class_weight = jnp.einsum(
        "brwa,ac->brwc",
        counted.astype(jnp.bfloat16),
        anchor_pick,
        preferred_element_type=jnp.float32,
    )
    positive_own = lax.dynamic_slice_in_dim(positive, first_row, row_count, 1)
    box_own = lax.dynamic_slice_in_dim(box_target, first_row, row_count, 1)
    box_weight = jnp.repeat(positive_own, 4, axis=-1).astype(jnp.float32)
    focal_local, focal_pull = jax.vjp(
        lambda logit_in: focal_sum(logit_in, class_target, class_weight), logits
    )
    huber_local, huber_pull = jax.vjp(
        lambda guess: huber_sum(guess - box_own, box_weight), predicted
    )
    positives = lax.psum(jnp.sum(positive.astype(jnp.float32)), "img")
    focal_total, huber_total = lax.psum((focal_local, huber_local), ("img", "cls"))
    ema_new = EMA_KEEP * ema_old + (1.0 - EMA_KEEP) * jnp.maximum(positives, 1.0)
    box_norm = jnp.maximum(positives, 1.0)
    loss_value = focal_total / ema_new + huber_total / box_norm
    logit_grad = focal_pull(1.0 / ema_new)[0].astype(jnp.bfloat16)
    guess_grad = huber_pull(1.0 / box_norm)[0].astype(jnp.bfloat16)
    logit_pad = jnp.pad(logit_grad, ((0, 0), (1, 1), (1, 1), (0, 0)))
    class_in_part = conv_apply(logit_pad, class_taps, ids_all, full_rows, True)
    class_in_whole = lax.psum(class_in_part, "cls")
    class_in_grad = lax.dynamic_slice_in_dim(class_in_whole, first_row, row_count, 1)
    class_head_grad = conv_grad(tower_pad, logit_grad, ids_all, full_rows).reshape(9 * C, -1)
    class_grad = lax.psum_scatter(class_head_grad, "img", scatter_dimension=0, tiled=True)
    guess_rim = pad_cols(padded_2(guess_grad, (("cls", 1),), 1))
    box_in_grad = conv_apply(guess_rim, box_w, ids_mid, row_count, True)
    box_head_grad = conv_grad(box_tower, guess_grad, ids_mid, row_count)
    class_pre_grad = gelu_back(class_pre, class_in_grad).astype(jnp.bfloat16)
    box_pre_grad = gelu_back(box_pre[:, 1 : row_count + 1], box_in_grad).astype(jnp.bfloat16)
    both_grads = jnp.concatenate([class_pre_grad, box_pre_grad], axis=-1)
    both_rim = pad_cols(padded_2(both_grads, (("cls", 1),), 1))
    feature_grad = conv_apply(both_rim[..., :C], tower_w[0], ids_mid, row_count, True) + conv_apply(
        both_rim[..., C:], tower_w[1], ids_mid, row_count, True
    )
    tower_grad = jnp.stack(
        [
            conv_grad(feature_mid, class_pre_grad, ids_mid, row_count),
            conv_grad(feature_mid, box_pre_grad, ids_mid, row_count),
        ]
    )
    tower_bias_grad = jnp.stack(
        [
            jnp.sum(class_pre_grad, axis=(0, 1, 2), dtype=jnp.float32),
            jnp.sum(box_pre_grad, axis=(0, 1, 2), dtype=jnp.float32),
        ]
    )
    feature_low = feature_grad.astype(jnp.bfloat16).reshape(-1, C)
    lat_grad = lax.dot_general(
        stem_out, feature_low, (((0,), (0,)), ((), ())), preferred_element_type=jnp.float32
    )
    lat_bias_grad = jnp.sum(feature_low, axis=0, dtype=jnp.float32)
    stem_out_grad = lax.dot_general(
        feature_low, lat_w, (((1,), (1,)), ((), ())), preferred_element_type=jnp.float32
    )
    stem_pre_grad = gelu_back(stem_pre, stem_out_grad).astype(jnp.bfloat16)
    stem_grad = lax.dot_general(
        patch_rows, stem_pre_grad, (((0,), (0,)), ((), ())), preferred_element_type=jnp.float32
    )
    stem_bias_grad = jnp.sum(stem_pre_grad, axis=0, dtype=jnp.float32)
    flat_grad = jnp.concatenate(
        [
            stem_grad.reshape(-1),
            stem_bias_grad,
            lat_grad.reshape(-1),
            lat_bias_grad,
            tower_grad.reshape(-1),
            tower_bias_grad.reshape(-1),
            box_head_grad.reshape(-1),
        ]
    )
    shared_grad = lax.psum_scatter(flat_grad, ("img", "cls"), scatter_dimension=0, tiled=True)
    shared_new, shared_m_new, shared_v_new = adamw_update(
        shared_params, shared_m, shared_v, shared_grad
    )
    class_new, class_m_new, class_v_new = adamw_update(class_params, class_m, class_v, class_grad)
    return (
        loss_value,
        ema_new,
        shared_new,
        shared_m_new,
        shared_v_new,
        class_new,
        class_m_new,
        class_v_new,
    )


def solution(mesh):
    placed = (
        P("img", "cls", None),
        P("img", None, None),
        P("img", None, None),
        P("img", None),
        P("img", None, None),
        P(),
        P(("img", "cls")),
        P(("img", "cls")),
        P(("img", "cls")),
        P("img", "cls"),
        P("img", "cls"),
        P("img", "cls"),
    )
    return jax.shard_map(
        local,
        mesh=mesh,
        in_specs=placed,
        out_specs=(
            P(),
            P(),
            P(("img", "cls")),
            P(("img", "cls")),
            P(("img", "cls")),
            P("img", "cls"),
            P("img", "cls"),
            P("img", "cls"),
        ),
        check_vma=False,
    )
```

profile of v0, /device:TPU:0, one launch (start us, length us, event | category | flops | bytes accessed | tf_op | source)
XLA Modules:
  0.0 3260.5 jit_solution(15356272991598240388)
XLA Ops:
  23.2 6.1 shift-left_or_fusion
  29.2 6.0 reshape.410
  36.6 24.0 psum.29
  63.8 1186.8 %gather_fusion.1 = f32[110592,4]{1,0:T(8,128)} fusion(f32[2,16,4]{2,1,0:T(8,128)S(1)} %copy.186, s32[110592]{0:T(1024)S(1)} %reshape.410), kind=kCustom, calls=%fused_computation.1 | custom fusion | bytes 4423680 | tf_op jit(solution)/shard_map/vmap()/gather | solution.py:79
  1250.6 29.9 copy.187
  1280.5 47.7 %reshape.419 = f32[2,64,96,9,4]{3,2,1,0,4:T(8,128)} reshape(f32[110592,4]{0,1:T(4,128)S(1)} %copy.187) | data formatting | bytes 3538944 | tf_op jit(solution)/shard_map/vmap()/gather | solution.py:79
  1328.2 18.2 broadcast_select_fusion
  1346.3 33.7 %all-gather = bf16[8,288,180]{1,2,0:T(8,128)(2,1)S(1)} all-gather(bf16[1,288,180]{1,2,0:T(8,128)(2,1)S(1)} %copy-done.67), channel_id=1, replica_groups=mesh['img'=8,'cls'=4] {'img'}, dimensions={0}, use_global_device_ids=true | all-gather | bytes 933120 | tf_op jit(solution)/shard_map/all_gather | solution.py:202
  1382.0 923.2 %gather_fusion = s32[110592]{0:T(1024)S(1)} fusion(s32[2,16]{1,0:T(2,128)S(1)} %copy-done, s32[110592]{0:T(1024)S(1)} %reshape.410), kind=kCustom, calls=%fused_computation | custom fusion | bytes 1769472 | tf_op jit(solution)/shard_map/vmap()/gather | solution.py:75
  2305.2 7.5 reshape.413
  2312.8 4.6 copy.173
  2319.8 15.5 copy.188
  2395.1 7.2 multiply_convert_fusion
  2419.8 8.7 fusion.87
  2446.3 6.1 collective-permute-start.2
  2486.5 7.4 convert_reduce_fusion
  2508.0 9.6 fusion.60
  2517.5 7.4 fusion.62
  2524.9 7.7 fusion.64
  2532.6 7.3 fusion.66
  2539.8 7.2 fusion.68
  2547.1 7.3 fusion.70
  2554.4 7.4 fusion.72
  2561.8 7.3 fusion.74
  2569.1 38.0 %fusion.127 = (u8[64,96,180]{1,2,0:T(8,128)(4,1)S(1)}, f32[2,64,96,180]{2,3,1,0:T(8,128)}) fusion(f32[2,64,96,180]{2,3,1,0:T(8,128)} %fusion.74, f32[2,64,96,180]{2,3,1,0:T(8,128)} %fusion.72, f32[2,64,96,180]{2,3,1,0:T(8,128)} %fusion.70, f32[2,64,96,180]{2,3,1,0:T(8,128)} %fusion.68, bf16[2304,180]{0,1:T(8,128)(2,1)S(1)} %copy-done.25, ...), kind=kOutput, calls=%fused_computation.177 | convolution fusion | flops 1165467648 | bytes 87134208 | tf_op jit(solution)/shard_map/dot_general | solution.py:146
  2607.1 34.8 %fusion.6 = (bf16[2,64,96,180]{2,3,1,0:T(8,128)(2,1)S(1)}, f32[]{:T(128)}) fusion(f32[2,64,96,180]{2,3,1,0:T(8,128)} %get-tuple-element.136, f32[]{:T(128)S(6)} %div.54, u8[64,96,180]{1,2,0:T(8,128)(4,1)S(1)} %get-tuple-element.135, u8[64,96,180]{1,2,0:T(8,128)(4,1)} %fusion.137, s32[180]{0:T(256)S(1)} %copy-done.167, ...), kind=kOutput, calls=%fused_computation.15 | convolution fusion | flops 161576528 | bytes 15606488 | tf_op jit(solution)/shard_map/brwa,ac->brwc/dot_general | solution.py:249
  2641.9 6.3 fusion.25
  2648.2 7.5 fusion.28
  2655.7 7.7 fusion.31
  2663.3 6.7 fusion.34
  2670.1 7.4 fusion.36
  2677.5 7.8 fusion.39
  2685.3 5.8 fusion.42
  2691.1 7.9 fusion.45
  2699.0 38.6 %add_add_fusion = f32[2,64,96,256]{3,2,1,0:T(8,128)} fusion(f32[2,64,96,256]{3,2,1,0:T(8,128)} %fusion.25, f32[2,64,96,256]{3,2,1,0:T(8,128)} %fusion.28, f32[2,64,96,256]{3,2,1,0:T(8,128)} %fusion.31, f32[2,64,96,256]{3,2,1,0:T(8,128)} %fusion.34, f32[2,64,96,256]{3,2,1,0:T(8,128)} %fusion.36, f32[2,64,96,256]{3,2,1,0:T(8,128)} %fusion.39, ...), kind=kOutput, calls=%fused_computation.7 | convolution fusion | flops 1159839744 | bytes 117780480 | tf_op jit(solution)/shard_map/dot_general | solution.py:141
  2737.7 8.6 fusion.286
  2746.3 8.6 fusion.284
  2754.9 8.2 fusion.282
  2763.2 4.3 fusion.280
  2767.5 4.8 fusion.288
  2772.3 4.3 fusion.278
  2776.6 4.5 fusion.276
  2792.1 164.9 %all-reduce.14.cloned.1.call-done = f32[2,64,96,256]{3,2,1,0:T(8,128)} async-done(((f32[2,64,96,256]{3,2,1,0:T(8,128)}), f32[2,64,96,256]{3,2,1,0:T(8,128)}) %all-reduce.14.cloned.1.call-update) | async-done | bytes 12582928 | tf_op jit(solution)/shard_map/psum | solution.py:273
  2972.9 4.6 copy.319
  3020.4 19.7 convert_reduce_fusion.2
  3052.8 41.1 %dynamic-update-slice.14 = f32[1378304]{0:T(1024)} dynamic-update-slice(f32[1378304]{0:T(1024)} %constant_dynamic-update-slice_fusion.3, f32[1179648]{0:T(1024)} %bitcast.623, s32[]{} %constant.195) | dynamic-update-slice | bytes 9437188
  3097.2 43.1 %all-reduce.9 = (f32[]{:T(128)}, f32[]{:T(128)}) all-reduce(f32[]{:T(128)} %get-tuple-element.57, f32[]{:T(128)} %get-tuple-element.97), channel_id=1, replica_groups=mesh['img'=8,'cls'=4] {'img','cls'}, use_global_device_ids=true, to_apply=%region_2.3 | all-reduce | flops 2 | bytes 16 | tf_op jit(solution)/shard_map/psum | solution.py:265
  3145.5 104.2 %all-reduce.18.cloned.1.call-done = f32[1378304]{0:T(1024)} async-done(((f32[1378304]{0:T(1024)}), f32[1378304]{0:T(1024)}) %all-reduce.18.cloned.1.call-update) | async-done | bytes 5513232
  (551 shorter events, 256.5 us)
Async XLA Ops:
  7.2 1374.9 %copy-start = (s32[2,16]{1,0:T(2,128)S(1)}, s32[2,16]{1,0:T(2,128)}, u32[]{:S(2)}) copy-start(s32[2,16]{1,0:T(2,128)} %param.15) | copy-start | bytes 388
  7.2 2335.3 %all-reduce.16.cloned.1.call-start = ((), (), s32[]{:S(2)}) async-start(), calls=%async_computation.4 | async-start | bytes 5513216
  11.0 2496.9 %all-gather.3.cloned.1.call-start = ((), (), s32[]{:S(2)}) async-start(), calls=%async_computation.1 | async-start | bytes 7864320 | tf_op jit(solution)/shard_map/all_gather | solution.py:235
  18.0 17.2 copy-start.95
  29.2 34.5 %copy-start.165 = (f32[2,16,4]{1,2,0:T(4,128)S(1)}, f32[2,16,4]{1,2,0:T(4,128)}, u32[]{:S(2)}) copy-start(f32[2,16,4]{1,2,0:T(4,128)} %param.16) | copy-start | bytes 1540
  1328.2 18.2 copy-start.67
  2319.8 15.5 copy-start.64
  2319.8 16.2 copy-start.59
  2336.7 136.5 %copy-start.118 = (pred[2,16,96]{2,1,0:T(8,128)(4,1)}, pred[2,16,96]{2,1,0:T(8,128)(4,1)S(1)}, u32[]{:S(2)}) copy-start(pred[2,16,96]{2,1,0:T(8,128)(4,1)S(1)} %get-tuple-element.127) | copy-start | bytes 9220
  2336.7 149.8 %copy-start.116 = (pred[2,16,96]{2,1,0:T(8,128)(4,1)}, pred[2,16,96]{2,1,0:T(8,128)(4,1)S(1)}, u32[]{:S(2)}) copy-start(pred[2,16,96]{2,1,0:T(8,128)(4,1)S(1)} %get-tuple-element.123) | copy-start | bytes 9220
  2336.7 157.2 %copy-start.120 = (pred[2,16,96]{2,1,0:T(8,128)(4,1)}, pred[2,16,96]{2,1,0:T(8,128)(4,1)S(1)}, u32[]{:S(2)}) copy-start(pred[2,16,96]{2,1,0:T(8,128)(4,1)S(1)} %get-tuple-element.121) | copy-start | bytes 9220
  2336.7 161.0 %copy-start.122 = (pred[2,16,96]{2,1,0:T(8,128)(4,1)}, pred[2,16,96]{2,1,0:T(8,128)(4,1)S(1)}, u32[]{:S(2)}) copy-start(pred[2,16,96]{2,1,0:T(8,128)(4,1)S(1)} %get-tuple-element.124) | copy-start | bytes 9220
  2348.8 12.7 copy-start.88
  2350.4 148.5 %copy-start.8 = (bf16[3072,256]{1,0:T(8,128)(2,1)}, bf16[3072,256]{1,0:T(8,128)(2,1)S(1)}, u32[]{:S(2)}) copy-start(bf16[3072,256]{1,0:T(8,128)(2,1)S(1)} %fusion.76) | copy-start | bytes 4718596
  2350.4 16.0 copy-start.87
  2350.4 16.7 copy-start.86
  2350.4 17.4 copy-start.85
  2350.4 18.1 copy-start.84
  2350.4 18.8 copy-start.83
  2350.4 19.5 copy-start.82
  2350.4 29.7 copy-start.128
  2351.2 31.5 collective-permute-start
  2352.6 30.1 collective-permute-start.1
  2354.0 30.1 copy-start.41
  2355.0 29.7 copy-start.43
  2363.1 19.6 copy-start.51
  2387.0 116.3 %copy-start.3 = (bf16[2,20,96,256]{3,2,1,0:T(8,128)(2,1)}, bf16[2,20,96,256]{3,2,1,0:T(8,128)(2,1)S(1)}, u32[]{:S(2)}) copy-start(bf16[2,20,96,256]{3,2,1,0:T(8,128)(2,1)S(1)} %pad_maximum_fusion.3) | copy-start | bytes 5898244
  2402.3 554.7 %all-reduce.14.cloned.1.call-start = ((), (), s32[]{:S(2)}) async-start(), calls=%async_computation.2 | async-start | bytes 25165824 | tf_op jit(solution)/shard_map/psum | solution.py:273
  2444.3 20.7 copy-start.22
  2445.0 26.9 collective-permute-start.3
  2446.3 25.6 collective-permute-start.2
  2493.9 10.5 copy-start.5
  2569.1 38.0 %copy-start.113 = (pred[2,9,64,96]{3,2,0,1:T(32,128)(4,1)S(1)}, pred[2,9,64,96]{3,2,0,1:T(32,128)(4,1)}, u32[]{:S(2)}) copy-start(pred[2,9,64,96]{3,2,0,1:T(32,128)(4,1)} %ne.54) | copy-start | bytes 331780
  2569.1 38.0 %copy-start.167 = (s32[180]{0:T(256)S(1)}, s32[180]{0:T(256)}, u32[]{:S(2)}) copy-start(s32[180]{0:T(256)} %copy-done.166) | copy-start | bytes 2164
  2641.9 49.2 %copy-start.2 = (bf16[2,64,96,180]{2,3,1,0:T(8,128)(2,1)}, bf16[2,64,96,180]{2,3,1,0:T(8,128)(2,1)S(1)}, u32[]{:S(2)}) copy-start(bf16[2,64,96,180]{2,3,1,0:T(8,128)(2,1)S(1)} %get-tuple-element.56) | copy-start | bytes 13271044
  2737.6 404.1 %reduce-scatter.2.cloned.1.call-start = ((), (), s32[]{:S(2)}) async-start(), calls=%async_computation.3 | async-start | bytes 2654208 | tf_op jit(solution)/shard_map/reduce_scatter | solution.py:276
  2746.3 16.8 slice-start
  2746.3 16.9 slice-start.2
  2789.0 168.1 %copy-start.19 = (f32[2,16,96,256]{3,2,1,0:T(8,128)S(1)}, f32[2,16,96,256]{3,2,1,0:T(8,128)}, u32[]{:S(2)}) copy-start(f32[2,16,96,256]{3,2,1,0:T(8,128)} %get-tuple-element.134) | copy-start | bytes 9437188
  2792.1 457.5 %all-reduce.18.cloned.1.call-start = ((), (), s32[]{:S(2)}) async-start(), calls=%async_computation.5 | async-start | bytes 11026432
  2977.5 7.0 collective-permute-start.5
  2978.8 5.7 collective-permute-start.4
  2986.4 22.0 copy-start.7
  3052.8 42.4 %copy-start.35 = (f32[82944]{0:T(1024)S(1)}, f32[82944]{0:T(1024)}, u32[]{:S(2)}) copy-start(f32[82944]{0:T(1024)} %reshape.408) | copy-start | bytes 995332
  3096.0 153.7 %copy-start.65 = (f32[43072]{0:T(1024)S(1)}, f32[43072]{0:T(1024)}, u32[]{:S(2)}) copy-start(f32[43072]{0:T(1024)} %param.18) | copy-start | bytes 516868
  3096.0 153.6 %copy-start.110 = (f32[43072]{0:T(1024)S(1)}, f32[43072]{0:T(1024)}, u32[]{:S(2)}) copy-start(f32[43072]{0:T(1024)} %param.19) | copy-start | bytes 516868
  3096.0 153.6 %copy-start.111 = (f32[43072]{0:T(1024)S(1)}, f32[43072]{0:T(1024)}, u32[]{:S(2)}) copy-start(f32[43072]{0:T(1024)} %param.20) | copy-start | bytes 516868
  3096.0 155.5 %copy-start.1 = (s32[2,16]{1,0:T(2,128)S(1)}, s32[2,16]{1,0:T(2,128)}, u32[]{:S(2)}) copy-start(s32[2,16]{1,0:T(2,128)} %param.15) | copy-start | bytes 388
  (136 other events, 425.5 us)
Sparse Core Ops, SparseCore 0:
  13.5 138.4 all-reduce.15
  2402.5 47.3 all-gather.2
  2737.7 219.2 all-reduce.13
  2960.4 69.3 reduce-scatter.1
  3096.1 153.4 all-reduce.17
where the time goes:
time: 3270 us; the launch traced here: 3260 us
  local copies, waits for them, and re-layouts  2340 us (72%)
  matrix products  464 us (14%)
  waiting for transfers between devices  269 us (8%)
  blocking collectives  101 us (3%)
  other arithmetic  46.6 us (1%)
    gather x3, local copies, waits for them, and re-layouts, pick_delta(): return table[index]  1260 us
    gather x5, local copies, waits for them, and re-layouts, pick_label(): return table[index]  945 us
    dot_general x36, matrix products, conv_apply(): lax.dot_general(masked_in, weight, (((3,), (1,)), ((), ())), preferred_el...  177 us
    psum x1, waiting for transfers between devices, local(): class_in_whole = lax.psum(class_in_part, 'cls')  165 us
    dot_general x36, matrix products, conv_apply(): lax.dot_general(masked_in, weight, (((3,), (0,)), ((), ())), preferred_el...  157 us
    unnamed x7, waiting for transfers between devices  104 us
    dot_general x36, matrix products, conv_grad(): lax.dot_general(masked_in, grad_out, (((0, 1, 2), (0, 1, 2)), ((), ())),...  81.7 us
    unnamed x364, local copies, waits for them, and re-layouts  67.4 us
  transfers between devices with their start and end apart: 11, of which 2 were waited for; matrix products, arithmetic and copies ran while one was open for 79% of the time, Pallas kernels for 0%

commit v1 on v0

v1 whole, which is shorter than its diff:
```python
import functools

import jax
import jax.numpy as jnp
from jax import lax
from jax.experimental import pallas as pl
from jax.experimental.pallas import tpu as pltpu
from jax.sharding import PartitionSpec as P

C = 256
CLASSES = 80
ANCH = 9
PATCH = 192
BOX_OUT = 36
CLS_OUT = ANCH * CLASSES
STEP = 5
GT = 16
HALO = 4
SLOT = 16
BOX_ROWS = 4 * SLOT
LANE = 128
WIDE = 768

PRIOR = -4.59511985013459
ALPHA = 0.25
HUBER = 1.0 / 9.0
EMA_KEEP = 0.9
RATE = 0.01
MOMENT_ONE = 0.5
MOMENT_TWO = 0.5
DECAY = 0.05
EPSILON = 1e-08

BF = jnp.bfloat16
F32 = jnp.float32
TAPS = [(di, dj) for di in (-1, 0, 1) for dj in (-1, 0, 1)]
NN = (((1,), (0,)), ((), ()))
NT = (((1,), (1,)), ((), ()))
TN = (((0,), (0,)), ((), ()))
K0 = 0.7978845608028654
K1 = 0.044715


def mm(a, b, dims=NN):
    return lax.dot_general(a, b, dims, preferred_element_type=F32)


def gelu(x):
    return 0.5 * x * (1.0 + jnp.tanh(K0 * (x + K1 * x * x * x)))


def gelu_slope(x):
    square = x * x
    th = jnp.tanh(K0 * (x + K1 * x * square))
    return 0.5 * (1.0 + th) + (0.5 * K0) * x * (1.0 - th * th) * (1.0 + 3.0 * K1 * square)


def columns_of(x, pairs, width):
    return [x[:, width * k : width * (k + 1)] for k in range(pairs)]


def stem_kernel(pairs, cols, rows, x_ref, h_ref, w_ref, b_ref, lw_ref, lb_ref, pre_ref, so_ref, f_ref, t_ref):
    step = pl.program_id(0)
    canvases = x_ref.shape[0]
    own_rows = canvases * rows
    total = (rows + 2 * HALO) * cols

    @pl.when(step == 0)
    def _():
        for c in range(canvases):
            for n in range(2):
                t_ref[c, n, 0:8, :] = jnp.zeros((8, LANE), F32)
                t_ref[c, n, 8 + total : 16 + total, :] = jnp.zeros((8, LANE), F32)

    x = x_ref[...].reshape(own_rows, x_ref.shape[2])
    own = columns_of(x, pairs, 2 * PATCH)
    rim = columns_of(h_ref[...], pairs, 2 * PATCH)
    pre = mm(jnp.concatenate(own + rim, axis=0), w_ref[...]) + b_ref[...]
    count = pairs * own_rows
    pre_ref[...] = pre[:count]
    out = gelu(pre).astype(BF)
    so_ref[...] = out[:count]
    for half in range(2):
        feat = mm(out[:, half * C : half * C + C], lw_ref[...]) + lb_ref[...]
        for k in range(pairs):
            j = step * 2 * pairs + 2 * k + half
            for c in range(canvases):
                at = k * own_rows + c * rows
                rim_at = count + k * 2 * HALO * canvases + c * 2 * HALO
                for n in range(2):
                    side = slice(n * LANE, n * LANE + LANE)
                    place = pl.ds(8 + HALO * cols + j, rows, stride=cols)
                    t_ref[c, n, place, :] = feat[at : at + rows, side]
                    place = pl.ds(8 + j, HALO, stride=cols)
                    t_ref[c, n, place, :] = feat[rim_at : rim_at + HALO, side]
                    place = pl.ds(8 + (HALO + rows) * cols + j, HALO, stride=cols)
                    t_ref[c, n, place, :] = feat[rim_at + HALO : rim_at + 2 * HALO, side]

    @pl.when(step == pl.num_programs(0) - 1)
    def _():
        piece = 4 * cols

        def move(i, carry):
            base = pl.multiple_of(i * piece, 16)
            for c in range(canvases):
                for n in range(2):
                    value = t_ref[c, n, pl.ds(base, piece + 16), :]
                    for k in range(3):
                        moved = value[7 + k : 7 + k + piece].astype(BF)
                        f_ref[c, k, pl.ds(base, piece), n * LANE : n * LANE + LANE] = moved
            return carry

        lax.fori_loop(0, total // piece, move, 0)


def stem_back_kernel(pairs, cols, rows, x_ref, fg_ref, so_ref, pre_ref, lw_ref, sw_out, sb_out, lw_out, lb_out):
    step = pl.program_id(0)
    canvases = x_ref.shape[0]

    @pl.when(step == 0)
    def _():
        sw_out[...] = jnp.zeros_like(sw_out)
        sb_out[...] = jnp.zeros_like(sb_out)
        lw_out[...] = jnp.zeros_like(lw_out)
        lb_out[...] = jnp.zeros_like(lb_out)

    x = x_ref[...].reshape(canvases * rows, x_ref.shape[2])
    own = jnp.concatenate(columns_of(x, pairs, 2 * PATCH), axis=0)
    low = []
    for half in range(2):
        parts = []
        for k in range(pairs):
            j = step * 2 * pairs + 2 * k + half
            for c in range(canvases):
                place = pl.ds(j, rows, stride=cols)
                parts.append(jnp.concatenate([fg_ref[c, n, place, :] for n in range(2)], axis=1))
        grad32 = jnp.concatenate(parts, axis=0)
        grad = grad32.astype(BF)
        cut = slice(half * C, half * C + C)
        lw_out[...] += mm(so_ref[:, cut], grad, TN)
        lb_out[...] += jnp.sum(grad32, axis=0, keepdims=True)
        back = mm(grad, lw_ref[...], NT) * gelu_slope(pre_ref[:, cut])
        back = back.astype(BF)
        sb_out[...] += jnp.sum(back.astype(F32), axis=0, keepdims=True)
        low.append(back)
    both = mm(own, jnp.concatenate(low, axis=1), TN)
    sw_out[...] += both[:PATCH, :C] + both[PATCH:, C:]


def head_kernel(
    cols, rows, scal_ref, f_ref, mk_ref, lab_ref, btt_ref, e_ref, wt_ref, tb_ref, wct_ref, wb_ref,
    dwc_ref, dwt_ref, dwb_ref, db_ref, fg_ref, sums_ref,
    mx_ref, x_ref, pre_ref, bt_ref, lgt_ref, lgs_ref, lg_ref, g_ref,
):
    own = rows * cols
    edge = HALO * cols
    total = own + 2 * edge
    shift = [cols * di + dj for di, dj in TAPS]

    @pl.when(pl.program_id(0) == 0)
    def _():
        dwc_ref[...] = jnp.zeros_like(dwc_ref)
        dwt_ref[...] = jnp.zeros_like(dwt_ref)
        dwb_ref[...] = jnp.zeros_like(dwb_ref)
        db_ref[...] = jnp.zeros_like(db_ref)
        sums_ref[...] = jnp.zeros_like(sums_ref)
        lg_ref[CLS_OUT:, :] = jnp.zeros((WIDE - CLS_OUT, 256), F32)

    def spread(i, carry):
        at = pl.multiple_of(i * 384, 128)
        wide = mm(mk_ref[0, :, pl.ds(at, 384)], e_ref[...], TN).astype(BF)
        for t in range(9):
            mx_ref[t, pl.ds(at, 384), :] = wide[:, t * LANE : (t + 1) * LANE]
        return carry

    lax.fori_loop(0, total // 384, spread, 0)

    def twice(mask):
        return jnp.concatenate([mask, mask], axis=1)

    def build(source, at, count, row):
        for t, (di, dj) in enumerate(TAPS):
            value = source[dj + 1, pl.ds(at + cols * di, count), :]
            x_ref[pl.ds(row, count), t * C : (t + 1) * C] = value * twice(mx_ref[t, pl.ds(at, count), :])

    first_tower = cols
    tower_rows = total - 2 * cols
    first_logit = edge - 256
    logit_cells = own + 512
    first_g = edge - 128
    g_cells = own + 256

    def heads(ct32_ref, ct_ref):
        zero = jnp.zeros((cols + 8, C), F32)
        ct32_ref[0 : cols + 8, :] = zero
        ct32_ref[8 + total - cols : 16 + total, :] = zero
        zero = jnp.zeros((cols, C), BF)
        bt_ref[0:cols, :] = zero
        bt_ref[total - cols : total, :] = zero
        piece = tower_rows // 3

        def tower(i, carry):
            row = pl.multiple_of(i * piece, 16)
            at = pl.multiple_of(first_tower + i * piece, 16)
            build(f_ref.at[0], at, piece, row)
            pre = mm(x_ref[pl.ds(row, piece), :], wt_ref[...]) + tb_ref[...]
            pre_ref[pl.ds(row, piece), :] = pre
            out = gelu(pre)
            ct32_ref[pl.ds(pl.multiple_of(8 + at, 8), piece), :] = out[:, :C]
            bt_ref[pl.ds(at, piece), :] = out[:, C:].astype(BF)
            return carry

        lax.fori_loop(0, 3, tower, 0)

        def move(i, carry):
            base = pl.multiple_of(i * edge, 16)
            value = ct32_ref[pl.ds(base, edge + 16), :]
            for k in range(3):
                ct_ref[k, pl.ds(base, edge), :] = value[7 + k : 7 + k + edge].astype(BF)
            return carry

        lax.fori_loop(0, total // edge, move, 0)
        inv_ema = scal_ref[0]
        number = lax.broadcasted_iota(jnp.int32, (CLASSES, 256), 0).astype(F32)
        lane = lax.broadcasted_iota(jnp.int32, (8, 256), 1)

        def logits(q, carry):
            row = pl.multiple_of(q * 256, 128)
            at = pl.multiple_of(first_logit + q * 256, 128)
            build(ct_ref, at, 256, row)
            lg_ref[0:CLS_OUT, :] = mm(wct_ref[...], x_ref[pl.ds(row, 256), :], NT) + PRIOR
            place = lane + at
            mine = ((place >= edge) & (place < edge + own)).astype(F32)

            def focal(a, total_focal):
                here = pl.multiple_of(a * CLASSES, 16)
                value = lg_ref[pl.ds(here, CLASSES), :]
                label = jnp.broadcast_to(lab_ref[0, pl.ds(a, 1), pl.ds(at, 256)], (CLASSES, 256))
                hit = label == number
                side = jnp.where(hit, -value, value)
                small = jnp.exp(-jnp.abs(side))
                ratio = 1.0 / (1.0 + small)
                tiny = small * (1.0 - small * (0.5 - small * (1.0 / 3.0)))
                cross = jnp.maximum(side, 0.0) + jnp.where(small < 0.01, tiny, jnp.log(1.0 + small))
                prob = jnp.where(side >= 0.0, ratio, small * ratio)
                square = prob * prob
                weight = jnp.where(hit, ALPHA, 1.0 - ALPHA)
                weight = jnp.where(label > -1.5, weight, 0.0)
                loss = weight * square * cross
                pull = weight * square * (2.0 * (1.0 - prob) * cross + prob) * inv_ema
                pull = jnp.where(hit, -pull, pull)
                lg_ref[pl.ds(here, CLASSES), :] = pull
                lgt_ref[pl.ds(here, CLASSES), pl.ds(row, 256)] = pull.astype(BF)
                return total_focal + jnp.sum(loss.reshape(CLASSES // 8, 8, 256), axis=0)

            sums_ref[0:8, :] += lax.fori_loop(0, ANCH, focal, jnp.zeros((8, 256), F32)) * mine
            lgs_ref[pl.ds(row, 256), :] = lg_ref[...].T.astype(BF)
            return carry

        lax.fori_loop(0, logit_cells // 256, logits, 0)

        def class_weights(i, carry):
            at = pl.multiple_of(i * 256, 128)
            dwc_ref[:, pl.ds(at, 256)] += mm(lgt_ref[:, 256 : 256 + own], x_ref[256 : 256 + own, pl.ds(at, 256)])
            return carry

        lax.fori_loop(0, 9, class_weights, 0)

    pl.run_scoped(heads, pltpu.VMEM((total + 16, C), F32), pltpu.VMEM((3, total, C), BF))

    def boxes(y_ref, gg_ref, xg_ref):
        inv_norm = scal_ref[1]

        def outer(i, carry):
            at = pl.multiple_of(i * 768, 128)
            y_ref[:, pl.ds(at, 768)] = mm(wb_ref[...], bt_ref[pl.ds(at, 768), :], NT)
            return carry

        lax.fori_loop(0, total // 768, outer, 0)
        lane = lax.broadcasted_iota(jnp.int32, (SLOT, total), 1)
        mine = (lane >= edge) & (lane < edge + own)

        def guess(m, carry):
            acc = jnp.zeros((SLOT, total), F32)
            for t in range(9):
                value = y_ref[pl.ds(pl.multiple_of(t * BOX_ROWS + m * SLOT, 8), SLOT), :]
                moved = pltpu.roll(value, (-shift[t]) % total, 1)
                acc += moved * mk_ref[0, t : t + 1, :].astype(F32)
            differ = acc - btt_ref[0, m]
            positive = lab_ref[0] >= 0.0
            size = jnp.abs(differ)
            loss = jnp.where(size < HUBER, 0.5 * differ * differ / HUBER, size - 0.5 * HUBER)
            loss = jnp.where(positive & mine, loss, 0.0)
            part = loss[:, 0:256]
            for k in range(1, total // 256):
                part += loss[:, k * 256 : (k + 1) * 256]
            sums_ref[8:16, :] += part[0:8] + part[8:16]
            pull = jnp.minimum(jnp.maximum(differ / HUBER, -1.0), 1.0) * inv_norm
            pull = jnp.where(positive, pull, 0.0)
            gg_ref[pl.ds(pl.multiple_of(m * SLOT, 8), SLOT), :] = pull
            return carry

        lax.fori_loop(0, 4, guess, 0)
        for t in range(9):
            moved = pltpu.roll(gg_ref[...], shift[t] % total, 1)
            xg_ref[t * BOX_ROWS : (t + 1) * BOX_ROWS, :] = (moved * mk_ref[0, 8 - t : 9 - t, :].astype(F32)).astype(BF)
        dwb_ref[...] += mm(xg_ref[:, edge : edge + own], bt_ref[edge : edge + own, :])

        def into(q, carry):
            row = pl.multiple_of(q * 256, 128)
            grad = mm(xg_ref[:, pl.ds(pl.multiple_of(first_g + row, 128), 256)], wb_ref[...], TN)
            pre = pre_ref[pl.ds(pl.multiple_of(first_g - first_tower + row, 16), 256), C:]
            g_ref[pl.ds(row, 256), C:] = (grad * gelu_slope(pre)).astype(BF)
            return carry

        lax.fori_loop(0, g_cells // 256, into, 0)

    pl.run_scoped(
        boxes,
        pltpu.VMEM((9 * BOX_ROWS, total), F32),
        pltpu.VMEM((BOX_ROWS, total), F32),
        pltpu.VMEM((9 * BOX_ROWS, total), BF),
    )

    def class_back(z_ref):
        z_ref[:, 0:8, :] = jnp.zeros((3, 8, C), F32)
        z_ref[:, 8 + g_cells : 16 + g_cells, :] = jnp.zeros((3, 8, C), F32)
        piece = g_cells // 4

        def multiply(i, carry):
            row = pl.multiple_of(i * piece, 16)
            for k in range(3):
                acc = jnp.zeros((piece, C), F32)
                for r in range(3):
                    t = r * 3 + k
                    source = row + first_g - cols * (r - 1)
                    mask = mx_ref[t, pl.ds(pl.multiple_of(source, 16), piece), :]
                    value = lgs_ref[pl.ds(pl.multiple_of(source - first_logit, 16), piece), :]
                    value = value * jnp.concatenate([mask] * (WIDE // LANE), axis=1)
                    acc += mm(value[:, :CLS_OUT], wct_ref[:, t * C : t * C + C])
                z_ref[k, pl.ds(pl.multiple_of(8 + row, 8), piece), :] = acc
            return carry

        lax.fori_loop(0, 4, multiply, 0)

        def collect(q, carry):
            row = pl.multiple_of(q * 256, 128)
            grad = z_ref[1, pl.ds(pl.multiple_of(8 + row, 8), 256), :]
            grad += z_ref[0, pl.ds(row, 272), :][9:265] + z_ref[2, pl.ds(row, 272), :][7:263]
            pre = pre_ref[pl.ds(pl.multiple_of(first_g - first_tower + row, 16), 256), :C]
            g_ref[pl.ds(row, 256), :C] = (grad * gelu_slope(pre)).astype(BF)
            return carry

        lax.fori_loop(0, g_cells // 256, collect, 0)

    pl.run_scoped(class_back, pltpu.VMEM((3, g_cells + 16, C), F32))

    def tower_back(z_ref, gt_ref):
        def flip(q, carry):
            row = pl.multiple_of(q * 256, 128)
            part = g_ref[pl.ds(pl.multiple_of(edge - first_g + row, 16), 256), :].astype(F32)
            gt_ref[:, pl.ds(row, 256)] = part.T.astype(BF)
            db_ref[...] += jnp.sum(part, axis=0, keepdims=True)
            build(f_ref.at[0], pl.multiple_of(edge + row, 16), 256, row)
            return carry

        lax.fori_loop(0, own // 256, flip, 0)

        def tower_weights(i, carry):
            at = pl.multiple_of(i * 256, 128)
            dwt_ref[:, pl.ds(at, 256)] += mm(gt_ref[...], x_ref[0:own, pl.ds(at, 256)])
            return carry

        lax.fori_loop(0, 9, tower_weights, 0)
        first_z = edge - 16
        piece = (own + 32) // 2

        def multiply(i, carry):
            row = pl.multiple_of(i * piece, 16)
            for k in range(3):
                acc = jnp.zeros((piece, C), F32)
                for r in range(3):
                    t = r * 3 + k
                    source = row + first_z - cols * (r - 1)
                    mask = mx_ref[t, pl.ds(pl.multiple_of(source, 16), piece), :]
                    value = g_ref[pl.ds(pl.multiple_of(source - first_g, 16), piece), :]
                    value = value * jnp.concatenate([mask] * (2 * C // LANE), axis=1)
                    acc += mm(value, wt_ref[t * C : t * C + C, :], NT)
                z_ref[k, pl.ds(row, piece), :] = acc
            return carry

        lax.fori_loop(0, 2, multiply, 0)

        def collect(q, carry):
            row = pl.multiple_of(q * 256, 128)
            base = pl.multiple_of(row + 8, 8)
            grad = z_ref[1, pl.ds(pl.multiple_of(16 + row, 8), 256), :]
            grad += z_ref[0, pl.ds(base, 272), :][9:265] + z_ref[2, pl.ds(base, 272), :][7:263]
            grad = grad.astype(BF).astype(F32)
            for n in range(2):
                fg_ref[0, n, pl.ds(row, 256), :] = grad[:, n * LANE : n * LANE + LANE]
            return carry

        lax.fori_loop(0, own // 256, collect, 0)

    pl.run_scoped(
        tower_back,
        pltpu.VMEM((3, own + 32, C), F32),
        pltpu.VMEM((2 * C, own), BF),
    )


def whole(shape):
    return pl.BlockSpec(shape, lambda *_: (0,) * len(shape))


def shape_of(shape, dtype=F32):
    return jax.ShapeDtypeStruct(shape, dtype)


VMEM_LIMIT = 63 * 1024 * 1024


def stem_forward(patches, rim, stem_w, stem_b, lat_w, lat_b):
    canvases, rows, width = patches.shape
    cols = width // PATCH
    pairs = 8
    steps = cols // (2 * pairs)
    chunk = 2 * pairs * PATCH
    zero = jnp.zeros((PATCH, C), BF)
    w2 = jnp.concatenate(
        [jnp.concatenate([stem_w, zero], axis=1), jnp.concatenate([zero, stem_w], axis=1)], axis=0
    )
    b2 = jnp.concatenate([stem_b, stem_b]).astype(F32)[None]
    count = pairs * canvases * rows
    total = (rows + 2 * HALO) * cols
    return pl.pallas_call(
        functools.partial(stem_kernel, pairs, cols, rows),
        grid=(steps,),
        in_specs=[
            pl.BlockSpec((canvases, rows, chunk), lambda s: (0, 0, s)),
            pl.BlockSpec((2 * HALO * canvases, chunk), lambda s: (0, s)),
            whole((2 * PATCH, 2 * C)),
            whole((1, 2 * C)),
            whole((C, C)),
            whole((1, C)),
        ],
        out_specs=[
            pl.BlockSpec((count, 2 * C), lambda s: (s, 0)),
            pl.BlockSpec((count, 2 * C), lambda s: (s, 0)),
            whole((canvases, 3, total, C)),
        ],
        out_shape=[
            shape_of((steps * count, 2 * C)),
            shape_of((steps * count, 2 * C), BF),
            shape_of((canvases, 3, total, C), BF),
        ],
        scratch_shapes=[pltpu.VMEM((canvases, 2, total + 16, LANE), F32)],
        compiler_params=pltpu.CompilerParams(vmem_limit_bytes=VMEM_LIMIT),
        name="stem",
    )(patches, rim, w2, b2, lat_w, lat_b.astype(F32)[None])


def stem_backward(patches, feature_grad, stem_out, stem_pre, lat_w):
    canvases, rows, width = patches.shape
    cols = width // PATCH
    pairs = 8
    steps = cols // (2 * pairs)
    chunk = 2 * pairs * PATCH
    count = pairs * canvases * rows
    return pl.pallas_call(
        functools.partial(stem_back_kernel, pairs, cols, rows),
        grid=(steps,),
        in_specs=[
            pl.BlockSpec((canvases, rows, chunk), lambda s: (0, 0, s)),
            whole((canvases, 2, rows * cols, LANE)),
            pl.BlockSpec((count, 2 * C), lambda s: (s, 0)),
            pl.BlockSpec((count, 2 * C), lambda s: (s, 0)),
            whole((C, C)),
        ],
        out_specs=[whole((PATCH, C)), whole((1, C)), whole((C, C)), whole((1, C))],
        out_shape=[shape_of((PATCH, C)), shape_of((1, C)), shape_of((C, C)), shape_of((1, C))],
        compiler_params=pltpu.CompilerParams(vmem_limit_bytes=VMEM_LIMIT),
        name="stem_back",
    )(patches, feature_grad, stem_out, stem_pre, lat_w)


def heads_call(rows, cols, scal, feats, masks, labels, box_target, wt, tb, wct, wb):
    canvases = feats.shape[0]
    own = rows * cols
    total = own + 2 * HALO * cols
    spread = jnp.repeat(jnp.eye(SLOT, 9, dtype=BF), LANE, axis=1)

    def per(shape):
        return pl.BlockSpec((1,) + shape, lambda c: (c,) + (0,) * len(shape))

    return pl.pallas_call(
        functools.partial(head_kernel, cols, rows),
        grid=(canvases,),
        in_specs=[
            pl.BlockSpec(memory_space=pltpu.SMEM),
            pl.BlockSpec((1, 3, total, C), lambda c: (c, 0, 0, 0), pipeline_mode=pl.Buffered(1)),
            per((SLOT, total)),
            per((SLOT, total)),
            per((4, SLOT, total)),
            whole(spread.shape),
            whole(wt.shape),
            whole(tb.shape),
            whole(wct.shape),
            whole(wb.shape),
        ],
        out_specs=[
            whole((CLS_OUT, 9 * C)),
            whole((2 * C, 9 * C)),
            whole((9 * BOX_ROWS, C)),
            whole((1, 2 * C)),
            per((2, own, LANE)),
            whole((16, 256)),
        ],
        out_shape=[
            shape_of((CLS_OUT, 9 * C)),
            shape_of((2 * C, 9 * C)),
            shape_of((9 * BOX_ROWS, C)),
            shape_of((1, 2 * C)),
            shape_of((canvases, 2, own, LANE)),
            shape_of((16, 256)),
        ],
        scratch_shapes=[
            pltpu.VMEM((9, total, LANE), BF),
            pltpu.VMEM((total - 2 * cols, 9 * C), BF),
            pltpu.VMEM((total - 2 * cols, 2 * C), F32),
            pltpu.VMEM((total, C), BF),
            pltpu.VMEM((CLS_OUT, own + 512), BF),
            pltpu.VMEM((own + 512, WIDE), BF),
            pltpu.VMEM((WIDE, 256), F32),
            pltpu.VMEM((own + 256, 2 * C), BF),
        ],
        compiler_params=pltpu.CompilerParams(vmem_limit_bytes=VMEM_LIMIT),
        name="heads",
    )(scal, feats, masks, labels, box_target, spread, wt, tb, wct, wb)


def unpack(flat_values):
    lengths = [PATCH * C, C, C * C, C, 18 * C * C, 2 * C, 9 * C * BOX_OUT]
    pieces = []
    offset = 0
    for length in lengths:
        pieces.append(flat_values[offset : offset + length])
        offset = offset + length
    return (
        pieces[0].reshape(PATCH, C),
        pieces[1],
        pieces[2].reshape(C, C),
        pieces[3],
        pieces[4].reshape(2, 9, C, C),
        pieces[5].reshape(2, C),
        pieces[6].reshape(9, C, BOX_OUT),
    )


def adamw_update(weight, first, second, grad):
    first_new = MOMENT_ONE * first + (1.0 - MOMENT_ONE) * grad
    second_new = MOMENT_TWO * second + (1.0 - MOMENT_TWO) * grad * grad
    first_hat = first_new / (1.0 - MOMENT_ONE**STEP)
    second_hat = second_new / (1.0 - MOMENT_TWO**STEP)
    weight_new = weight - RATE * (first_hat / (jnp.sqrt(second_hat) + EPSILON) + DECAY * weight)
    return (weight_new, first_new, second_new)


def cell_data(boxes, match, gt_labels, gt_deltas, first_row, rows, cols):
    full_rows = match.shape[2] // cols
    total = (rows + 2 * HALO) * cols
    place = jnp.arange(total, dtype=jnp.int32)[None]
    row = place // cols + (first_row - HALO)
    col = place % cols

    def crop(r, j):
        found = jnp.full((boxes.shape[0], total), -1, jnp.int32)
        for k in range(boxes.shape[1]):
            edge = boxes[:, k, :, None]
            inside = (r >= edge[:, 0]) & (r < edge[:, 2]) & (j >= edge[:, 1]) & (j < edge[:, 3])
            found = jnp.where(inside, k, found)
        return jnp.where((r >= 0) & (r < full_rows) & (j >= 0) & (j < cols), found, -1)

    centre = crop(row, col)
    valid = centre >= 0
    masks = jnp.stack([(crop(row + di, col + dj) == centre) & valid for di, dj in TAPS], axis=1)
    masks = jnp.pad(masks.astype(BF), ((0, 0), (0, SLOT - 9), (0, 0)))
    edge = HALO * cols
    near = jnp.pad(match, ((0, 0), (0, 0), (edge, edge)), constant_values=-2)
    near = lax.dynamic_slice_in_dim(near, first_row * cols, total, 2)
    near = jnp.where(valid[:, None], near, -2)
    near = jnp.pad(near, ((0, 0), (0, SLOT - 9), (0, 0)), constant_values=-2)
    labels = near
    targets = jnp.zeros((near.shape[0], 4) + near.shape[1:], F32)
    for g in range(gt_labels.shape[1]):
        labels = jnp.where(near == g, gt_labels[:, g, None, None], labels)
        targets = jnp.where((near == g)[:, None], gt_deltas[:, g, :, None, None], targets)
    return masks, labels.astype(F32), targets


def local(patches, boxes, match, gt_labels, gt_deltas, ema_old, shared_params, shared_m, shared_v, class_params, class_m, class_v):
    cls_rank = lax.axis_index("cls")
    cls_parts = lax.axis_size("cls")
    canvases, rows, width = patches.shape
    cols = width // PATCH
    own = rows * cols
    edge = HALO * cols
    masks, labels, targets = cell_data(boxes, match, gt_labels, gt_deltas, cls_rank * rows, rows, cols)
    count = jnp.sum((labels[:, :, edge : edge + own] >= 0.0).astype(F32))
    positives = lax.psum(count, ("img", "cls"))
    norm = jnp.maximum(positives, 1.0)
    ema_new = EMA_KEEP * ema_old + (1.0 - EMA_KEEP) * norm

    all_weights = lax.all_gather(shared_params.astype(BF), ("img", "cls"), axis=0, tiled=True)
    class_w = lax.all_gather(class_params.astype(BF), ("img", "cls"), axis=0)
    class_w = class_w.reshape(-1, cls_parts, *class_params.shape).transpose(0, 2, 1, 3).reshape(9, C, CLS_OUT)
    down = lax.ppermute(patches[:, rows - HALO :], "cls", [(i, i + 1) for i in range(cls_parts - 1)])
    up = lax.ppermute(patches[:, :HALO], "cls", [(i + 1, i) for i in range(cls_parts - 1)])
    rim = jnp.concatenate([down, up], axis=1).reshape(canvases * 2 * HALO, width)

    stem_w, stem_b, lat_w, lat_b, tower_w, tower_b, box_w = unpack(all_weights)
    stem_pre, stem_out, feats = stem_forward(patches, rim, stem_w, stem_b, lat_w, lat_b)
    wt = jnp.concatenate([tower_w[0].reshape(9 * C, C), tower_w[1].reshape(9 * C, C)], axis=1)
    tb = tower_b.reshape(1, 2 * C).astype(F32)
    wct = class_w.transpose(2, 0, 1).reshape(CLS_OUT, 9 * C)
    wb = jnp.pad(box_w.reshape(9, C, ANCH, 4).transpose(0, 3, 2, 1), ((0, 0), (0, 0), (0, SLOT - ANCH), (0, 0)))
    wb = wb.reshape(9 * BOX_ROWS, C)
    scal = jnp.stack([1.0 / ema_new, 1.0 / norm])
    dwc, dwt, dwb, db, feature_grad, sums = heads_call(
        rows, cols, scal, feats, masks, labels, targets, wt, tb, wct, wb
    )
    stem_g, stem_bg, lat_g, lat_bg = stem_backward(patches, feature_grad, stem_out, stem_pre, lat_w)
    focal, huber = lax.psum((jnp.sum(sums[0:8]), jnp.sum(sums[8:16])), ("img", "cls"))
    loss = focal / ema_new + huber / norm

    tower_g = dwt.reshape(2, C, 9 * C).transpose(0, 2, 1)
    box_g = dwb.reshape(9, 4, SLOT, C)[:, :, :ANCH].transpose(0, 3, 2, 1)
    flat = jnp.concatenate(
        [stem_g.reshape(-1), stem_bg.reshape(-1), lat_g.reshape(-1), lat_bg.reshape(-1), tower_g.reshape(-1), db.reshape(-1), box_g.reshape(-1)]
    )
    shared_grad = lax.psum_scatter(flat, ("img", "cls"), scatter_dimension=0, tiled=True)
    class_sum = lax.psum_scatter(dwc.T, "img", scatter_dimension=0, tiled=True)
    class_grad = lax.psum_scatter(class_sum, "cls", scatter_dimension=1, tiled=True)
    return (
        loss,
        ema_new,
        *adamw_update(shared_params, shared_m, shared_v, shared_grad),
        *adamw_update(class_params, class_m, class_v, class_grad),
    )


def solution(mesh):
    spread = P(("img", "cls"))
    block = P("img", "cls")
    return jax.shard_map(
        local,
        mesh=mesh,
        in_specs=(
            P("img", "cls", None),
            P("img", None, None),
            P("img", None, None),
            P("img", None),
            P("img", None, None),
            P(),
            spread,
            spread,
            spread,
            block,
            block,
            block,
        ),
        out_specs=(P(), P(), spread, spread, spread, block, block, block),
        check_vma=False,
    )
```

time: 3270 us -> 686 us (0.21)
  local copies, waits for them, and re-layouts: 2340 us -> 148 us
  matrix products: 464 us -> 0 us
  Pallas kernels: 0 us -> 159 us
  waiting for transfers between devices: 269 us -> 218 us
    gather x8 -> x0, local copies, waits for them, and re-layouts: 2210 us -> none  [the longest x3 1260 us: pick_delta(): return table[index]]
    dot_general x115 -> x0, matrix products: 464 us -> none  [the longest x36 177 us: conv_apply(): lax.dot_general(masked_in, weight, (((3,), (1,)), ((), ())), preferred_el...]
    psum x1 -> x0, waiting for transfers between devices: 165 us -> none  [local(): class_in_whole = lax.psum(class_in_part, 'cls')]
    pallas_call x0 -> x3, Pallas kernels: none -> 159 us  [the longest x1 136 us: heads_call(): pl.pallas_call(functools.partial(head_kernel, cols, rows), grid=(canvases...]
    unnamed x7 -> x8, waiting for transfers between devices: 104 us -> 196 us
    all_gather x1 -> x0, blocking collectives: 33.7 us -> none  [local(): lax.all_gather(class_params.astype(jnp.bfloat16), 'img', axis=0, tiled=True)]
    unnamed x364 -> x60, local copies, waits for them, and re-layouts: 67.4 us -> 92.1 us
  transfers between devices with their start and end apart: 11 -> 7, of which waited for: 2 -> 3; matrix products, arithmetic and copies ran while one was open for 79% -> 23% of each run, Pallas kernels for 0% -> 3%
where the time goes in v1:
time: 686 us; the launch traced here: 681 us
  waiting for transfers between devices  218 us (32%)
  Pallas kernels  159 us (23%)
  local copies, waits for them, and re-layouts  148 us (22%)
  blocking collectives  107 us (16%)
  other arithmetic  22.2 us (3%)
  between operations  19.9 us (3%)
    unnamed x8, waiting for transfers between devices  196 us
    pallas_call x1, Pallas kernels, heads_call(): pl.pallas_call(functools.partial(head_kernel, cols, rows), grid=(canvases...  136 us
    unnamed x60, local copies, waits for them, and re-layouts  92.1 us
    psum x1, blocking collectives, local(): positives = lax.psum(count, ('img', 'cls'))  44.2 us
    psum x1, blocking collectives, local(): lax.psum((jnp.sum(sums[0:8]), jnp.sum(sums[8:16])), ('img', 'cls'))  41.7 us
    all_gather x1, waiting for transfers between devices, local(): class_w = lax.all_gather(class_params.astype(BF), ('img', 'cls'), axis=0)  22.2 us
    unnamed x1, blocking collectives  21.6 us
    reshape x2, local copies, waits for them, and re-layouts, local(): class_w.reshape(-1, cls_parts, *class_params.shape).transpose(0, 2, 1, 3)  17.6 us
  transfers between devices with their start and end apart: 7, of which 3 were waited for; matrix products, arithmetic and copies ran while one was open for 23% of the time, Pallas kernels for 3%

profile of v1, /device:TPU:0, one launch (start us, length us, event | category | flops | bytes accessed | tf_op | source)
XLA Modules:
  0.0 681.2 jit_solution(16206300562252586840)
XLA Ops:
  7.2 0.9 convert_element_type.38
  8.4 0.9 dynamic-update-slice
  9.3 1.5 copy-done
  11.0 1.5 fusion.49
  12.5 2.4 collective-permute-start
  14.9 1.3 collective-permute-start.1
  21.3 44.2 %psum.21 = f32[]{:T(128)} all-reduce(f32[]{:T(128)} %convert_reduce_fusion), channel_id=1, replica_groups=mesh['img'=8,'cls'=4] {'img','cls'}, use_global_device_ids=true, to_apply=%region_1.2 | all-reduce | flops 1 | bytes 8 | tf_op jit(solution)/shard_map/psum | solution.py:611
  70.8 3.2 select_select_fusion.btt_ref
  74.7 1.1 maximum_bitcast_fusion.h_ref
  75.9 76.7 %all-reduce.14.cloned.1.call-done = bf16[1378304]{0:T(1024)(128)(2,1)} async-done(((bf16[1378304]{0:T(1024)(128)(2,1)}), bf16[1378304]{0:T(1024)(128)(2,1)}) %all-reduce.14.cloned.1.call-update) | async-done | bytes 2756624
  152.5 2.3 fusion.48
  155.8 1.2 slice_convert_fusion.1
  157.1 1.3 slice.424
  158.3 1.2 slice.426
  159.5 7.7 %reshape_reshape.4 = bf16[9,256,9,4]{3,2,1,0:T(8,128)(2,1)} reshape(bf16[82944]{0:T(1024)(128)(2,1)S(1)} %slice-done.1) | data formatting | bytes 331776 | tf_op jit(solution)/shard_map/reshape;reshape | solution.py:627
  167.2 9.6 %copy.37 = bf16[9,4,9,256]{3,2,1,0:T(8,128)(2,1)S(1)} copy(bf16[9,4,9,256]{1,2,3,0:T(8,128)(2,1)} %bitcast.45) | data formatting | bytes 331776
  176.9 0.7 pad.24.clone
  178.2 0.8 fusion.3.w_ref
  179.0 13.7 %stem.1 = (f32[1536,512]{1,0:T(8,128)}, bf16[1536,512]{1,0:T(8,128)(2,1)}, bf16[2,3,2304,256]{3,2,1,0:T(8,128)(2,1)}) custom-call(bf16[2,16,18432]{2,1,0:T(8,128)(2,1)} %x_ref.3, bf16[16,18432]{1,0:T(8,128)(2,1)} %maximum_bitcast_fusion.h_ref, bf16[384,512]{1,0:T(8,128)(2,1)} %fusion.3.w_ref, f32[1,512]{1,0:T(1,128)} %maximum_convert_fusion.b_ref, ...), custom_call_target="tpu_custom_call" | custom-call | tf_op jit(solution)/shard_map/stem/pallas_call | solution.py:437
  192.7 1.3 slice_convert_fusion
  193.9 3.2 pad_maximum_fusion.wt_ref
  197.2 22.2 %all-gather.4.cloned.1.call-done = bf16[32,288,180]{1,2,0:T(8,128)(2,1)} async-done(((bf16[1,288,180]{1,2,0:T(8,128)(2,1)}), bf16[32,288,180]{1,2,0:T(8,128)(2,1)}) %all-gather.4.cloned.1.call-update) | async-done | bytes 3317776 | tf_op jit(solution)/shard_map/all_gather | solution.py:616
  219.4 9.8 %copy.29 = bf16[8,4,288,180]{3,1,2,0:T(4,128)(2,1)} copy(bf16[8,4,288,180]{2,3,1,0:T(8,128)(2,1)} %bitcast.52) | data formatting | bytes 6635520 | tf_op jit(solution)/shard_map/reshape | solution.py:617
  229.2 7.8 %reshape.9589 = bf16[9,256,720]{2,1,0:T(8,128)(2,1)S(1)} reshape(bf16[8,288,4,180]{3,2,1,0:T(4,128)(2,1)} %bitcast.48) | data formatting | bytes 6635520 | tf_op jit(solution)/shard_map/reshape | solution.py:617
  237.0 3.9 copy.31.wct_ref
  241.0 136.0 %heads.1 = (f32[720,2304]{1,0:T(8,128)}, f32[512,2304]{1,0:T(8,128)}, f32[576,256]{1,0:T(8,128)}, f32[1,512]{1,0:T(1,128)}, f32[2,2,1536,128]{3,2,1,0:T(8,128)}, /*index=5*/f32[16,256]{1,0:T(8,128)}) custom-call(f32[2]{0:T(128)} %pad_maximum_fusion.1.scal_ref, bf16[2,3,2304,256]{3,2,1,0:T(8,128)(2,1)} %get-tuple-element.21.f_ref, ...), custom_call_target="tpu_custom_call" | custom-call | tf_op jit(solution)/shard_map/heads/pallas_call | solution.py:497
  377.0 7.9 %copy.34 = f32[2304,720]{1,0:T(8,128)} copy(f32[2304,720]{0,1:T(8,128)} %bitcast.50) | data formatting | bytes 13271040
  385.0 9.8 %stem_back.1 = (f32[192,256]{1,0:T(8,128)}, f32[1,256]{1,0:T(1,128)}, f32[256,256]{1,0:T(8,128)}, f32[1,256]{1,0:T(1,128)}) custom-call(bf16[2,16,18432]{2,1,0:T(8,128)(2,1)} %x_ref.3, f32[2,2,1536,128]{3,2,1,0:T(8,128)} %get-tuple-element.23.fg_ref, bf16[1536,512]{1,0:T(8,128)(2,1)} %get-tuple-element.24.so_ref, f32[1536,512]{1,0:T(8,128)} %get-tuple-element.25.pre_ref, ...), custom_call_target="tpu_custom_call" | custom-call | tf_op jit(solution)/shard_map/stem_back/pallas_call | solution.py:471
  394.8 1.0 copy.39
  395.8 1.1 copy.40
  396.9 6.1 copy.32
  403.0 7.1 %copy.41 = f32[576,2,8,128]{3,1,2,0:T(2,128)} copy(f32[576,2,8,128]{3,2,1,0:T(8,128)} %bitcast.47) | data formatting | bytes 9437184
  410.1 10.2 %copy.36 = f32[9,4,9,256]{1,2,3,0:T(8,128)} copy(f32[9,4,9,256]{3,2,1,0:T(8,128)S(1)} %bitcast.56) | data formatting | bytes 663552
  420.3 10.7 %reshape.9600 = f32[82944]{0:T(1024)S(1)} reshape(f32[9,256,9,4]{3,2,1,0:T(8,128)} %bitcast.44) | data formatting | bytes 663552 | tf_op jit(solution)/shard_map/reshape | solution.py:640
  431.1 0.7 constant_dynamic-update-slice_fusion.5
  431.8 1.3 constant_dynamic-update-slice_fusion.4
  433.1 1.7 constant_dynamic-update-slice_fusion.3
  434.8 1.3 constant_dynamic-update-slice_fusion.2
  436.1 41.1 %dynamic-update-slice.5 = f32[1378304]{0:T(1024)} dynamic-update-slice(f32[1378304]{0:T(1024)} %constant_dynamic-update-slice_fusion.2, f32[1179648]{0:T(1024)} %bitcast.46, s32[]{} %constant.188) | dynamic-update-slice | bytes 9437188
  477.2 1.3 constant_dynamic-update-slice_fusion.1
  478.5 0.8 constant_dynamic-update-slice_fusion
  481.8 41.7 %all-reduce.10 = (f32[]{:T(128)}, f32[]{:T(128)}) all-reduce(f32[]{:T(128)} %get-tuple-element.35, f32[]{:T(128)} %get-tuple-element.34), channel_id=1, replica_groups=mesh['img'=8,'cls'=4] {'img','cls'}, use_global_device_ids=true, to_apply=%region_3.4 | all-reduce | flops 2 | bytes 16 | tf_op jit(solution)/shard_map/psum | solution.py:634
  524.8 1.6 copy.35
  526.5 21.6 %fusion = f32[288,192]{0,1:T(8,128)S(1)} fusion(f32[288,720]{0,1:T(8,128)S(1)} %copy.35), kind=kCustom, calls=%all-reduce-scatter | all-reduce-scatter fusion | flops 221185 | bytes 1051136
  548.1 1.4 collective-permute-start.2
  549.6 119.5 %all-reduce.16.cloned.1.call-done = f32[1378304]{0:T(1024)} async-done(((f32[1378304]{0:T(1024)}), f32[1378304]{0:T(1024)}) %all-reduce.16.cloned.1.call-update) | async-done | bytes 5513232
  669.0 1.9 multiply_subtract_fusion.1
  671.4 1.1 multiply_subtract_fusion
  (96 shorter events, 13.7 us)
Async XLA Ops:
  7.2 145.4 %all-reduce.14.cloned.1.call-start = ((), (), s32[]{:S(2)}) async-start(), calls=%async_computation.1 | async-start | bytes 5513216
  9.3 1.6 copy-start
  10.9 5.3 copy-start.3
  10.9 6.3 copy-start.15
  10.9 6.5 copy-start.8
  10.9 208.5 %all-gather.4.cloned.1.call-start = ((), (), s32[]{:S(2)}) async-start(), calls=%async_computation.2 | async-start | bytes 4663296 | tf_op jit(solution)/shard_map/all_gather | solution.py:616
  12.5 62.2 %collective-permute-start = (bf16[2,4,18432]{2,1,0:T(4,128)(2,1)S(1)}, bf16[2,4,18432]{2,1,0:T(4,128)(2,1)S(1)}, u32[]{:S(2)}, u32[]{:S(2)}) collective-permute-start(bf16[2,4,18432]{2,1,0:T(4,128)(2,1)S(1)} %get-tuple-element.94), channel_id=1, source_target_pairs={{0,1},{1,2},{2,3},{4,5},{5,6},{6,7},{8,9},{9,10},{10,11},{12,13},{... | collective-permute-start | bytes 884744 | tf_op jit(solution)/shard_map/ppermute | solution.py:618
  14.9 59.8 %collective-permute-start.1 = (bf16[2,4,18432]{2,1,0:T(4,128)(2,1)S(1)}, bf16[2,4,18432]{2,1,0:T(4,128)(2,1)S(1)}, u32[]{:S(2)}, u32[]{:S(2)}) collective-permute-start(bf16[2,4,18432]{2,1,0:T(4,128)(2,1)S(1)} %get-tuple-element.95), channel_id=1, source_target_pairs={{1,0},{2,1},{3,2},{5,4},{6,5},{7,6},{9,8},{10,9},{11,10},{13,12},{... | collective-permute-start | bytes 884744 | tf_op jit(solution)/shard_map/ppermute | solution.py:619
  16.9 507.9 %reduce-scatter.6.cloned.1.call-start = ((), (), s32[]{:S(2)}) async-start(), calls=%async_computation.3 | async-start | bytes 7962624
  18.1 0.7 copy-start.5
  18.1 0.9 copy-start.11
  19.9 0.7 copy-start.2
  152.5 2.5 copy-start.1
  152.5 4.5 slice-start
  158.3 1.2 slice-start.1
  384.9 284.1 %all-reduce.16.cloned.1.call-start = ((), (), s32[]{:S(2)}) async-start(), calls=%async_computation.4 | async-start | bytes 11026432
  403.0 7.1 %copy-start.7 = (f32[576,256]{1,0:T(8,128)S(1)}, f32[576,256]{1,0:T(8,128)}, u32[]{:S(2)}) copy-start(f32[576,256]{1,0:T(8,128)} %get-tuple-element.32) | copy-start | bytes 1769476
  420.3 11.5 %copy-start.18 = (f32[1,256]{1,0:T(1,128)S(1)}, f32[1,256]{1,0:T(1,128)}, u32[]{:S(2)}) copy-start(f32[1,256]{1,0:T(1,128)} %get-tuple-element.27) | copy-start | bytes 3076
  420.3 14.5 %copy-start.17 = (f32[1,256]{1,0:T(1,128)S(1)}, f32[1,256]{1,0:T(1,128)}, u32[]{:S(2)}) copy-start(f32[1,256]{1,0:T(1,128)} %get-tuple-element.29) | copy-start | bytes 3076
  436.1 41.1 %copy-start.16 = (f32[1,512]{1,0:T(1,128)S(1)}, f32[1,512]{1,0:T(1,128)}, u32[]{:S(2)}) copy-start(f32[1,512]{1,0:T(1,128)} %get-tuple-element.31) | copy-start | bytes 6148
  479.3 0.7 copy-start.19
  479.3 1.9 copy-start.14
  526.4 142.6 %copy-start.6 = (f32[43072]{0:T(1024)S(1)}, f32[43072]{0:T(1024)}, u32[]{:S(2)}) copy-start(f32[43072]{0:T(1024)} %param.18) | copy-start | bytes 516868
  526.4 142.6 %copy-start.12 = (f32[43072]{0:T(1024)S(1)}, f32[43072]{0:T(1024)}, u32[]{:S(2)}) copy-start(f32[43072]{0:T(1024)} %param.19) | copy-start | bytes 516868
  526.4 142.6 %copy-start.13 = (f32[43072]{0:T(1024)S(1)}, f32[43072]{0:T(1024)}, u32[]{:S(2)}) copy-start(f32[43072]{0:T(1024)} %param.20) | copy-start | bytes 516868
  548.1 123.3 %copy-start.4 = (f32[288,180]{0,1:T(8,128)S(1)}, f32[288,180]{0,1:T(8,128)}, u32[]{:S(2)}) copy-start(f32[288,180]{0,1:T(8,128)} %param.21) | copy-start | bytes 622084
  548.1 123.3 %copy-start.9 = (f32[288,180]{0,1:T(8,128)S(1)}, f32[288,180]{0,1:T(8,128)}, u32[]{:S(2)}) copy-start(f32[288,180]{0,1:T(8,128)} %param.22) | copy-start | bytes 622084
  548.1 123.3 %copy-start.10 = (f32[288,180]{0,1:T(8,128)S(1)}, f32[288,180]{0,1:T(8,128)}, u32[]{:S(2)}) copy-start(f32[288,180]{0,1:T(8,128)} %param.23) | copy-start | bytes 622084
  548.1 122.8 %collective-permute-start.2 = (f32[288,36]{0,1:T(8,128)S(1)}, f32[288,36]{0,1:T(8,128)S(1)}, u32[]{:S(2)}, u32[]{:S(2)}) collective-permute-start(f32[288,36]{0,1:T(8,128)S(1)} %slice.442), channel_id=1, source_target_pairs={{0,1},{1,2},{2,3},{4,5},{5,6},{6,7},{8,9},{9,10},{10,11},{12,13},{... | collective-permute-start | bytes 124424
Sparse Core Ops, SparseCore 0:
  13.5 138.9 all-reduce.13
  156.0 63.3 all-gather.3
  385.1 128.2 reduce-scatter.5
  519.9 149.0 all-reduce.15

commit v2 on v1

--- a/solution.py
+++ b/solution.py
@@ -20,6 +20,7 @@
 BOX_ROWS = 4 * SLOT
 LANE = 128
 WIDE = 768
+GROUP = 16
 
 PRIOR = -4.59511985013459
 ALPHA = 0.25
@@ -31,6 +32,15 @@
 DECAY = 0.05
 EPSILON = 1e-08
 
+LENGTHS = [PATCH * C, C, C * C, C, 18 * C * C, 2 * C, 9 * C * BOX_OUT]
+TOWER_AT = sum(LENGTHS[:4]) // C
+LEAD = -TOWER_AT % 16
+TOWER_ROW = TOWER_AT + LEAD
+TAIL_ROW = TOWER_ROW + 18 * C
+FULL_ROWS = -(-(LEAD + sum(LENGTHS) // C) // 16) * 16
+HALF = 384
+MESH = pl.DeviceIdType.MESH
+
 BF = jnp.bfloat16
 F32 = jnp.float32
 TAPS = [(di, dj) for di in (-1, 0, 1) for dj in (-1, 0, 1)]
@@ -59,7 +69,7 @@
     return [x[:, width * k : width * (k + 1)] for k in range(pairs)]
 
 
-def stem_kernel(pairs, cols, rows, x_ref, h_ref, w_ref, b_ref, lw_ref, lb_ref, pre_ref, so_ref, f_ref, t_ref):
+def stem_kernel(pairs, cols, rows, x_ref, h_ref, head_ref, pre_ref, so_ref, f_ref, lw_ref, t_ref, w_ref, b_ref, lb_ref):
     step = pl.program_id(0)
     canvases = x_ref.shape[0]
     own_rows = canvases * rows
@@ -67,6 +77,15 @@
 
     @pl.when(step == 0)
     def _():
+        head = head_ref[...].astype(F32)
+        w_ref[...] = jnp.zeros_like(w_ref)
+        stem_w = head[LEAD : LEAD + PATCH].astype(BF)
+        w_ref[:PATCH, :C] = stem_w
+        w_ref[PATCH:, C:] = stem_w
+        bias = head[LEAD + PATCH : LEAD + PATCH + 1]
+        b_ref[...] = jnp.concatenate([bias, bias], axis=1)
+        lw_ref[...] = head[LEAD + PATCH + 1 : TOWER_ROW - 1].astype(BF)
+        lb_ref[...] = head[TOWER_ROW - 1 : TOWER_ROW]
         for c in range(canvases):
             for n in range(2):
                 t_ref[c, n, 0:8, :] = jnp.zeros((8, LANE), F32)
@@ -113,7 +132,7 @@
         lax.fori_loop(0, total // piece, move, 0)
 
 
-def stem_back_kernel(pairs, cols, rows, x_ref, fg_ref, so_ref, pre_ref, lw_ref, sw_out, sb_out, lw_out, lb_out):
+def stem_back_kernel(pairs, cols, rows, x_ref, fg_ref, so_ref, pre_ref, lw_ref, head_ref, sw_out, sb_out, lw_out, lb_out, h_ref):
     step = pl.program_id(0)
     canvases = x_ref.shape[0]
 
@@ -146,11 +165,64 @@
     both = mm(own, jnp.concatenate(low, axis=1), TN)
     sw_out[...] += both[:PATCH, :C] + both[PATCH:, C:]
 
+    @pl.when(step == pl.num_programs(0) - 1)
+    def _():
+        at = LEAD + PATCH
+        h_ref[0:LEAD, :] = jnp.zeros((LEAD, C), F32)
+        h_ref[LEAD:at, :] = sw_out[...]
+        h_ref[at : at + 1, :] = sb_out[...]
+        h_ref[at + 1 : TOWER_ROW - 1, :] = lw_out[...]
+        h_ref[TOWER_ROW - 1 :, :] = lb_out[...]
+        head_ref[...] = h_ref[...].astype(BF)
+
+
+def pipeline(count, build, work, finish, flush, bufs, outs):
+    build(0, bufs[0])
+
+    def step(s, k):
+        finish(s - 1, outs[1 - k])
+        build(jnp.minimum(s + 1, count - 1), bufs[1 - k])
+        work(s, bufs[k], outs[k])
+        flush(jnp.maximum(s - 1, 0))
+
+    def pair(i, carry):
+        step(2 * i, 0)
+        step(2 * i + 1, 1)
+        return carry
+
+    lax.fori_loop(0, count // 2, pair, 0)
+    finish(count - 1, outs[1])
+    flush(count - 1)
+
+
+def aligned(value, multiple):
+    return value if isinstance(value, int) else pl.multiple_of(value, multiple)
+
+
+def many(mask, count):
+    return jnp.concatenate([mask] * count, axis=1)
+
+
+def weight_sums(canvas, cols, edge, own, grad, source, mx_ref, sum_ref):
+    def go(x_ref):
+        def triple(n, carry):
+            at = pl.multiple_of(edge + cols * (n - 1), 16)
+            for k in range(3):
+                mask = mx_ref[n * 3 + k, edge : edge + own, :]
+                x_ref[:, k * C : k * C + C] = source[k, pl.ds(at, own), :] * many(mask, 2)
+            side = pl.ds(pl.multiple_of(n * 3 * C, C), 3 * C)
+            sum_ref[:, side] = jnp.where(canvas > 0, sum_ref[:, side], 0.0) + mm(grad(), x_ref[...])
+            return carry
+
+        lax.fori_loop(0, 3, triple, 0)
+
+    pl.run_scoped(go, pltpu.VMEM((own, 3 * C), BF))
+
 
 def head_kernel(
-    cols, rows, scal_ref, f_ref, mk_ref, lab_ref, btt_ref, e_ref, wt_ref, tb_ref, wct_ref, wb_ref,
+    cols, rows, scal_ref, f_ref, mk_ref, lab_ref, btt_ref, e_ref, full_ref, tb_ref, wct_ref, wb_ref,
     dwc_ref, dwt_ref, dwb_ref, db_ref, fg_ref, sums_ref,
-    mx_ref, x_ref, pre_ref, bt_ref, lgt_ref, lgs_ref, lg_ref, g_ref,
+    mx_ref, pre_ref, bt_ref, lgt_ref, lgs_ref, g_ref, wt_ref,
 ):
     own = rows * cols
     edge = HALO * cols
@@ -159,12 +231,12 @@
 
     @pl.when(pl.program_id(0) == 0)
     def _():
-        dwc_ref[...] = jnp.zeros_like(dwc_ref)
-        dwt_ref[...] = jnp.zeros_like(dwt_ref)
         dwb_ref[...] = jnp.zeros_like(dwb_ref)
         db_ref[...] = jnp.zeros_like(db_ref)
         sums_ref[...] = jnp.zeros_like(sums_ref)
-        lg_ref[CLS_OUT:, :] = jnp.zeros((WIDE - CLS_OUT, 256), F32)
+        for n in range(2):
+            here = TOWER_ROW + n * 9 * C
+            wt_ref[:, n * C : n * C + C] = full_ref[here : here + 9 * C, :]
 
     def spread(i, carry):
         at = pl.multiple_of(i * 384, 128)
@@ -178,10 +250,10 @@
     def twice(mask):
         return jnp.concatenate([mask, mask], axis=1)
 
-    def build(source, at, count, row):
+    def build(source, at, count, x_ref):
         for t, (di, dj) in enumerate(TAPS):
-            value = source[dj + 1, pl.ds(at + cols * di, count), :]
-            x_ref[pl.ds(row, count), t * C : (t + 1) * C] = value * twice(mx_ref[t, pl.ds(at, count), :])
+            value = source[dj + 1, pl.ds(pl.multiple_of(at + cols * di, 16), count), :]
+            x_ref[:, t * C : (t + 1) * C] = value * twice(mx_ref[t, pl.ds(at, count), :])
 
     first_tower = cols
     tower_rows = total - 2 * cols
@@ -199,18 +271,21 @@
         bt_ref[total - cols : total, :] = zero
         piece = tower_rows // 3
 
-        def tower(i, carry):
-            row = pl.multiple_of(i * piece, 16)
-            at = pl.multiple_of(first_tower + i * piece, 16)
-            build(f_ref.at[0], at, piece, row)
-            pre = mm(x_ref[pl.ds(row, piece), :], wt_ref[...]) + tb_ref[...]
-            pre_ref[pl.ds(row, piece), :] = pre
-            out = gelu(pre)
-            ct32_ref[pl.ds(pl.multiple_of(8 + at, 8), piece), :] = out[:, :C]
-            bt_ref[pl.ds(at, piece), :] = out[:, C:].astype(BF)
-            return carry
-
-        lax.fori_loop(0, 3, tower, 0)
+        def towers(x_ref):
+            def tower(i, carry):
+                row = pl.multiple_of(i * piece, 16)
+                at = pl.multiple_of(first_tower + i * piece, 16)
+                build(f_ref.at[0], at, piece, x_ref)
+                pre = mm(x_ref[...], wt_ref[...]) + tb_ref[...]
+                pre_ref[pl.ds(row, piece), :] = pre
+                out = gelu(pre)
+                ct32_ref[pl.ds(pl.multiple_of(8 + at, 8), piece), :] = out[:, :C]
+                bt_ref[pl.ds(at, piece), :] = out[:, C:].astype(BF)
+                return carry
+
+            lax.fori_loop(0, 3, tower, 0)
+
+        pl.run_scoped(towers, pltpu.VMEM((piece, 9 * C), BF))
 
         def move(i, carry):
             base = pl.multiple_of(i * edge, 16)
@@ -220,55 +295,86 @@
             return carry
 
         lax.fori_loop(0, total // edge, move, 0)
-        inv_ema = scal_ref[0]
-        number = lax.broadcasted_iota(jnp.int32, (CLASSES, 256), 0).astype(F32)
-        lane = lax.broadcasted_iota(jnp.int32, (8, 256), 1)
-
-        def logits(q, carry):
-            row = pl.multiple_of(q * 256, 128)
-            at = pl.multiple_of(first_logit + q * 256, 128)
-            build(ct_ref, at, 256, row)
-            lg_ref[0:CLS_OUT, :] = mm(wct_ref[...], x_ref[pl.ds(row, 256), :], NT) + PRIOR
-            place = lane + at
-            mine = ((place >= edge) & (place < edge + own)).astype(F32)
-
-            def focal(a, total_focal):
-                here = pl.multiple_of(a * CLASSES, 16)
-                value = lg_ref[pl.ds(here, CLASSES), :]
-                label = jnp.broadcast_to(lab_ref[0, pl.ds(a, 1), pl.ds(at, 256)], (CLASSES, 256))
-                hit = label == number
-                side = jnp.where(hit, -value, value)
-                small = jnp.exp(-jnp.abs(side))
-                ratio = 1.0 / (1.0 + small)
-                tiny = small * (1.0 - small * (0.5 - small * (1.0 / 3.0)))
-                cross = jnp.maximum(side, 0.0) + jnp.where(small < 0.01, tiny, jnp.log(1.0 + small))
-                prob = jnp.where(side >= 0.0, ratio, small * ratio)
-                square = prob * prob
-                weight = jnp.where(hit, ALPHA, 1.0 - ALPHA)
-                weight = jnp.where(label > -1.5, weight, 0.0)
-                loss = weight * square * cross
-                pull = weight * square * (2.0 * (1.0 - prob) * cross + prob) * inv_ema
-                pull = jnp.where(hit, -pull, pull)
-                lg_ref[pl.ds(here, CLASSES), :] = pull
-                lgt_ref[pl.ds(here, CLASSES), pl.ds(row, 256)] = pull.astype(BF)
-                return total_focal + jnp.sum(loss.reshape(CLASSES // 8, 8, 256), axis=0)
-
-            sums_ref[0:8, :] += lax.fori_loop(0, ANCH, focal, jnp.zeros((8, 256), F32)) * mine
-            lgs_ref[pl.ds(row, 256), :] = lg_ref[...].T.astype(BF)
-            return carry
-
-        lax.fori_loop(0, logit_cells // 256, logits, 0)
-
-        def class_weights(i, carry):
-            at = pl.multiple_of(i * 256, 128)
-            dwc_ref[:, pl.ds(at, 256)] += mm(lgt_ref[:, 256 : 256 + own], x_ref[256 : 256 + own, pl.ds(at, 256)])
-            return carry
-
-        lax.fori_loop(0, 9, class_weights, 0)
+        def logits(xa_ref, xb_ref, la_ref, lb_ref, st_ref, tt_ref):
+            inv_ema = scal_ref[0]
+            number = lax.broadcasted_iota(jnp.int32, (GROUP, 256), 0).astype(F32)
+            lane = lax.broadcasted_iota(jnp.int32, (8, 256), 1)
+            plan = column_plan()
+
+            def ready(q, x_ref):
+                build(ct_ref, pl.multiple_of(first_logit + q * 256, 128), 256, x_ref)
+
+            def work(q, x_ref, l_ref):
+                l_ref[...] = mm(wct_ref[...], x_ref[...], NT)
+
+            def focal(q, l_ref):
+                at = pl.multiple_of(first_logit + jnp.maximum(q, 0) * 256, 128)
+                spot = lane + at
+                mine = (spot >= edge) & (spot < edge + own) & (lane + q >= 0)
+                lines = [lab_ref[0, a : a + 1, pl.ds(at, 256)] for a in range(ANCH)]
+                rest = [jnp.where(line > -1.5, 1.0 - ALPHA, 0.0) for line in lines]
+                pulls = [line * inv_ema for line in rest]
+                total_focal = jnp.zeros((8, 256), F32)
+                for first in range(0, WIDE, GROUP):
+                    value = l_ref[first : first + GROUP, :] + PRIOR
+                    key = None
+                    for begin, count, anchor, klass in plan:
+                        if begin >= first + GROUP or begin + count <= first:
+                            continue
+                        if anchor < 0:
+                            parts = [jnp.full((GROUP, 256), n, F32) for n in (-2.0, 0.0, 0.0)]
+                        else:
+                            parts = [lines[anchor] - float(klass - (begin - first)), rest[anchor], pulls[anchor]]
+                            parts = [jnp.broadcast_to(part, (GROUP, 256)) for part in parts]
+                        if key is None:
+                            key, other, pull_other = parts
+                        else:
+                            later = number >= float(begin - first)
+                            key = jnp.where(later, parts[0], key)
+                            other = jnp.where(later, parts[1], other)
+                            pull_other = jnp.where(later, parts[2], pull_other)
+                    hit = key == number
+                    side = jnp.where(hit, -value, value)
+                    small = jnp.exp(-jnp.abs(side))
+                    whole_one = 1.0 + small
+                    ratio = pltpu.reciprocal(whole_one, approx=True)
+                    ratio = ratio * (2.0 - whole_one * ratio)
+                    part = small * ratio
+                    up = side >= 0.0
+                    prob = jnp.where(up, ratio, part)
+                    miss = jnp.where(up, part, ratio)
+                    tiny = small * (1.0 - 0.5 * small)
+                    cross = jnp.maximum(side, 0.0) + jnp.where(small < 0.001, tiny, jnp.log(whole_one))
+                    square = prob * prob
+                    value = square * cross * jnp.where(hit, ALPHA, other)
+                    pull = square * (2.0 * miss * cross + prob) * jnp.where(hit, -ALPHA * inv_ema, pull_other)
+                    l_ref[first : first + GROUP, :] = pull
+                    st_ref[first : first + GROUP, :] = pull.astype(BF)
+                    total_focal += jnp.sum(value.reshape(GROUP // 8, 8, 256), axis=0)
+                sums_ref[0:8, :] += jnp.where(mine, total_focal, 0.0)
+                tt_ref[...] = l_ref[...].T.astype(BF)
+
+            def flush(q):
+                row = pl.multiple_of(q * 256, 128)
+                lgt_ref[:, pl.ds(row, 256)] = st_ref[...]
+                lgs_ref[pl.ds(row, 256), :] = tt_ref[...]
+
+            pipeline(logit_cells // 256, ready, work, focal, flush, (xa_ref, xb_ref), (la_ref, lb_ref))
+
+        pl.run_scoped(
+            logits,
+            pltpu.VMEM((256, 9 * C), BF),
+            pltpu.VMEM((256, 9 * C), BF),
+            pltpu.VMEM((WIDE, 256), F32),
+            pltpu.VMEM((WIDE, 256), F32),
+            pltpu.VMEM((WIDE, 256), BF),
+            pltpu.VMEM((256, WIDE), BF),
+        )
+        weight_sums(pl.program_id(0), cols, edge, own, lambda: lgt_ref[:, 256 : 256 + own], ct_ref, mx_ref, dwc_ref)
 
     pl.run_scoped(heads, pltpu.VMEM((total + 16, C), F32), pltpu.VMEM((3, total, C), BF))
 
-    def boxes(y_ref, gg_ref, xg_ref):
+    def box_forward(gg_ref, y_ref):
         inv_norm = scal_ref[1]
 
         def outer(i, carry):
@@ -301,6 +407,8 @@
             return carry
 
         lax.fori_loop(0, 4, guess, 0)
+
+    def box_back(gg_ref, xg_ref):
         for t in range(9):
             moved = pltpu.roll(gg_ref[...], shift[t] % total, 1)
             xg_ref[t * BOX_ROWS : (t + 1) * BOX_ROWS, :] = (moved * mk_ref[0, 8 - t : 9 - t, :].astype(F32)).astype(BF)
@@ -315,12 +423,11 @@
 
         lax.fori_loop(0, g_cells // 256, into, 0)
 
-    pl.run_scoped(
-        boxes,
-        pltpu.VMEM((9 * BOX_ROWS, total), F32),
-        pltpu.VMEM((BOX_ROWS, total), F32),
-        pltpu.VMEM((9 * BOX_ROWS, total), BF),
-    )
+    def boxes(gg_ref):
+        pl.run_scoped(functools.partial(box_forward, gg_ref), pltpu.VMEM((9 * BOX_ROWS, total), F32))
+        pl.run_scoped(functools.partial(box_back, gg_ref), pltpu.VMEM((9 * BOX_ROWS, total), BF))
+
+    pl.run_scoped(boxes, pltpu.VMEM((BOX_ROWS, total), F32))
 
     def class_back(z_ref):
         z_ref[:, 0:8, :] = jnp.zeros((3, 8, C), F32)
@@ -337,7 +444,7 @@
                     mask = mx_ref[t, pl.ds(pl.multiple_of(source, 16), piece), :]
                     value = lgs_ref[pl.ds(pl.multiple_of(source - first_logit, 16), piece), :]
                     value = value * jnp.concatenate([mask] * (WIDE // LANE), axis=1)
-                    acc += mm(value[:, :CLS_OUT], wct_ref[:, t * C : t * C + C])
+                    acc += mm(value, wct_ref[:, t * C : t * C + C])
                 z_ref[k, pl.ds(pl.multiple_of(8 + row, 8), piece), :] = acc
             return carry
 
@@ -361,17 +468,10 @@
             part = g_ref[pl.ds(pl.multiple_of(edge - first_g + row, 16), 256), :].astype(F32)
             gt_ref[:, pl.ds(row, 256)] = part.T.astype(BF)
             db_ref[...] += jnp.sum(part, axis=0, keepdims=True)
-            build(f_ref.at[0], pl.multiple_of(edge + row, 16), 256, row)
             return carry
 
         lax.fori_loop(0, own // 256, flip, 0)
-
-        def tower_weights(i, carry):
-            at = pl.multiple_of(i * 256, 128)
-            dwt_ref[:, pl.ds(at, 256)] += mm(gt_ref[...], x_ref[0:own, pl.ds(at, 256)])
-            return carry
-
-        lax.fori_loop(0, 9, tower_weights, 0)
+        weight_sums(pl.program_id(0), cols, edge, own, lambda: gt_ref[...], f_ref.at[0], mx_ref, dwt_ref)
         first_z = edge - 16
         piece = (own + 32) // 2
 
@@ -418,20 +518,16 @@
     return jax.ShapeDtypeStruct(shape, dtype)
 
 
+VM = pl.BlockSpec(memory_space=pltpu.VMEM)
 VMEM_LIMIT = 63 * 1024 * 1024
 
 
-def stem_forward(patches, rim, stem_w, stem_b, lat_w, lat_b):
+def stem_forward(patches, rim, head):
     canvases, rows, width = patches.shape
     cols = width // PATCH
     pairs = 8
     steps = cols // (2 * pairs)
     chunk = 2 * pairs * PATCH
-    zero = jnp.zeros((PATCH, C), BF)
-    w2 = jnp.concatenate(
-        [jnp.concatenate([stem_w, zero], axis=1), jnp.concatenate([zero, stem_w], axis=1)], axis=0
-    )
-    b2 = jnp.concatenate([stem_b, stem_b]).astype(F32)[None]
     count = pairs * canvases * rows
     total = (rows + 2 * HALO) * cols
     return pl.pallas_call(
@@ -440,25 +536,29 @@
         in_specs=[
             pl.BlockSpec((canvases, rows, chunk), lambda s: (0, 0, s)),
             pl.BlockSpec((2 * HALO * canvases, chunk), lambda s: (0, s)),
-            whole((2 * PATCH, 2 * C)),
-            whole((1, 2 * C)),
-            whole((C, C)),
-            whole((1, C)),
+            whole(head.shape),
         ],
         out_specs=[
             pl.BlockSpec((count, 2 * C), lambda s: (s, 0)),
             pl.BlockSpec((count, 2 * C), lambda s: (s, 0)),
             whole((canvases, 3, total, C)),
+            whole((C, C)),
         ],
         out_shape=[
             shape_of((steps * count, 2 * C)),
             shape_of((steps * count, 2 * C), BF),
             shape_of((canvases, 3, total, C), BF),
-        ],
-        scratch_shapes=[pltpu.VMEM((canvases, 2, total + 16, LANE), F32)],
+            shape_of((C, C), BF),
+        ],
+        scratch_shapes=[
+            pltpu.VMEM((canvases, 2, total + 16, LANE), F32),
+            pltpu.VMEM((2 * PATCH, 2 * C), BF),
+            pltpu.VMEM((1, 2 * C), F32),
+            pltpu.VMEM((1, C), F32),
+        ],
         compiler_params=pltpu.CompilerParams(vmem_limit_bytes=VMEM_LIMIT),
         name="stem",
-    )(patches, rim, w2, b2, lat_w, lat_b.astype(F32)[None])
+    )(patches, rim, head)
 
 
 def stem_backward(patches, feature_grad, stem_out, stem_pre, lat_w):
@@ -478,14 +578,92 @@
             pl.BlockSpec((count, 2 * C), lambda s: (s, 0)),
             whole((C, C)),
         ],
-        out_specs=[whole((PATCH, C)), whole((1, C)), whole((C, C)), whole((1, C))],
-        out_shape=[shape_of((PATCH, C)), shape_of((1, C)), shape_of((C, C)), shape_of((1, C))],
+        out_specs=whole((TOWER_ROW, C)),
+        out_shape=shape_of((TOWER_ROW, C), BF),
+        scratch_shapes=[
+            pltpu.VMEM((PATCH, C), F32),
+            pltpu.VMEM((1, C), F32),
+            pltpu.VMEM((C, C), F32),
+            pltpu.VMEM((1, C), F32),
+            pltpu.VMEM((TOWER_ROW, C), F32),
+        ],
         compiler_params=pltpu.CompilerParams(vmem_limit_bytes=VMEM_LIMIT),
         name="stem_back",
     )(patches, feature_grad, stem_out, stem_pre, lat_w)
 
 
-def heads_call(rows, cols, scal, feats, masks, labels, box_target, wt, tb, wct, wb):
+BOX_CUTS = [(BOX_OUT * n // C, BOX_OUT * n % C) for n in range(64)]
+
+
+def box_in_kernel(tail_ref, o_ref, t_ref, d_ref, u_ref):
+    tail = tail_ref[...].astype(F32)
+    count = tail.shape[0]
+    lane = lax.broadcasted_iota(jnp.int32, (40, LANE), 1)
+    for n in range(2):
+        t_ref[n, 0:count, :] = tail[:, n * LANE : n * LANE + LANE]
+        t_ref[n, count:, :] = jnp.zeros((t_ref.shape[1] - count, LANE), F32)
+    lines = []
+    for r in range(9):
+        lines.append(jnp.concatenate([t_ref[n, pl.ds(2 + r, 40, stride=9), :] for n in range(2)], axis=1))
+    for s, (r, at) in enumerate(BOX_CUTS):
+        wide = jnp.concatenate([lines[r], lines[min(r + 1, 8)]], axis=1)
+        d_ref[pl.ds(s, 40, stride=64), :] = jnp.where(lane < BOX_OUT, wide[:, at : at + LANE], 0.0)
+    for t in range(9):
+        turned = d_ref[t * C : t * C + C, :].T
+        for n in range(2):
+            u_ref[n] = turned[:, n * LANE : n * LANE + LANE]
+        for m in range(4):
+            here = t * BOX_ROWS + m * SLOT
+            parts = [u_ref[n, pl.ds(m, SLOT, stride=4), :] for n in range(2)]
+            o_ref[here : here + SLOT, :] = jnp.concatenate(parts, axis=1).astype(BF)
+
+
+def box_out_kernel(w_ref, b_ref, o_ref, t_ref, d_ref, u_ref):
+    u_ref[...] = jnp.zeros_like(u_ref)
+    d_ref[9 * C :, :] = jnp.zeros((d_ref.shape[0] - 9 * C, LANE), F32)
+    for t in range(9):
+        for m in range(4):
+            here = t * BOX_ROWS + m * SLOT
+            for n in range(2):
+                u_ref[n, pl.ds(m, SLOT, stride=4), :] = w_ref[here : here + SLOT, n * LANE : n * LANE + LANE]
+        d_ref[t * C : t * C + C, :] = jnp.concatenate([u_ref[0], u_ref[1]], axis=1).T
+    lines = [jnp.zeros((40, 2 * C), F32) for _ in range(9)]
+    zero = jnp.zeros((40, 2 * C - LANE), F32)
+    for s, (r, at) in enumerate(BOX_CUTS):
+        wide = jnp.concatenate([d_ref[pl.ds(s, 40, stride=64), :], zero], axis=1)
+        lines[r] = lines[r] + (pltpu.roll(wide, at, 1) if at else wide)
+    t_ref[...] = jnp.zeros_like(t_ref)
+    for r in range(9):
+        line = lines[r][:, :C]
+        if r:
+            line = line + lines[r - 1][:, C:]
+        for n in range(2):
+            t_ref[n, pl.ds(2 + r, 40, stride=9), :] = line[:, n * LANE : n * LANE + LANE]
+    for n in range(2):
+        for k in range(2):
+            at = k * C + n * LANE
+            t_ref[n, k : k + 1, :] = b_ref[:, at : at + LANE]
+    rows = o_ref.shape[0]
+    o_ref[...] = jnp.concatenate([t_ref[0, 0:rows, :], t_ref[1, 0:rows, :]], axis=1).astype(BF)
+
+
+def box_call(kernel, shape, kind, name, *args):
+    return pl.pallas_call(
+        kernel,
+        in_specs=[VM] * len(args),
+        out_specs=VM,
+        out_shape=shape_of(shape, kind),
+        scratch_shapes=[
+            pltpu.VMEM((2, 368, LANE), F32),
+            pltpu.VMEM((40 * 64, LANE), F32),
+            pltpu.VMEM((2, LANE, LANE), F32),
+        ],
+        compiler_params=pltpu.CompilerParams(vmem_limit_bytes=VMEM_LIMIT),
+        name=name,
+    )(*args)
+
+
+def heads_call(rows, cols, scal, feats, masks, labels, box_target, full, tb, wct, wb):
     canvases = feats.shape[0]
     own = rows * cols
     total = own + 2 * HALO * cols
@@ -504,13 +682,13 @@
             per((SLOT, total)),
             per((4, SLOT, total)),
             whole(spread.shape),
-            whole(wt.shape),
+            whole(full.shape),
             whole(tb.shape),
             whole(wct.shape),
             whole(wb.shape),
         ],
         out_specs=[
-            whole((CLS_OUT, 9 * C)),
+            whole((WIDE, 9 * C)),
             whole((2 * C, 9 * C)),
             whole((9 * BOX_ROWS, C)),
             whole((1, 2 * C)),
@@ -518,7 +696,7 @@
             whole((16, 256)),
         ],
         out_shape=[
-            shape_of((CLS_OUT, 9 * C)),
+            shape_of((WIDE, 9 * C)),
             shape_of((2 * C, 9 * C)),
             shape_of((9 * BOX_ROWS, C)),
             shape_of((1, 2 * C)),
@@ -527,35 +705,378 @@
         ],
         scratch_shapes=[
             pltpu.VMEM((9, total, LANE), BF),
-            pltpu.VMEM((total - 2 * cols, 9 * C), BF),
             pltpu.VMEM((total - 2 * cols, 2 * C), F32),
             pltpu.VMEM((total, C), BF),
-            pltpu.VMEM((CLS_OUT, own + 512), BF),
+            pltpu.VMEM((WIDE, own + 512), BF),
             pltpu.VMEM((own + 512, WIDE), BF),
-            pltpu.VMEM((WIDE, 256), F32),
             pltpu.VMEM((own + 256, 2 * C), BF),
+            pltpu.VMEM((9 * C, 2 * C), BF),
         ],
         compiler_params=pltpu.CompilerParams(vmem_limit_bytes=VMEM_LIMIT),
         name="heads",
-    )(scal, feats, masks, labels, box_target, spread, wt, tb, wct, wb)
-
-
-def unpack(flat_values):
-    lengths = [PATCH * C, C, C * C, C, 18 * C * C, 2 * C, 9 * C * BOX_OUT]
-    pieces = []
-    offset = 0
-    for length in lengths:
-        pieces.append(flat_values[offset : offset + length])
-        offset = offset + length
-    return (
-        pieces[0].reshape(PATCH, C),
-        pieces[1],
-        pieces[2].reshape(C, C),
-        pieces[3],
-        pieces[4].reshape(2, 9, C, C),
-        pieces[5].reshape(2, C),
-        pieces[6].reshape(9, C, BOX_OUT),
+    )(scal, feats, masks, labels, box_target, spread, full, tb, wct, wb)
+
+
+def place():
+    img = lax.axis_index("img")
+    cls = lax.axis_index("cls")
+    return img // 2, img % 2, cls // 2, cls % 2
+
+
+def target(z, y, x, c):
+    return (z * 2 + y, x * 2 + c)
+
+
+def owner(z, y, x, c):
+    return ((z * 2 + y) * 2 + x) * 2 + c
+
+
+def enter(peers):
+    barrier = pltpu.get_barrier_semaphore()
+    for peer in peers:
+        pl.semaphore_signal(barrier, inc=1, device_id=peer, device_id_type=MESH)
+    pl.semaphore_wait(barrier, len(peers))
+
+
+class Mail:
+    def __init__(self, send_sems, recv_sems):
+        self.send_sems, self.recv_sems, self.used, self.sent = send_sems, recv_sems, 0, []
+
+    def push(self, source, landing, peer):
+        copy = pltpu.make_async_remote_copy(
+            src_ref=source,
+            dst_ref=landing,
+            send_sem=self.send_sems.at[self.used],
+            recv_sem=self.recv_sems.at[self.used],
+            device_id=peer,
+            device_id_type=MESH,
+        )
+        self.used += 1
+        copy.start()
+        self.sent.append(copy)
+        return copy
+
+    def close(self):
+        for copy in self.sent:
+            copy.wait_send()
+
+
+def window_row(index, shard):
+    return pl.multiple_of((index * shard + LEAD * C) // (16 * C) * 16, 16)
+
+
+def gather_kernel(shard, s_ref, k_ref, n_ref, full_ref, head_ref, count_ref, first_ref, last_ref, sh_ref, kx_ref, send_sems, recv_sems):
+    z, y, x, c = place()
+    block = k_ref.shape[0]
+    win = s_ref.shape[0]
+    others = [(k, j) for k in range(4) for j in range(2) if k or j]
+    ring = [((z + k) % 4, (y + j) % 2) for k, j in others]
+    enter([target(zz, yy, x, c) for zz, yy in ring] + [target(z, y, 1 - x, c), target(z, y, x, 1 - c)])
+    mail = Mail(send_sems, recv_sems)
+    me = owner(z, y, x, c)
+
+    def rows(zz, yy):
+        return pl.ds(pl.multiple_of((zz * 2 + yy) * block, 16), block)
+
+    def lanes(cc):
+        return pl.ds(pl.multiple_of(cc * HALF, LANE), HALF)
+
+    got_kx = mail.push(k_ref, kx_ref, target(z, y, 1 - x, c))
+    counts = [mail.push(n_ref, count_ref.at[z * 2 + y], target(zz, yy, x, c)) for zz, yy in ring]
+    slot = sh_ref.at[me]
+    got_z = [mail.push(s_ref, slot, target((z + k) % 4, y, x, c)) for k in range(1, 4)]
+    got_y = [mail.push(s_ref, slot, target(z, 1 - y, x, c))]
+    got_x = [mail.push(s_ref, slot, target(z, y, 1 - x, c))]
+    got_c = [mail.push(s_ref, slot, target(z, y, x, 1 - c))]
+    count_ref[z * 2 + y] = n_ref[...]
+    sh_ref[me] = s_ref[...]
+
+    got_kx.wait_recv()
+    mine = head_ref.at[rows(z, y), lanes(c)]
+    head_ref[rows(z, y), lanes(c)] = k_ref[...] + kx_ref[...]
+    got_kz = [mail.push(mine, mine, target((z + k) % 4, y, x, c)) for k in range(1, 4)]
+    got_ky = [mail.push(mine, mine, target(z, 1 - y, x, c))]
+    got_kc = [mail.push(mine, mine, target(z, y, x, 1 - c))]
+
+    for k in range(1, 4):
+        got_z[k - 1].wait_recv()
+        slot = sh_ref.at[owner((z + 4 - k) % 4, y, x, c)]
+        got_y.append(mail.push(slot, slot, target(z, 1 - y, x, c)))
+        got_x.append(mail.push(slot, slot, target(z, y, 1 - x, c)))
+        got_c.append(mail.push(slot, slot, target(z, y, x, 1 - c)))
+    for k in range(1, 4):
+        got_kz[k - 1].wait_recv()
+        part = head_ref.at[rows((z + 4 - k) % 4, y), lanes(c)]
+        got_ky.append(mail.push(part, part, target(z, 1 - y, x, c)))
+        got_kc.append(mail.push(part, part, target(z, y, x, 1 - c)))
+    for k in range(4):
+        got_y[k].wait_recv()
+        slot = sh_ref.at[owner((z + 4 - k) % 4, 1 - y, x, c)]
+        got_x.append(mail.push(slot, slot, target(z, y, 1 - x, c)))
+        got_c.append(mail.push(slot, slot, target(z, y, x, 1 - c)))
+    for k in range(4):
+        got_ky[k].wait_recv()
+        part = head_ref.at[rows((z + 4 - k) % 4, 1 - y), lanes(c)]
+        got_kc.append(mail.push(part, part, target(z, y, x, 1 - c)))
+    for k in range(8):
+        got_x[k].wait_recv()
+        slot = sh_ref.at[owner((z + 4 - k % 4) % 4, (y + k // 4) % 2, 1 - x, c)]
+        got_c.append(mail.push(slot, slot, target(z, y, x, 1 - c)))
+    for copy in got_c + got_kc + counts:
+        copy.wait_recv()
+    full_ref[...] = jnp.zeros_like(full_ref)
+
+    def merge(d, carry):
+        full_ref[pl.ds(window_row(d, shard), win), :] += sh_ref[d]
+        return carry
+
+    lax.fori_loop(0, 32, merge, 0)
+    first_ref[...] = full_ref[0:TOWER_ROW, :]
+    last_ref[...] = full_ref[TAIL_ROW:FULL_ROWS, :]
+    mail.close()
+
+
+def scatter_kernel(
+    shard, head_ref, tower_ref, tail_ref, k_ref, n_ref, s_out, k_out, n_out,
+    full_ref, sc_ref, sx_ref, sy_ref, sz_ref, kc_ref, ky_ref, kz_ref, kx_ref, mine_ref, peer_ref, far_ref, nz_ref, send_sems, recv_sems,
+):
+    z, y, x, c = place()
+    block = kx_ref.shape[1]
+    win = s_out.shape[0]
+    enter([target((z + k) % 4, y, x, c) for k in range(1, 4)] + [target(z, 1 - y, x, c), target(z, y, 1 - x, c), target(z, y, x, 1 - c)])
+    mail = Mail(send_sems, recv_sems)
+
+    def rows(zz, yy):
+        return pl.ds(pl.multiple_of((zz * 2 + yy) * block, 16), block)
+
+    def lanes(cc):
+        return pl.ds(pl.multiple_of(cc * HALF, LANE), HALF)
+
+    def window(zz, yy, xx, cc):
+        return pl.ds(window_row(owner(zz, yy, xx, cc), shard), win)
+
+    mine_ref[0] = n_ref[...]
+    sum_c = mail.push(mine_ref.at[0], peer_ref.at[0], target(z, y, x, 1 - c))
+    spots = [(j, k) for j in (1, 0) for k in (1, 2, 3, 0)]
+    got_kc = []
+    for n, (j, k) in enumerate(spots):
+        part = k_ref.at[rows((z + k) % 4, (y + j) % 2), lanes(1 - c)]
+        got_kc.append(mail.push(part, kc_ref.at[n], target(z, y, x, 1 - c)))
+    full_ref[0:TOWER_ROW, :] = head_ref[...]
+    full_ref[TOWER_ROW:TAIL_ROW, :] = tower_ref[...]
+    full_ref[TAIL_ROW:FULL_ROWS, :] = tail_ref[...]
+    got_c = []
+    for i in (1, 0):
+        for n, (j, k) in enumerate(spots):
+            part = full_ref.at[window((z + k) % 4, (y + j) % 2, (x + i) % 2, 1 - c), :]
+            got_c.append(mail.push(part, sc_ref.at[(1 - i) * 8 + n], target(z, y, x, 1 - c)))
+
+    sum_c.wait_recv()
+    mine_ref[1] = mine_ref[0] + peer_ref[0]
+    sum_x = mail.push(mine_ref.at[1], peer_ref.at[1], target(z, y, 1 - x, c))
+
+    got_ky = []
+    for n, (j, k) in enumerate(spots):
+        got_kc[n].wait_recv()
+        kc_ref[n] = kc_ref[n] + k_ref[rows((z + k) % 4, (y + j) % 2), lanes(c)]
+        if j == 1:
+            got_ky.append(mail.push(kc_ref.at[n], ky_ref.at[n], target(z, 1 - y, x, c)))
+    got_x = []
+    for n, (j, k) in enumerate(spots):
+        got_c[n].wait_recv()
+        sc_ref[n] = sc_ref[n] + full_ref[window((z + k) % 4, (y + j) % 2, 1 - x, c), :]
+        got_x.append(mail.push(sc_ref.at[n], sx_ref.at[n], target(z, y, 1 - x, c)))
+
+    sum_x.wait_recv()
+    mine_ref[2] = mine_ref[1] + peer_ref[1]
+    sum_y = mail.push(mine_ref.at[2], peer_ref.at[2], target(z, 1 - y, x, c))
+
+    got_kz = []
+    for n in range(4):
+        got_ky[n].wait_recv()
+        kc_ref[4 + n] = kc_ref[4 + n] + ky_ref[n]
+        if n < 3:
+            got_kz.append(mail.push(kc_ref.at[4 + n], kz_ref.at[n], target((z + n + 1) % 4, y, x, c)))
+    got_y = []
+    for n, (j, k) in enumerate(spots):
+        got_c[8 + n].wait_recv()
+        got_x[n].wait_recv()
+        total = sc_ref[8 + n].astype(F32) + full_ref[window((z + k) % 4, (y + j) % 2, x, c), :].astype(F32)
+        sc_ref[8 + n] = (total + sx_ref[n].astype(F32)).astype(BF)
+        if j == 1:
+            got_y.append(mail.push(sc_ref.at[8 + n], sy_ref.at[n], target(z, 1 - y, x, c)))
+
+    sum_y.wait_recv()
+    mine_ref[3] = mine_ref[2] + peer_ref[2]
+    nz_ref[z] = mine_ref[3]
+    sum_z = [mail.push(mine_ref.at[3], nz_ref.at[z], target((z + k) % 4, y, x, c)) for k in range(1, 4)]
+
+    total = kc_ref[7].astype(F32)
+    for n in range(3):
+        got_kz[n].wait_recv()
+        total += kz_ref[n].astype(F32)
+    kx_ref[0] = total.astype(BF)
+    got_kx = mail.push(kx_ref.at[0], kx_ref.at[1], target(z, y, 1 - x, c))
+    got_z = []
+    for n in range(4):
+        got_y[n].wait_recv()
+        sc_ref[12 + n] = sc_ref[12 + n] + sy_ref[n]
+        if n < 3:
+            got_z.append(mail.push(sc_ref.at[12 + n], sz_ref.at[n], target((z + n + 1) % 4, y, x, c)))
+    total = sc_ref[15].astype(F32)
+    for n in range(3):
+        got_z[n].wait_recv()
+        total += sz_ref[n].astype(F32)
+    s_out[...] = total
+    for copy in sum_z:
+        copy.wait_recv()
+    n_out[...] = (nz_ref[0] + nz_ref[1]) + (nz_ref[2] + nz_ref[3])
+    got_kx.wait_recv()
+    k_out[...] = kx_ref[0].astype(F32) + kx_ref[1].astype(F32)
+    mail.close()
+
+
+def fast_mesh(img_parts, cls_parts, class_rows):
+    return img_parts == 8 and cls_parts == 4 and class_rows % 16 == 0
+
+
+def flat_place(index, shard):
+    return (index * shard + LEAD * C) % (16 * C)
+
+
+def gather_all(shared_params, class_params, count):
+    img, cls = lax.axis_index("img"), lax.axis_index("cls")
+    img_parts, cls_parts = lax.axis_size("img"), lax.axis_size("cls")
+    shard = shared_params.shape[0]
+    block, part = class_params.shape
+    if not fast_mesh(img_parts, cls_parts, block):
+        flat = lax.all_gather(shared_params.astype(BF), ("img", "cls"), axis=0, tiled=True)
+        full = jnp.pad(flat, (LEAD * C, FULL_ROWS * C - LEAD * C - flat.shape[0])).reshape(FULL_ROWS, C)
+        head = lax.all_gather(class_params.astype(BF), ("img", "cls"), axis=0)
+        head = head.reshape(img_parts, cls_parts, block, part).transpose(0, 2, 1, 3).reshape(-1, CLS_OUT)
+        pieces = []
+        for half in range(2):
+            pieces += [head[:, 180 * half : 180 * half + 180], head[:, 360 + 180 * half : 540 + 180 * half]]
+            pieces.append(jnp.zeros((head.shape[0], HALF - 360), BF))
+        return full, full[:TOWER_ROW], full[TAIL_ROW:], jnp.concatenate(pieces, axis=1), lax.psum(count, "img")
+    rows = -(-(shard + 16 * C) // (16 * C)) * 16
+    window = lax.dynamic_update_slice(
+        jnp.zeros((rows * C,), BF), shared_params.astype(BF), (flat_place(img * cls_parts + cls, shard),)
+    ).reshape(rows, C)
+    wide = jnp.pad(class_params.astype(BF), ((0, 0), (part, HALF - part)))
+    wide = lax.dynamic_slice_in_dim(
+        jnp.pad(wide, ((0, 0), (0, part))), jnp.where(cls // 2 == 0, part, 0), HALF, 1
     )
+    number = jnp.broadcast_to(count, (8, LANE))
+    full, head, counts, first, last = pl.pallas_call(
+        functools.partial(gather_kernel, shard),
+        in_specs=[VM, VM, VM],
+        out_specs=[VM] * 5,
+        out_shape=[
+            shape_of((FULL_ROWS, C), BF),
+            shape_of((img_parts * block, 2 * HALF), BF),
+            shape_of((img_parts, 8, LANE)),
+            shape_of((TOWER_ROW, C), BF),
+            shape_of((FULL_ROWS - TAIL_ROW, C), BF),
+        ],
+        scratch_shapes=[
+            pltpu.VMEM((img_parts * cls_parts, rows, C), BF),
+            pltpu.VMEM((block, HALF), BF),
+            pltpu.SemaphoreType.DMA((54,)),
+            pltpu.SemaphoreType.DMA((54,)),
+        ],
+        compiler_params=pltpu.CompilerParams(collective_id=0, has_side_effects=True, vmem_limit_bytes=VMEM_LIMIT),
+        name="gather",
+    )(window, wide, number)
+    return full, first, last, head, jnp.sum(counts[:, 0, 0])
+
+
+def scatter_all(head, tower, tail, class_grad, sums, shard, block, part):
+    img, cls = lax.axis_index("img"), lax.axis_index("cls")
+    img_parts, cls_parts = lax.axis_size("img"), lax.axis_size("cls")
+    if not fast_mesh(img_parts, cls_parts, block):
+        flat = jnp.concatenate([head, tower, tail], axis=0).reshape(-1)
+        flat = flat[LEAD * C : LEAD * C + shard * img_parts * cls_parts].astype(F32)
+        shared = lax.psum_scatter(flat, ("img", "cls"), scatter_dimension=0, tiled=True)
+        pieces = [class_grad[:, at : at + 180] for at in (0, HALF, 180, HALF + 180)]
+        whole_grad = lax.psum_scatter(
+            jnp.concatenate(pieces, axis=1).astype(F32), "img", scatter_dimension=0, tiled=True
+        )
+        return shared, lax.psum_scatter(whole_grad, "cls", scatter_dimension=1, tiled=True), lax.psum(sums, ("img", "cls"))
+    rows = -(-(shard + 16 * C) // (16 * C)) * 16
+    window, wide, sums = pl.pallas_call(
+        functools.partial(scatter_kernel, shard),
+        in_specs=[VM] * 5,
+        out_specs=[VM] * 3,
+        out_shape=[shape_of((rows, C)), shape_of((block, HALF)), shape_of(sums.shape)],
+        scratch_shapes=[
+            pltpu.VMEM((FULL_ROWS, C), BF),
+            pltpu.VMEM((16, rows, C), BF),
+            pltpu.VMEM((8, rows, C), BF),
+            pltpu.VMEM((4, rows, C), BF),
+            pltpu.VMEM((3, rows, C), BF),
+            pltpu.VMEM((8, block, HALF), BF),
+            pltpu.VMEM((4, block, HALF), BF),
+            pltpu.VMEM((3, block, HALF), BF),
+            pltpu.VMEM((2, block, HALF), BF),
+            pltpu.VMEM((4,) + sums.shape, F32),
+            pltpu.VMEM((3,) + sums.shape, F32),
+            pltpu.VMEM((8, LANE), F32),
+            pltpu.VMEM((4,) + sums.shape, F32),
+            pltpu.SemaphoreType.DMA((53,)),
+            pltpu.SemaphoreType.DMA((53,)),
+        ],
+        compiler_params=pltpu.CompilerParams(collective_id=1, has_side_effects=True, vmem_limit_bytes=VMEM_LIMIT),
+        name="scatter",
+    )(head, tower, tail, class_grad, sums)
+    flat = lax.dynamic_slice_in_dim(window.reshape(-1), flat_place(img * cls_parts + cls, shard), shard)
+    grad = lax.dynamic_slice_in_dim(wide, jnp.where(cls // 2 == 0, 0, part), part, 1)
+    return flat, grad, sums
+
+
+def turn_kernel(k_ref, o_ref):
+    o_ref[...] = k_ref[...].T
+
+
+def turn(head):
+    return pl.pallas_call(
+        turn_kernel,
+        grid=(9,),
+        in_specs=[pl.BlockSpec((C, 2 * HALF), lambda t: (t, 0))],
+        out_specs=pl.BlockSpec((2 * HALF, C), lambda t: (0, t)),
+        out_shape=shape_of((2 * HALF, 9 * C), BF),
+        name="turn",
+    )(head)
+
+
+def turn_back_kernel(k_ref, t_ref, ko_ref, to_ref):
+    ko_ref[...] = k_ref[...].astype(BF).T
+    for n in range(2):
+        to_ref[n] = t_ref[n * C : n * C + C, :].astype(BF).T
+
+
+def turn_back(class_grad, tower_grad):
+    return pl.pallas_call(
+        turn_back_kernel,
+        grid=(9,),
+        in_specs=[pl.BlockSpec((2 * HALF, C), lambda t: (0, t)), pl.BlockSpec((2 * C, C), lambda t: (0, t))],
+        out_specs=[pl.BlockSpec((C, 2 * HALF), lambda t: (t, 0)), pl.BlockSpec((2, C, C), lambda t: (0, t, 0))],
+        out_shape=[shape_of((9 * C, 2 * HALF), BF), shape_of((2, 9 * C, C), BF)],
+        name="turn_back",
+    )(class_grad, tower_grad)
+
+
+def column_plan():
+    plan = []
+    for half in range(2):
+        for group in range(2):
+            column, row, end = 360 * group + 180 * half, HALF * half + 180 * group, 360 * group + 180 * half + 180
+            while column < end:
+                count = min(end, (column // CLASSES + 1) * CLASSES) - column
+                plan.append((row, count, column // CLASSES, column % CLASSES))
+                column, row = column + count, row + count
+        plan.append((HALF * half + 360, HALF - 360, -1, 0))
+    return plan
 
 
 def adamw_update(weight, first, second, grad):
@@ -565,6 +1086,16 @@
     second_hat = second_new / (1.0 - MOMENT_TWO**STEP)
     weight_new = weight - RATE * (first_hat / (jnp.sqrt(second_hat) + EPSILON) + DECAY * weight)
     return (weight_new, first_new, second_new)
+
+
+def valid_positives(boxes, match, full_rows, cols):
+    place = jnp.arange(full_rows * cols, dtype=jnp.int32)
+    row, col = place // cols, place % cols
+    inside = jnp.zeros((boxes.shape[0], full_rows * cols), bool)
+    for k in range(boxes.shape[1]):
+        edge = boxes[:, k, :, None]
+        inside |= (row >= edge[:, 0]) & (row < edge[:, 2]) & (col >= edge[:, 1]) & (col < edge[:, 3])
+    return ((match >= 0) & inside[:, None]).astype(F32)
 
 
 def cell_data(boxes, match, gt_labels, gt_deltas, first_row, rows, cols):
@@ -604,44 +1135,29 @@
     cls_parts = lax.axis_size("cls")
     canvases, rows, width = patches.shape
     cols = width // PATCH
-    own = rows * cols
-    edge = HALO * cols
     masks, labels, targets = cell_data(boxes, match, gt_labels, gt_deltas, cls_rank * rows, rows, cols)
-    count = jnp.sum((labels[:, :, edge : edge + own] >= 0.0).astype(F32))
-    positives = lax.psum(count, ("img", "cls"))
+    full_rows = match.shape[2] // cols
+    count = jnp.sum(valid_positives(boxes, match, full_rows, cols))
+    full, first, last, head, positives = gather_all(shared_params, class_params, count)
     norm = jnp.maximum(positives, 1.0)
     ema_new = EMA_KEEP * ema_old + (1.0 - EMA_KEEP) * norm
-
-    all_weights = lax.all_gather(shared_params.astype(BF), ("img", "cls"), axis=0, tiled=True)
-    class_w = lax.all_gather(class_params.astype(BF), ("img", "cls"), axis=0)
-    class_w = class_w.reshape(-1, cls_parts, *class_params.shape).transpose(0, 2, 1, 3).reshape(9, C, CLS_OUT)
     down = lax.ppermute(patches[:, rows - HALO :], "cls", [(i, i + 1) for i in range(cls_parts - 1)])
     up = lax.ppermute(patches[:, :HALO], "cls", [(i + 1, i) for i in range(cls_parts - 1)])
     rim = jnp.concatenate([down, up], axis=1).reshape(canvases * 2 * HALO, width)
-
-    stem_w, stem_b, lat_w, lat_b, tower_w, tower_b, box_w = unpack(all_weights)
-    stem_pre, stem_out, feats = stem_forward(patches, rim, stem_w, stem_b, lat_w, lat_b)
-    wt = jnp.concatenate([tower_w[0].reshape(9 * C, C), tower_w[1].reshape(9 * C, C)], axis=1)
-    tb = tower_b.reshape(1, 2 * C).astype(F32)
-    wct = class_w.transpose(2, 0, 1).reshape(CLS_OUT, 9 * C)
-    wb = jnp.pad(box_w.reshape(9, C, ANCH, 4).transpose(0, 3, 2, 1), ((0, 0), (0, 0), (0, SLOT - ANCH), (0, 0)))
-    wb = wb.reshape(9 * BOX_ROWS, C)
+    tb = last[0:2].reshape(1, 2 * C).astype(F32)
+    wb = box_call(box_in_kernel, (9 * BOX_ROWS, C), BF, "box_in", last)
+    stem_pre, stem_out, feats, lat_w = stem_forward(patches, rim, first)
     scal = jnp.stack([1.0 / ema_new, 1.0 / norm])
     dwc, dwt, dwb, db, feature_grad, sums = heads_call(
-        rows, cols, scal, feats, masks, labels, targets, wt, tb, wct, wb
+        rows, cols, scal, feats, masks, labels, targets, full, tb, turn(head), wb
     )
-    stem_g, stem_bg, lat_g, lat_bg = stem_backward(patches, feature_grad, stem_out, stem_pre, lat_w)
-    focal, huber = lax.psum((jnp.sum(sums[0:8]), jnp.sum(sums[8:16])), ("img", "cls"))
-    loss = focal / ema_new + huber / norm
-
-    tower_g = dwt.reshape(2, C, 9 * C).transpose(0, 2, 1)
-    box_g = dwb.reshape(9, 4, SLOT, C)[:, :, :ANCH].transpose(0, 3, 2, 1)
-    flat = jnp.concatenate(
-        [stem_g.reshape(-1), stem_bg.reshape(-1), lat_g.reshape(-1), lat_bg.reshape(-1), tower_g.reshape(-1), db.reshape(-1), box_g.reshape(-1)]
+    first_grad = stem_backward(patches, feature_grad, stem_out, stem_pre, lat_w)
+    class_turned, tower_turned = turn_back(dwc, dwt)
+    last_grad = box_call(box_out_kernel, last.shape, BF, "box_out", dwb, db)
+    shared_grad, class_grad, sums = scatter_all(
+        first_grad, tower_turned.reshape(18 * C, C), last_grad, class_turned, sums, shared_params.shape[0], *class_params.shape
     )
-    shared_grad = lax.psum_scatter(flat, ("img", "cls"), scatter_dimension=0, tiled=True)
-    class_sum = lax.psum_scatter(dwc.T, "img", scatter_dimension=0, tiled=True)
-    class_grad = lax.psum_scatter(class_sum, "cls", scatter_dimension=1, tiled=True)
+    loss = jnp.sum(sums[0:8]) / ema_new + jnp.sum(sums[8:16]) / norm
     return (
         loss,
         ema_new,

time: 686 us -> 318 us (0.46)
  waiting for transfers between devices: 218 us -> 0.01 us
  local copies, waits for them, and re-layouts: 148 us -> 14 us
  Pallas kernels: 159 us -> 274 us
  blocking collectives: 107 us -> 0 us
  between operations: 19.9 us -> 6.08 us
    unnamed x8 -> x0, waiting for transfers between devices: 196 us -> none
    pallas_call x0 -> x6, Pallas kernels: none -> 123 us  [the longest x1 49.8 us: scatter_all(): pl.pallas_call(functools.partial(scatter_kernel, shard), in_specs=[VM] *...]
    psum x2 -> x0, blocking collectives: 85.9 us -> none  [the longest x1 44.2 us: local(): positives = lax.psum(count, ('img', 'cls'))]
    unnamed x60 -> x38, local copies, waits for them, and re-layouts: 92.1 us -> 6.33 us
    reshape x5 -> x1, local copies, waits for them, and re-layouts: 38.4 us -> 0.68 us  [gather_all(): window = lax.dynamic_update_slice(jnp.zeros((rows * C,), BF), shared_para...]
    all_gather x1 -> x0, waiting for transfers between devices: 22.2 us -> none  [local(): class_w = lax.all_gather(class_params.astype(BF), ('img', 'cls'), axis=0)]
    unnamed x1 -> x0, blocking collectives: 21.6 us -> none
    another operation x2 -> x1, local copies, waits for them, and re-layouts: 7.73 us -> 0.01 us  [valid_positives(): edge = boxes[:, k, :, None]]
  transfers between devices with their start and end apart: 7 -> 2, of which waited for: 3 -> 0; matrix products, arithmetic and copies ran while one was open for 23% -> 7% of each run, Pallas kernels for 3% -> 19%
where the time goes in v2:
time: 318 us; the launch traced here: 316 us
  Pallas kernels  274 us (86%)
  other arithmetic  17.5 us (6%)
  local copies, waits for them, and re-layouts  14 us (4%)
  between operations  6.08 us (2%)
  starting transfers between devices  4.49 us (1%)
    pallas_call x1, Pallas kernels, heads_call(): pl.pallas_call(functools.partial(head_kernel, cols, rows), grid=(canvases...  129 us
    pallas_call x1, Pallas kernels, scatter_all(): pl.pallas_call(functools.partial(scatter_kernel, shard), in_specs=[VM] *...  49.8 us
    pallas_call x1, Pallas kernels, gather_all(): pl.pallas_call(functools.partial(gather_kernel, shard), in_specs=[VM, VM,...  49 us
    pallas_call x1, Pallas kernels, stem_forward(): pl.pallas_call(functools.partial(stem_kernel, pairs, cols, rows), grid=(s...  13.8 us
    pallas_call x1, Pallas kernels, turn_back(): pl.pallas_call(turn_back_kernel, grid=(9,), in_specs=[pl.BlockSpec((2 * H...  10.2 us
    pallas_call x1, Pallas kernels, stem_backward(): pl.pallas_call(functools.partial(stem_back_kernel, pairs, cols, rows), gr...  9.4 us
    pallas_call x1, Pallas kernels, turn(): pl.pallas_call(turn_kernel, grid=(9,), in_specs=[pl.BlockSpec((C, 2 * HAL...  7.43 us
  transfers between devices with their start and end apart: 2, of which 0 were waited for; matrix products, arithmetic and copies ran while one was open for 7% of the time, Pallas kernels for 19%

profile of v2, /device:TPU:0, one launch (start us, length us, event | category | flops | bytes accessed | tf_op | source)
XLA Modules:
  0.0 316.4 jit_solution(15919376554331831640)
XLA Ops:
  0.7 2.4 fusion.52
  3.0 3.2 %collective-permute-start = (bf16[2,4,18432]{2,1,0:T(4,128)(2,1)}, bf16[2,4,18432]{2,1,0:T(4,128)(2,1)}, u32[]{:S(2)}, u32[]{:S(2)}) collective-permute-start(bf16[2,4,18432]{2,1,0:T(4,128)(2,1)} %get-tuple-element.126), channel_id=1, source_target_pairs={{0,1},{1,2},{2,3},{4,5},{5,6},{6,7},{8,9},{9,10},{10,11},{12,13},{... | collective-permute-start | bytes 884744 | tf_op jit(solution)/shard_map/ppermute | solution.py:1144
  6.2 1.3 collective-permute-start.1
  7.7 0.2 slice_reduce_fusion.46
  7.9 0.3 copy.39
  8.2 0.9 dynamic_update_slice.3
  9.1 0.7 reshape.9827.s_ref
  10.0 0.3 slice_reduce_fusion.38
  10.2 0.4 and_or_fusion
  10.6 1.1 fusion
  11.7 0.8 pad_dynamic-slice_fusion.1.k_ref
  12.5 1.2 broadcast_in_dim.476.n_ref
  13.8 49.0 %gather.1 = (bf16[5408,256]{1,0:T(8,128)(2,1)}, bf16[2304,768]{1,0:T(8,128)(2,1)}, f32[8,8,128]{2,1,0:T(8,128)}, bf16[464,256]{1,0:T(8,128)(2,1)}, bf16[336,256]{1,0:T(8,128)(2,1)}) custom-call(bf16[192,256]{1,0:T(8,128)(2,1)} %reshape.9827.s_ref, bf16[288,384]{1,0:T(8,128)(2,1)} %pad_dynamic-slice_fusion.1.k_ref, f32[8,128]{1,0:T(8,128)} %broadcast_in_dim.476.n_ref), custom_call_target="tpu_custom_call" | custom-call | tf_op jit(solution)/shard_map/gather/pallas_call | solution.py:971
  62.7 3.2 %box_in.1.wb_ref = bf16[576,256]{1,0:T(8,128)(2,1)} custom-call(bf16[336,256]{1,0:T(8,128)(2,1)} %get-tuple-element.32.tail_ref), custom_call_target="tpu_custom_call" | custom-call | tf_op jit(solution)/shard_map/box_in/pallas_call | solution.py:651
  65.9 0.7 convert_bitcast_fusion
  66.8 1.8 copy.43
  68.6 0.1 fusion.43
  68.8 0.6 broadcast_compare_fusion.15
  69.5 0.2 slice_reduce_fusion.17
  69.7 7.4 %turn.1.wct_ref = bf16[768,2304]{1,0:T(8,128)(2,1)} custom-call(bf16[2304,768]{1,0:T(8,128)(2,1)} %get-tuple-element.33.k_ref), custom_call_target="tpu_custom_call" | custom-call | tf_op jit(solution)/shard_map/turn/pallas_call | solution.py:1042
  77.1 1.4 slice_reduce_fusion.18
  79.9 0.6 copy.48
  80.5 0.4 slice_reduce_fusion.34
  81.0 0.6 copy.51
  81.8 0.1 copy.41
  81.9 0.6 pad_maximum_fusion.scal_ref
  82.6 0.3 compare_and_fusion.54
  82.9 0.4 compare_and_fusion.55
  83.4 0.6 compare_and_fusion.60
  84.0 0.2 compare_and_fusion.64
  84.2 0.6 compare_and_fusion.62
  84.9 0.3 stack.11
  85.1 1.1 select_convert_fusion.lab_ref
  86.3 3.2 select_select_fusion.btt_ref
  89.4 0.7 pad_convert_fusion.mk_ref
  90.1 2.2 maximum_bitcast_fusion.h_ref
  92.3 13.8 %stem.1 = (f32[1536,512]{1,0:T(8,128)}, bf16[1536,512]{1,0:T(8,128)(2,1)}, bf16[2,3,2304,256]{3,2,1,0:T(8,128)(2,1)}, bf16[256,256]{1,0:T(8,128)(2,1)}) custom-call(bf16[2,16,18432]{2,1,0:T(8,128)(2,1)} %x_ref.3, bf16[16,18432]{1,0:T(8,128)(2,1)} %maximum_bitcast_fusion.h_ref, bf16[464,256]{1,0:T(8,128)(2,1)} %get-tuple-element.29.head_ref), custom_call_target="tpu_custom_call" | custom-call | tf_op jit(solution)/shard_map/stem/pallas_call | solution.py:533
  106.1 128.6 %heads.1 = (f32[768,2304]{1,0:T(8,128)}, f32[512,2304]{1,0:T(8,128)}, f32[576,256]{1,0:T(8,128)}, f32[1,512]{1,0:T(1,128)}, f32[2,2,1536,128]{3,2,1,0:T(8,128)}, /*index=5*/f32[16,256]{1,0:T(8,128)}) custom-call(f32[2]{0:T(128)} %pad_maximum_fusion.scal_ref, bf16[2,3,2304,256]{3,2,1,0:T(8,128)(2,1)} %get-tuple-element.30.f_ref, ...), custom_call_target="tpu_custom_call" | custom-call | tf_op jit(solution)/shard_map/heads/pallas_call | solution.py:675
  234.8 3.0 box_out.1.tail_ref
  237.7 10.2 %turn_back.1 = (bf16[2304,768]{1,0:T(8,128)(2,1)}, bf16[2,2304,256]{2,1,0:T(8,128)(2,1)}) custom-call(f32[768,2304]{1,0:T(8,128)} %get-tuple-element.38.k_ref, f32[512,2304]{1,0:T(8,128)} %get-tuple-element.39.t_ref), custom_call_target="tpu_custom_call" | custom-call | tf_op jit(solution)/shard_map/turn_back/pallas_call | solution.py:1059
  247.9 9.4 %stem_back.1.head_ref = bf16[464,256]{1,0:T(8,128)(2,1)} custom-call(bf16[2,16,18432]{2,1,0:T(8,128)(2,1)} %x_ref.3, f32[2,2,1536,128]{3,2,1,0:T(8,128)} %get-tuple-element.34.fg_ref, bf16[1536,512]{1,0:T(8,128)(2,1)} %get-tuple-element.35.so_ref, f32[1536,512]{1,0:T(8,128)} %get-tuple-element.36.pre_ref, bf16[256,256]{1,0:T(8,128)(2,1)} %get-tuple-element.37.lw_ref), custom_call_target="tpu_custom_call" | custom-call | tf_op jit(solution)/shard_map/stem_back/pallas_call | solution.py:571
  257.3 49.8 %scatter.1 = (f32[192,256]{1,0:T(8,128)}, f32[288,384]{1,0:T(8,128)}, f32[16,256]{1,0:T(8,128)}) custom-call(bf16[464,256]{1,0:T(8,128)(2,1)} %stem_back.1.head_ref, bf16[4608,256]{1,0:T(8,128)(2,1)} %bitcast.21, bf16[336,256]{1,0:T(8,128)(2,1)} %box_out.1.tail_ref, bf16[2304,768]{1,0:T(8,128)(2,1)} %get-tuple-element.43.k_ref, ...), custom_call_target="tpu_custom_call" | custom-call | tf_op jit(solution)/shard_map/scatter/pallas_call | solution.py:1007
  307.1 1.3 multiply_subtract_fusion
  308.5 0.9 copy.44
  309.4 0.9 copy.45
  310.2 0.9 copy.46
  311.2 0.6 slice_reduce_fusion
  313.2 1.0 multiply_subtract_fusion.1
  (49 shorter events, 0.8 us)
Async XLA Ops:
  0.6 7.0 %copy-start.13 = (s32[2,3,4]{2,0,1:T(2,128)S(1)}, s32[2,3,4]{2,0,1:T(2,128)}, u32[]{:S(2)}) copy-start(s32[2,3,4]{2,0,1:T(2,128)} %param.13) | copy-start | bytes 292
  0.6 7.2 %copy-start = (s32[2,9,6144]{2,0,1:T(2,128)S(1)}, s32[2,9,6144]{2,0,1:T(2,128)}, u32[]{:S(2)}) copy-start(s32[2,9,6144]{2,0,1:T(2,128)} %param.14) | copy-start | bytes 1327108
  0.7 7.5 %copy-start.4 = (f32[43072]{0:T(1024)S(1)}, f32[43072]{0:T(1024)}, u32[]{:S(2)}) copy-start(f32[43072]{0:T(1024)} %param.18) | copy-start | bytes 516868
  3.0 6.8 %copy-start.2 = (f32[288,180]{0,1:T(8,128)S(1)}, f32[288,180]{0,1:T(8,128)}, u32[]{:S(2)}) copy-start(f32[288,180]{0,1:T(8,128)} %param.21) | copy-start | bytes 622084
  3.0 87.1 %collective-permute-start = (bf16[2,4,18432]{2,1,0:T(4,128)(2,1)}, bf16[2,4,18432]{2,1,0:T(4,128)(2,1)}, u32[]{:S(2)}, u32[]{:S(2)}) collective-permute-start(bf16[2,4,18432]{2,1,0:T(4,128)(2,1)} %get-tuple-element.126), channel_id=1, source_target_pairs={{0,1},{1,2},{2,3},{4,5},{5,6},{6,7},{8,9},{9,10},{10,11},{12,13},{... | collective-permute-start | bytes 884744 | tf_op jit(solution)/shard_map/ppermute | solution.py:1144
  6.2 83.9 %collective-permute-start.1 = (bf16[2,4,18432]{2,1,0:T(4,128)(2,1)}, bf16[2,4,18432]{2,1,0:T(4,128)(2,1)}, u32[]{:S(2)}, u32[]{:S(2)}) collective-permute-start(bf16[2,4,18432]{2,1,0:T(4,128)(2,1)} %get-tuple-element.127), channel_id=1, source_target_pairs={{1,0},{2,1},{3,2},{5,4},{6,5},{7,6},{9,8},{10,9},{11,10},{13,12},{... | collective-permute-start | bytes 884744 | tf_op jit(solution)/shard_map/ppermute | solution.py:1145
  68.7 0.7 copy-start.3
  69.7 10.8 %copy-start.8 = (s32[2,16]{1,0:T(2,128)S(1)}, s32[2,16]{1,0:T(2,128)}, u32[]{:S(2)}) copy-start(s32[2,16]{1,0:T(2,128)} %param.15) | copy-start | bytes 388
  69.7 12.0 %copy-start.6 = (f32[288,180]{0,1:T(8,128)S(1)}, f32[288,180]{0,1:T(8,128)}, u32[]{:S(2)}) copy-start(f32[288,180]{0,1:T(8,128)} %param.22) | copy-start | bytes 622084
  69.7 12.1 %copy-start.7 = (f32[288,180]{0,1:T(8,128)S(1)}, f32[288,180]{0,1:T(8,128)}, u32[]{:S(2)}) copy-start(f32[288,180]{0,1:T(8,128)} %param.23) | copy-start | bytes 622084
  257.3 49.8 %copy-start.1 = (f32[288,180]{1,0:T(8,128)S(1)}, f32[288,180]{1,0:T(8,128)}, u32[]{:S(2)}) copy-start(f32[288,180]{1,0:T(8,128)} %copy.43) | copy-start | bytes 622084
  308.5 2.6 copy-start.9
  308.5 2.7 copy-start.12
  308.5 4.7 %copy-start.5 = (f32[43072]{0:T(1024)S(1)}, f32[43072]{0:T(1024)}, u32[]{:S(2)}) copy-start(f32[43072]{0:T(1024)} %param.18) | copy-start | bytes 516868
  308.5 4.7 %copy-start.10 = (f32[43072]{0:T(1024)S(1)}, f32[43072]{0:T(1024)}, u32[]{:S(2)}) copy-start(f32[43072]{0:T(1024)} %param.19) | copy-start | bytes 516868
  308.5 4.6 %copy-start.11 = (f32[43072]{0:T(1024)S(1)}, f32[43072]{0:T(1024)}, u32[]{:S(2)}) copy-start(f32[43072]{0:T(1024)} %param.20) | copy-start | bytes 516868

commit v3 on v2

--- a/solution.py
+++ b/solution.py
@@ -176,25 +176,6 @@
         head_ref[...] = h_ref[...].astype(BF)
 
 
-def pipeline(count, build, work, finish, flush, bufs, outs):
-    build(0, bufs[0])
-
-    def step(s, k):
-        finish(s - 1, outs[1 - k])
-        build(jnp.minimum(s + 1, count - 1), bufs[1 - k])
-        work(s, bufs[k], outs[k])
-        flush(jnp.maximum(s - 1, 0))
-
-    def pair(i, carry):
-        step(2 * i, 0)
-        step(2 * i + 1, 1)
-        return carry
-
-    lax.fori_loop(0, count // 2, pair, 0)
-    finish(count - 1, outs[1])
-    flush(count - 1)
-
-
 def aligned(value, multiple):
     return value if isinstance(value, int) else pl.multiple_of(value, multiple)
 
@@ -220,9 +201,9 @@
 
 
 def head_kernel(
-    cols, rows, scal_ref, f_ref, mk_ref, lab_ref, btt_ref, e_ref, full_ref, tb_ref, wct_ref, wb_ref,
-    dwc_ref, dwt_ref, dwb_ref, db_ref, fg_ref, sums_ref,
-    mx_ref, pre_ref, bt_ref, lgt_ref, lgs_ref, g_ref, wt_ref,
+    cols, rows, scal_ref, f_ref, mk_ref, lab_ref, btt_ref, e_ref, full_ref, tb_ref, head_ref, wb_ref,
+    class_ref, tower_ref, dwb_ref, db_ref, fg_ref, sums_ref,
+    mx_ref, pre_ref, bt_ref, lgt_ref, lgs_ref, g_ref, wt_ref, wct_ref, dwc_ref, dwt_ref, copy_sems,
 ):
     own = rows * cols
     edge = HALO * cols
@@ -234,9 +215,25 @@
         dwb_ref[...] = jnp.zeros_like(dwb_ref)
         db_ref[...] = jnp.zeros_like(db_ref)
         sums_ref[...] = jnp.zeros_like(sums_ref)
-        for n in range(2):
-            here = TOWER_ROW + n * 9 * C
-            wt_ref[:, n * C : n * C + C] = full_ref[here : here + 9 * C, :]
+        def fetch(held_ref):
+            copies = [pltpu.make_async_copy(head_ref, held_ref, copy_sems.at[2])]
+            for n in range(2):
+                rows_of = full_ref.at[TOWER_ROW + n * 9 * C : TOWER_ROW + (n + 1) * 9 * C, :]
+                copies.append(pltpu.make_async_copy(rows_of, wt_ref.at[:, n * C : n * C + C], copy_sems.at[n]))
+            for copy in copies:
+                copy.start()
+            copies[0].wait()
+
+            def turn(t, carry):
+                at = pl.multiple_of(t * C, C)
+                wct_ref[:, pl.ds(at, C)] = held_ref[pl.ds(at, C), :].T
+                return carry
+
+            lax.fori_loop(0, 9, turn, 0)
+            for copy in copies[1:]:
+                copy.wait()
+
+        pl.run_scoped(fetch, pltpu.VMEM((9 * C, WIDE), BF))
 
     def spread(i, carry):
         at = pl.multiple_of(i * 384, 128)
@@ -295,7 +292,7 @@
             return carry
 
         lax.fori_loop(0, total // edge, move, 0)
-        def logits(xa_ref, xb_ref, la_ref, lb_ref, st_ref, tt_ref):
+        def logits(xa_ref, la_ref):
             inv_ema = scal_ref[0]
             number = lax.broadcasted_iota(jnp.int32, (GROUP, 256), 0).astype(F32)
             lane = lax.broadcasted_iota(jnp.int32, (8, 256), 1)
@@ -308,9 +305,10 @@
                 l_ref[...] = mm(wct_ref[...], x_ref[...], NT)
 
             def focal(q, l_ref):
-                at = pl.multiple_of(first_logit + jnp.maximum(q, 0) * 256, 128)
+                row = pl.multiple_of(q * 256, 128)
+                at = pl.multiple_of(first_logit + row, 128)
                 spot = lane + at
-                mine = (spot >= edge) & (spot < edge + own) & (lane + q >= 0)
+                mine = (spot >= edge) & (spot < edge + own)
                 lines = [lab_ref[0, a : a + 1, pl.ds(at, 256)] for a in range(ANCH)]
                 rest = [jnp.where(line > -1.5, 1.0 - ALPHA, 0.0) for line in lines]
                 pulls = [line * inv_ema for line in rest]
@@ -349,27 +347,20 @@
                     value = square * cross * jnp.where(hit, ALPHA, other)
                     pull = square * (2.0 * miss * cross + prob) * jnp.where(hit, -ALPHA * inv_ema, pull_other)
                     l_ref[first : first + GROUP, :] = pull
-                    st_ref[first : first + GROUP, :] = pull.astype(BF)
+                    lgt_ref[first : first + GROUP, pl.ds(row, 256)] = pull.astype(BF)
                     total_focal += jnp.sum(value.reshape(GROUP // 8, 8, 256), axis=0)
                 sums_ref[0:8, :] += jnp.where(mine, total_focal, 0.0)
-                tt_ref[...] = l_ref[...].T.astype(BF)
-
-            def flush(q):
-                row = pl.multiple_of(q * 256, 128)
-                lgt_ref[:, pl.ds(row, 256)] = st_ref[...]
-                lgs_ref[pl.ds(row, 256), :] = tt_ref[...]
-
-            pipeline(logit_cells // 256, ready, work, focal, flush, (xa_ref, xb_ref), (la_ref, lb_ref))
-
-        pl.run_scoped(
-            logits,
-            pltpu.VMEM((256, 9 * C), BF),
-            pltpu.VMEM((256, 9 * C), BF),
-            pltpu.VMEM((WIDE, 256), F32),
-            pltpu.VMEM((WIDE, 256), F32),
-            pltpu.VMEM((WIDE, 256), BF),
-            pltpu.VMEM((256, WIDE), BF),
-        )
+                lgs_ref[pl.ds(row, 256), :] = l_ref[...].T.astype(BF)
+
+            def logits_of(q, carry):
+                ready(q, xa_ref)
+                work(q, xa_ref, la_ref)
+                focal(q, la_ref)
+                return carry
+
+            lax.fori_loop(0, logit_cells // 256, logits_of, 0)
+
+        pl.run_scoped(logits, pltpu.VMEM((256, 9 * C), BF), pltpu.VMEM((WIDE, 256), F32))
         weight_sums(pl.program_id(0), cols, edge, own, lambda: lgt_ref[:, 256 : 256 + own], ct_ref, mx_ref, dwc_ref)
 
     pl.run_scoped(heads, pltpu.VMEM((total + 16, C), F32), pltpu.VMEM((3, total, C), BF))
@@ -508,6 +499,28 @@
         pltpu.VMEM((3, own + 32, C), F32),
         pltpu.VMEM((2 * C, own), BF),
     )
+
+    @pl.when(pl.program_id(0) == pl.num_programs(0) - 1)
+    def _():
+        def deliver(class_held, tower_held):
+            def turn(t, carry):
+                at = pl.multiple_of(t * C, C)
+                tower_held[pl.ds(at, C), :] = dwt_ref[0:C, pl.ds(at, C)].astype(BF).T
+                tower_held[pl.ds(pl.multiple_of(9 * C + at, C), C), :] = dwt_ref[C:, pl.ds(at, C)].astype(BF).T
+                class_held[pl.ds(at, C), :] = dwc_ref[:, pl.ds(at, C)].astype(BF).T
+                return carry
+
+            lax.fori_loop(0, 9, turn, 0)
+            copies = [
+                pltpu.make_async_copy(class_held, class_ref, copy_sems.at[0]),
+                pltpu.make_async_copy(tower_held, tower_ref, copy_sems.at[1]),
+            ]
+            for copy in copies:
+                copy.start()
+            for copy in copies:
+                copy.wait()
+
+        pl.run_scoped(deliver, pltpu.VMEM((9 * C, WIDE), BF), pltpu.VMEM((18 * C, C), BF))
 
 
 def whole(shape):
@@ -663,7 +676,7 @@
     )(*args)
 
 
-def heads_call(rows, cols, scal, feats, masks, labels, box_target, full, tb, wct, wb):
+def heads_call(rows, cols, scal, feats, masks, labels, box_target, full, tb, head, wb):
     canvases = feats.shape[0]
     own = rows * cols
     total = own + 2 * HALO * cols
@@ -682,22 +695,22 @@
             per((SLOT, total)),
             per((4, SLOT, total)),
             whole(spread.shape),
-            whole(full.shape),
+            pl.BlockSpec(memory_space=pl.ANY),
             whole(tb.shape),
-            whole(wct.shape),
+            pl.BlockSpec(memory_space=pl.ANY),
             whole(wb.shape),
         ],
         out_specs=[
-            whole((WIDE, 9 * C)),
-            whole((2 * C, 9 * C)),
+            pl.BlockSpec(memory_space=pl.ANY),
+            pl.BlockSpec(memory_space=pl.ANY),
             whole((9 * BOX_ROWS, C)),
             whole((1, 2 * C)),
             per((2, own, LANE)),
             whole((16, 256)),
         ],
         out_shape=[
-            shape_of((WIDE, 9 * C)),
-            shape_of((2 * C, 9 * C)),
+            shape_of((9 * C, WIDE), BF),
+            shape_of((18 * C, C), BF),
             shape_of((9 * BOX_ROWS, C)),
             shape_of((1, 2 * C)),
             shape_of((canvases, 2, own, LANE)),
@@ -711,10 +724,14 @@
             pltpu.VMEM((own + 512, WIDE), BF),
             pltpu.VMEM((own + 256, 2 * C), BF),
             pltpu.VMEM((9 * C, 2 * C), BF),
+            pltpu.VMEM((WIDE, 9 * C), BF),
+            pltpu.VMEM((WIDE, 9 * C), F32),
+            pltpu.VMEM((2 * C, 9 * C), F32),
+            pltpu.SemaphoreType.DMA((3,)),
         ],
         compiler_params=pltpu.CompilerParams(vmem_limit_bytes=VMEM_LIMIT),
         name="heads",
-    )(scal, feats, masks, labels, box_target, spread, full, tb, wct, wb)
+    )(scal, feats, masks, labels, box_target, spread, full, tb, head, wb)
 
 
 def place():
@@ -1034,38 +1051,6 @@
     return flat, grad, sums
 
 
-def turn_kernel(k_ref, o_ref):
-    o_ref[...] = k_ref[...].T
-
-
-def turn(head):
-    return pl.pallas_call(
-        turn_kernel,
-        grid=(9,),
-        in_specs=[pl.BlockSpec((C, 2 * HALF), lambda t: (t, 0))],
-        out_specs=pl.BlockSpec((2 * HALF, C), lambda t: (0, t)),
-        out_shape=shape_of((2 * HALF, 9 * C), BF),
-        name="turn",
-    )(head)
-
-
-def turn_back_kernel(k_ref, t_ref, ko_ref, to_ref):
-    ko_ref[...] = k_ref[...].astype(BF).T
-    for n in range(2):
-        to_ref[n] = t_ref[n * C : n * C + C, :].astype(BF).T
-
-
-def turn_back(class_grad, tower_grad):
-    return pl.pallas_call(
-        turn_back_kernel,
-        grid=(9,),
-        in_specs=[pl.BlockSpec((2 * HALF, C), lambda t: (0, t)), pl.BlockSpec((2 * C, C), lambda t: (0, t))],
-        out_specs=[pl.BlockSpec((C, 2 * HALF), lambda t: (t, 0)), pl.BlockSpec((2, C, C), lambda t: (0, t, 0))],
-        out_shape=[shape_of((9 * C, 2 * HALF), BF), shape_of((2, 9 * C, C), BF)],
-        name="turn_back",
-    )(class_grad, tower_grad)
-
-
 def column_plan():
     plan = []
     for half in range(2):
@@ -1148,14 +1133,13 @@
     wb = box_call(box_in_kernel, (9 * BOX_ROWS, C), BF, "box_in", last)
     stem_pre, stem_out, feats, lat_w = stem_forward(patches, rim, first)
     scal = jnp.stack([1.0 / ema_new, 1.0 / norm])
-    dwc, dwt, dwb, db, feature_grad, sums = heads_call(
-        rows, cols, scal, feats, masks, labels, targets, full, tb, turn(head), wb
+    class_grad, tower_grad, dwb, db, feature_grad, sums = heads_call(
+        rows, cols, scal, feats, masks, labels, targets, full, tb, head, wb
     )
     first_grad = stem_backward(patches, feature_grad, stem_out, stem_pre, lat_w)
-    class_turned, tower_turned = turn_back(dwc, dwt)
     last_grad = box_call(box_out_kernel, last.shape, BF, "box_out", dwb, db)
     shared_grad, class_grad, sums = scatter_all(
-        first_grad, tower_turned.reshape(18 * C, C), last_grad, class_turned, sums, shared_params.shape[0], *class_params.shape
+        first_grad, tower_grad, last_grad, class_grad, sums, shared_params.shape[0], *class_params.shape
     )
     loss = jnp.sum(sums[0:8]) / ema_new + jnp.sum(sums[8:16]) / norm
     return (

time: 318 us -> 302 us (0.950)
  Pallas kernels: 274 us -> 259 us
    pallas_call x2 -> x0, Pallas kernels: 17.6 us -> none  [the longest x1 10.2 us: turn_back(): pl.pallas_call(turn_back_kernel, grid=(9,), in_specs=[pl.BlockSpec((2 * H...]
  transfers between devices with their start and end apart: 2 -> 2, of which waited for: 0 -> 0; matrix products, arithmetic and copies ran while one was open for 7% -> 7% of each run, Pallas kernels for 19% -> 17%
where the time goes in v3:
time: 302 us; the launch traced here: 301 us
  Pallas kernels  259 us (86%)
  other arithmetic  17.4 us (6%)
  local copies, waits for them, and re-layouts  14 us (5%)
  between operations  6.08 us (2%)
  starting transfers between devices  4.47 us (1%)
    pallas_call x1, Pallas kernels, heads_call(): pl.pallas_call(functools.partial(head_kernel, cols, rows), grid=(canvases...  131 us
    pallas_call x1, Pallas kernels, scatter_all(): pl.pallas_call(functools.partial(scatter_kernel, shard), in_specs=[VM] *...  49.8 us
    pallas_call x1, Pallas kernels, gather_all(): pl.pallas_call(functools.partial(gather_kernel, shard), in_specs=[VM, VM,...  49.1 us
    pallas_call x1, Pallas kernels, stem_forward(): pl.pallas_call(functools.partial(stem_kernel, pairs, cols, rows), grid=(s...  13.8 us
    pallas_call x1, Pallas kernels, stem_backward(): pl.pallas_call(functools.partial(stem_back_kernel, pairs, cols, rows), gr...  9.4 us
    unnamed x38, local copies, waits for them, and re-layouts  6.31 us
    pallas_call x2, Pallas kernels, box_call(): pl.pallas_call(kernel, in_specs=[VM] * len(args), out_specs=VM, out_shape...  6.15 us
  transfers between devices with their start and end apart: 2, of which 0 were waited for; matrix products, arithmetic and copies ran while one was open for 7% of the time, Pallas kernels for 17%

profile of v3, /device:TPU:0, one launch (start us, length us, event | category | flops | bytes accessed | tf_op | source)
XLA Modules:
  0.0 301.3 jit_solution(7325588534294350684)
XLA Ops:
  0.7 2.4 fusion.52
  3.0 3.2 %collective-permute-start = (bf16[2,4,18432]{2,1,0:T(4,128)(2,1)}, bf16[2,4,18432]{2,1,0:T(4,128)(2,1)}, u32[]{:S(2)}, u32[]{:S(2)}) collective-permute-start(bf16[2,4,18432]{2,1,0:T(4,128)(2,1)} %get-tuple-element.122), channel_id=1, source_target_pairs={{0,1},{1,2},{2,3},{4,5},{5,6},{6,7},{8,9},{9,10},{10,11},{12,13},{... | collective-permute-start | bytes 884744 | tf_op jit(solution)/shard_map/ppermute | solution.py:1129
  6.2 1.3 collective-permute-start.1
  7.6 0.2 slice_reduce_fusion.46
  7.9 0.3 copy.39
  8.2 0.9 dynamic_update_slice.3
  9.1 0.7 reshape.9824.s_ref
  9.8 0.1 copy.38
  9.9 0.3 slice_reduce_fusion.38
  10.2 0.4 and_or_fusion
  10.6 1.1 fusion
  11.7 0.8 pad_dynamic-slice_fusion.1.k_ref
  12.5 1.2 broadcast_in_dim.476.n_ref
  13.8 49.1 %gather.1 = (bf16[5408,256]{1,0:T(8,128)(2,1)}, bf16[2304,768]{1,0:T(8,128)(2,1)}, f32[8,8,128]{2,1,0:T(8,128)}, bf16[464,256]{1,0:T(8,128)(2,1)}, bf16[336,256]{1,0:T(8,128)(2,1)}) custom-call(bf16[192,256]{1,0:T(8,128)(2,1)} %reshape.9824.s_ref, bf16[288,384]{1,0:T(8,128)(2,1)} %pad_dynamic-slice_fusion.1.k_ref, f32[8,128]{1,0:T(8,128)} %broadcast_in_dim.476.n_ref), custom_call_target="tpu_custom_call" | custom-call | tf_op jit(solution)/shard_map/gather/pallas_call | solution.py:988
  62.8 3.2 %box_in.1.wb_ref = bf16[576,256]{1,0:T(8,128)(2,1)} custom-call(bf16[336,256]{1,0:T(8,128)(2,1)} %get-tuple-element.30.tail_ref), custom_call_target="tpu_custom_call" | custom-call | tf_op jit(solution)/shard_map/box_in/pallas_call | solution.py:664
  66.0 0.7 convert_bitcast_fusion
  66.8 1.8 copy.43
  68.6 0.1 fusion.43
  68.9 0.6 broadcast_compare_fusion.15
  69.5 0.2 slice_reduce_fusion.17
  69.8 1.4 slice_reduce_fusion.18
  72.5 0.6 copy.48
  73.1 0.4 slice_reduce_fusion.34
  73.6 0.6 copy.51
  74.3 0.1 copy.40
  74.4 0.1 copy.41
  74.6 0.6 pad_maximum_fusion.scal_ref
  75.2 0.3 compare_and_fusion.54
  75.5 0.4 compare_and_fusion.55
  76.0 0.6 compare_and_fusion.60
  76.6 0.2 compare_and_fusion.64
  76.8 0.6 compare_and_fusion.62
  77.5 0.3 stack.11
  77.7 1.1 select_convert_fusion.lab_ref
  78.9 3.1 %select_select_fusion.btt_ref = f32[2,4,16,2304]{3,2,1,0:T(8,128)} fusion(f32[2,4]{1,0:T(2,128)S(1)} %get-tuple-element.84, f32[2,4]{1,0:T(2,128)S(1)} %get-tuple-element.85, f32[2,4]{1,0:T(2,128)S(1)} %get-tuple-element.71, f32[2,4]{1,0:T(2,128)S(1)} %get-tuple-element.72, f32[2,4]{1,0:T(2,128)S(1)} %get-tuple-element.73, f32[2,4]{1,0:T(2,128)S(1)} %get-tuple-element.74, ...), kind=kLoop, calls=%fused_computation | loop fusion | flops 4718592 | bytes 2359808 | tf_op jit(solution)/shard_map/jit(_where)/select_n | solution.py:1114
  82.0 0.7 pad_convert_fusion.mk_ref
  82.7 2.2 maximum_bitcast_fusion.h_ref
  84.8 13.8 %stem.1 = (f32[1536,512]{1,0:T(8,128)}, bf16[1536,512]{1,0:T(8,128)(2,1)}, bf16[2,3,2304,256]{3,2,1,0:T(8,128)(2,1)}, bf16[256,256]{1,0:T(8,128)(2,1)}) custom-call(bf16[2,16,18432]{2,1,0:T(8,128)(2,1)} %x_ref.3, bf16[16,18432]{1,0:T(8,128)(2,1)} %maximum_bitcast_fusion.h_ref, bf16[464,256]{1,0:T(8,128)(2,1)} %get-tuple-element.27.head_ref), custom_call_target="tpu_custom_call" | custom-call | tf_op jit(solution)/shard_map/stem/pallas_call | solution.py:546
  98.6 131.2 %heads.1 = (bf16[2304,768]{1,0:T(8,128)(2,1)}, bf16[4608,256]{1,0:T(8,128)(2,1)}, f32[576,256]{1,0:T(8,128)}, f32[1,512]{1,0:T(1,128)}, f32[2,2,1536,128]{3,2,1,0:T(8,128)}, /*index=5*/f32[16,256]{1,0:T(8,128)}) custom-call(f32[2]{0:T(128)} %pad_maximum_fusion.scal_ref, bf16[2,3,2304,256]{3,2,1,0:T(8,128)(2,1)} %get-tuple-element.28.f_ref, ...), custom_call_target="tpu_custom_call" | custom-call | tf_op jit(solution)/shard_map/heads/pallas_call | solution.py:688
  229.9 3.0 box_out.1.tail_ref
  232.8 9.4 %stem_back.1.head_ref = bf16[464,256]{1,0:T(8,128)(2,1)} custom-call(bf16[2,16,18432]{2,1,0:T(8,128)(2,1)} %x_ref.3, f32[2,2,1536,128]{3,2,1,0:T(8,128)} %get-tuple-element.32.fg_ref, bf16[1536,512]{1,0:T(8,128)(2,1)} %get-tuple-element.33.so_ref, f32[1536,512]{1,0:T(8,128)} %get-tuple-element.34.pre_ref, bf16[256,256]{1,0:T(8,128)(2,1)} %get-tuple-element.35.lw_ref), custom_call_target="tpu_custom_call" | custom-call | tf_op jit(solution)/shard_map/stem_back/pallas_call | solution.py:584
  242.2 49.8 %scatter.1 = (f32[192,256]{1,0:T(8,128)}, f32[288,384]{1,0:T(8,128)}, f32[16,256]{1,0:T(8,128)}) custom-call(bf16[464,256]{1,0:T(8,128)(2,1)} %stem_back.1.head_ref, bf16[4608,256]{1,0:T(8,128)(2,1)} %get-tuple-element.36.tower_ref, bf16[336,256]{1,0:T(8,128)(2,1)} %box_out.1.tail_ref, bf16[2304,768]{1,0:T(8,128)(2,1)} %get-tuple-element.39.k_ref, ...), custom_call_target="tpu_custom_call" | custom-call | tf_op jit(solution)/shard_map/scatter/pallas_call | solution.py:1024
  292.0 1.3 multiply_subtract_fusion
  293.4 0.9 copy.44
  294.2 0.9 copy.45
  295.1 0.9 copy.46
  296.1 0.6 slice_reduce_fusion
  298.0 1.0 multiply_subtract_fusion.1
  (47 shorter events, 0.5 us)
Async XLA Ops:
  0.6 7.0 %copy-start.13 = (s32[2,3,4]{2,0,1:T(2,128)S(1)}, s32[2,3,4]{2,0,1:T(2,128)}, u32[]{:S(2)}) copy-start(s32[2,3,4]{2,0,1:T(2,128)} %param.13) | copy-start | bytes 292
  0.6 7.2 %copy-start = (s32[2,9,6144]{2,0,1:T(2,128)S(1)}, s32[2,9,6144]{2,0,1:T(2,128)}, u32[]{:S(2)}) copy-start(s32[2,9,6144]{2,0,1:T(2,128)} %param.14) | copy-start | bytes 1327108
  0.7 7.5 %copy-start.4 = (f32[43072]{0:T(1024)S(1)}, f32[43072]{0:T(1024)}, u32[]{:S(2)}) copy-start(f32[43072]{0:T(1024)} %param.18) | copy-start | bytes 516868
  3.0 6.8 %copy-start.2 = (f32[288,180]{0,1:T(8,128)S(1)}, f32[288,180]{0,1:T(8,128)}, u32[]{:S(2)}) copy-start(f32[288,180]{0,1:T(8,128)} %param.21) | copy-start | bytes 622084
  3.0 79.6 %collective-permute-start = (bf16[2,4,18432]{2,1,0:T(4,128)(2,1)}, bf16[2,4,18432]{2,1,0:T(4,128)(2,1)}, u32[]{:S(2)}, u32[]{:S(2)}) collective-permute-start(bf16[2,4,18432]{2,1,0:T(4,128)(2,1)} %get-tuple-element.122), channel_id=1, source_target_pairs={{0,1},{1,2},{2,3},{4,5},{5,6},{6,7},{8,9},{9,10},{10,11},{12,13},{... | collective-permute-start | bytes 884744 | tf_op jit(solution)/shard_map/ppermute | solution.py:1129
  6.2 76.5 %collective-permute-start.1 = (bf16[2,4,18432]{2,1,0:T(4,128)(2,1)}, bf16[2,4,18432]{2,1,0:T(4,128)(2,1)}, u32[]{:S(2)}, u32[]{:S(2)}) collective-permute-start(bf16[2,4,18432]{2,1,0:T(4,128)(2,1)} %get-tuple-element.123), channel_id=1, source_target_pairs={{1,0},{2,1},{3,2},{5,4},{6,5},{7,6},{9,8},{10,9},{11,10},{13,12},{... | collective-permute-start | bytes 884744 | tf_op jit(solution)/shard_map/ppermute | solution.py:1130
  68.8 0.8 copy-start.3
  68.8 4.3 %copy-start.8 = (s32[2,16]{1,0:T(2,128)S(1)}, s32[2,16]{1,0:T(2,128)}, u32[]{:S(2)}) copy-start(s32[2,16]{1,0:T(2,128)} %param.15) | copy-start | bytes 388
  68.8 5.5 %copy-start.6 = (f32[288,180]{0,1:T(8,128)S(1)}, f32[288,180]{0,1:T(8,128)}, u32[]{:S(2)}) copy-start(f32[288,180]{0,1:T(8,128)} %param.22) | copy-start | bytes 622084
  68.9 5.5 %copy-start.7 = (f32[288,180]{0,1:T(8,128)S(1)}, f32[288,180]{0,1:T(8,128)}, u32[]{:S(2)}) copy-start(f32[288,180]{0,1:T(8,128)} %param.23) | copy-start | bytes 622084
  242.2 49.8 %copy-start.1 = (f32[288,180]{1,0:T(8,128)S(1)}, f32[288,180]{1,0:T(8,128)}, u32[]{:S(2)}) copy-start(f32[288,180]{1,0:T(8,128)} %copy.43) | copy-start | bytes 622084
  293.3 2.6 copy-start.9
  293.3 2.7 copy-start.12
  293.4 4.7 %copy-start.5 = (f32[43072]{0:T(1024)S(1)}, f32[43072]{0:T(1024)}, u32[]{:S(2)}) copy-start(f32[43072]{0:T(1024)} %param.18) | copy-start | bytes 516868
  293.4 4.7 %copy-start.10 = (f32[43072]{0:T(1024)S(1)}, f32[43072]{0:T(1024)}, u32[]{:S(2)}) copy-start(f32[43072]{0:T(1024)} %param.19) | copy-start | bytes 516868
  293.4 4.6 %copy-start.11 = (f32[43072]{0:T(1024)S(1)}, f32[43072]{0:T(1024)}, u32[]{:S(2)}) copy-start(f32[43072]{0:T(1024)} %param.20) | copy-start | bytes 516868

commit v4 on v3

--- a/solution.py
+++ b/solution.py
@@ -93,7 +93,12 @@
 
     x = x_ref[...].reshape(own_rows, x_ref.shape[2])
     own = columns_of(x, pairs, 2 * PATCH)
-    rim = columns_of(h_ref[...], pairs, 2 * PATCH)
+    half = pl.num_programs(0) // 2
+    lanes = pl.ds(pl.multiple_of(step % half * x.shape[1], LANE), x.shape[1])
+    many_rows = h_ref.shape[1] // 2
+    near = [h_ref[n, :, lanes].astype(F32) for n in range(2)]
+    near = [jnp.where(step < half, one[:many_rows], one[many_rows:]) for one in near]
+    rim = columns_of(jnp.concatenate(near, axis=0).astype(BF), pairs, 2 * PATCH)
     pre = mm(jnp.concatenate(own + rim, axis=0), w_ref[...]) + b_ref[...]
     count = pairs * own_rows
     pre_ref[...] = pre[:count]
@@ -105,15 +110,16 @@
             j = step * 2 * pairs + 2 * k + half
             for c in range(canvases):
                 at = k * own_rows + c * rows
-                rim_at = count + k * 2 * HALO * canvases + c * 2 * HALO
+                up_at = count + k * 2 * HALO * canvases + c * HALO
+                down_at = up_at + HALO * canvases
                 for n in range(2):
                     side = slice(n * LANE, n * LANE + LANE)
                     place = pl.ds(8 + HALO * cols + j, rows, stride=cols)
                     t_ref[c, n, place, :] = feat[at : at + rows, side]
                     place = pl.ds(8 + j, HALO, stride=cols)
-                    t_ref[c, n, place, :] = feat[rim_at : rim_at + HALO, side]
+                    t_ref[c, n, place, :] = feat[up_at : up_at + HALO, side]
                     place = pl.ds(8 + (HALO + rows) * cols + j, HALO, stride=cols)
-                    t_ref[c, n, place, :] = feat[rim_at + HALO : rim_at + 2 * HALO, side]
+                    t_ref[c, n, place, :] = feat[down_at : down_at + HALO, side]
 
     @pl.when(step == pl.num_programs(0) - 1)
     def _():
@@ -548,7 +554,7 @@
         grid=(steps,),
         in_specs=[
             pl.BlockSpec((canvases, rows, chunk), lambda s: (0, 0, s)),
-            pl.BlockSpec((2 * HALO * canvases, chunk), lambda s: (0, s)),
+            whole(rim.shape),
             whole(head.shape),
         ],
         out_specs=[
@@ -782,13 +788,14 @@
     return pl.multiple_of((index * shard + LEAD * C) // (16 * C) * 16, 16)
 
 
-def gather_kernel(shard, s_ref, k_ref, n_ref, full_ref, head_ref, count_ref, first_ref, last_ref, sh_ref, kx_ref, send_sems, recv_sems):
+def gather_kernel(shard, s_ref, k_ref, n_ref, r_ref, full_ref, head_ref, count_ref, first_ref, last_ref, rim_ref, sh_ref, kx_ref, send_sems, recv_sems):
     z, y, x, c = place()
     block = k_ref.shape[0]
     win = s_ref.shape[0]
     others = [(k, j) for k in range(4) for j in range(2) if k or j]
     ring = [((z + k) % 4, (y + j) % 2) for k, j in others]
-    enter([target(zz, yy, x, c) for zz, yy in ring] + [target(z, y, 1 - x, c), target(z, y, x, 1 - c)])
+    line = [(z * 2 + y, (x * 2 + c + step) % 4) for step in (1, 3)]
+    enter([target(zz, yy, x, c) for zz, yy in ring] + [target(z, y, 1 - x, c), target(z, y, x, 1 - c)] + line)
     mail = Mail(send_sems, recv_sems)
     me = owner(z, y, x, c)
 
@@ -805,6 +812,7 @@
     got_y = [mail.push(s_ref, slot, target(z, 1 - y, x, c))]
     got_x = [mail.push(s_ref, slot, target(z, y, 1 - x, c))]
     got_c = [mail.push(s_ref, slot, target(z, y, x, 1 - c))]
+    rims = [mail.push(r_ref.at[n], rim_ref.at[n], line[n]) for n in range(2)]
     count_ref[z * 2 + y] = n_ref[...]
     sh_ref[me] = s_ref[...]
 
@@ -839,7 +847,7 @@
         got_x[k].wait_recv()
         slot = sh_ref.at[owner((z + 4 - k % 4) % 4, (y + k // 4) % 2, 1 - x, c)]
         got_c.append(mail.push(slot, slot, target(z, y, x, 1 - c)))
-    for copy in got_c + got_kc + counts:
+    for copy in got_c + got_kc + counts + rims:
         copy.wait_recv()
     full_ref[...] = jnp.zeros_like(full_ref)
 
@@ -961,7 +969,7 @@
     return (index * shard + LEAD * C) % (16 * C)
 
 
-def gather_all(shared_params, class_params, count):
+def gather_all(shared_params, class_params, count, edges):
     img, cls = lax.axis_index("img"), lax.axis_index("cls")
     img_parts, cls_parts = lax.axis_size("img"), lax.axis_size("cls")
     shard = shared_params.shape[0]
@@ -975,7 +983,9 @@
         for half in range(2):
             pieces += [head[:, 180 * half : 180 * half + 180], head[:, 360 + 180 * half : 540 + 180 * half]]
             pieces.append(jnp.zeros((head.shape[0], HALF - 360), BF))
-        return full, full[:TOWER_ROW], full[TAIL_ROW:], jnp.concatenate(pieces, axis=1), lax.psum(count, "img")
+        ways = [[(i, (i + step) % cls_parts) for i in range(cls_parts)] for step in (1, cls_parts - 1)]
+        rim = jnp.stack([lax.ppermute(edges[n], "cls", ways[n]) for n in range(2)])
+        return full, full[:TOWER_ROW], full[TAIL_ROW:], jnp.concatenate(pieces, axis=1), lax.psum(count, "img"), rim
     rows = -(-(shard + 16 * C) // (16 * C)) * 16
     window = lax.dynamic_update_slice(
         jnp.zeros((rows * C,), BF), shared_params.astype(BF), (flat_place(img * cls_parts + cls, shard),)
@@ -985,27 +995,28 @@
         jnp.pad(wide, ((0, 0), (0, part))), jnp.where(cls // 2 == 0, part, 0), HALF, 1
     )
     number = jnp.broadcast_to(count, (8, LANE))
-    full, head, counts, first, last = pl.pallas_call(
+    full, head, counts, first, last, rim = pl.pallas_call(
         functools.partial(gather_kernel, shard),
-        in_specs=[VM, VM, VM],
-        out_specs=[VM] * 5,
+        in_specs=[VM] * 4,
+        out_specs=[VM] * 6,
         out_shape=[
             shape_of((FULL_ROWS, C), BF),
             shape_of((img_parts * block, 2 * HALF), BF),
             shape_of((img_parts, 8, LANE)),
             shape_of((TOWER_ROW, C), BF),
             shape_of((FULL_ROWS - TAIL_ROW, C), BF),
+            shape_of(edges.shape, BF),
         ],
         scratch_shapes=[
             pltpu.VMEM((img_parts * cls_parts, rows, C), BF),
             pltpu.VMEM((block, HALF), BF),
-            pltpu.SemaphoreType.DMA((54,)),
-            pltpu.SemaphoreType.DMA((54,)),
+            pltpu.SemaphoreType.DMA((56,)),
+            pltpu.SemaphoreType.DMA((56,)),
         ],
         compiler_params=pltpu.CompilerParams(collective_id=0, has_side_effects=True, vmem_limit_bytes=VMEM_LIMIT),
         name="gather",
-    )(window, wide, number)
-    return full, first, last, head, jnp.sum(counts[:, 0, 0])
+    )(window, wide, number, edges)
+    return full, first, last, head, jnp.sum(counts[:, 0, 0]), rim
 
 
 def scatter_all(head, tower, tail, class_grad, sums, shard, block, part):
@@ -1117,18 +1128,16 @@
 
 def local(patches, boxes, match, gt_labels, gt_deltas, ema_old, shared_params, shared_m, shared_v, class_params, class_m, class_v):
     cls_rank = lax.axis_index("cls")
-    cls_parts = lax.axis_size("cls")
     canvases, rows, width = patches.shape
     cols = width // PATCH
     masks, labels, targets = cell_data(boxes, match, gt_labels, gt_deltas, cls_rank * rows, rows, cols)
     full_rows = match.shape[2] // cols
     count = jnp.sum(valid_positives(boxes, match, full_rows, cols))
-    full, first, last, head, positives = gather_all(shared_params, class_params, count)
+    edges = jnp.stack([patches[:, rows - HALO :], patches[:, :HALO]]).reshape(2, canvases * HALO, width)
+    edges = jnp.concatenate([edges[..., : width // 2], edges[..., width // 2 :]], axis=1)
+    full, first, last, head, positives, rim = gather_all(shared_params, class_params, count, edges)
     norm = jnp.maximum(positives, 1.0)
     ema_new = EMA_KEEP * ema_old + (1.0 - EMA_KEEP) * norm
-    down = lax.ppermute(patches[:, rows - HALO :], "cls", [(i, i + 1) for i in range(cls_parts - 1)])
-    up = lax.ppermute(patches[:, :HALO], "cls", [(i + 1, i) for i in range(cls_parts - 1)])
-    rim = jnp.concatenate([down, up], axis=1).reshape(canvases * 2 * HALO, width)
     tb = last[0:2].reshape(1, 2 * C).astype(F32)
     wb = box_call(box_in_kernel, (9 * BOX_ROWS, C), BF, "box_in", last)
     stem_pre, stem_out, feats, lat_w = stem_forward(patches, rim, first)

time: 302 us -> 294 us (0.974)
  starting transfers between devices: 4.47 us -> 0 us
    ppermute x2 -> x0, starting transfers between devices: 4.47 us -> none  [the longest x1 3.19 us: local(): lax.ppermute(patches[:, rows - HALO:], 'cls', [(i, i + 1) for i in range(...]
    unnamed x38 -> x35, local copies, waits for them, and re-layouts: 6.31 us -> 6.62 us
  transfers between devices with their start and end apart: 2 -> 0, of which waited for: 0 -> 0; matrix products, arithmetic and copies ran while one was open for 7% -> 0% of each run, Pallas kernels for 17% -> 0%
where the time goes in v4:
time: 294 us; the launch traced here: 293 us
  Pallas kernels  258 us (88%)
  other arithmetic  15.2 us (5%)
  local copies, waits for them, and re-layouts  13.3 us (5%)
  between operations  6.03 us (2%)
    pallas_call x1, Pallas kernels, heads_call(): pl.pallas_call(functools.partial(head_kernel, cols, rows), grid=(canvases...  132 us
    pallas_call x1, Pallas kernels, gather_all(): pl.pallas_call(functools.partial(gather_kernel, shard), in_specs=[VM] * 4...  48.8 us
    pallas_call x1, Pallas kernels, scatter_all(): pl.pallas_call(functools.partial(scatter_kernel, shard), in_specs=[VM] *...  48.8 us
    pallas_call x1, Pallas kernels, stem_forward(): pl.pallas_call(functools.partial(stem_kernel, pairs, cols, rows), grid=(s...  13.8 us
    pallas_call x1, Pallas kernels, stem_backward(): pl.pallas_call(functools.partial(stem_back_kernel, pairs, cols, rows), gr...  9.41 us
    unnamed x35, local copies, waits for them, and re-layouts  6.62 us
    pallas_call x2, Pallas kernels, box_call(): pl.pallas_call(kernel, in_specs=[VM] * len(args), out_specs=VM, out_shape...  6.15 us

profile of v4, /device:TPU:0, one launch (start us, length us, event | category | flops | bytes accessed | tf_op | source)
XLA Modules:
  0.0 293.0 jit_solution(18117549559456866805)
XLA Ops:
  0.6 0.7 slice_bitcast_fusion.2
  1.3 0.3 slice_reduce_fusion.38
  1.7 0.2 slice_reduce_fusion.46
  1.9 0.1 fusion.43
  2.1 1.3 copy.39
  3.4 0.6 broadcast_compare_fusion.15
  4.1 0.2 slice_reduce_fusion.17
  4.3 3.2 %select_select_fusion.btt_ref = f32[2,4,16,2304]{3,2,1,0:T(8,128)} fusion(f32[2,4]{1,0:T(2,128)S(1)} %get-tuple-element.86, f32[2,4]{1,0:T(2,128)S(1)} %get-tuple-element.87, f32[2,4]{1,0:T(2,128)S(1)} %get-tuple-element.73, f32[2,4]{1,0:T(2,128)S(1)} %get-tuple-element.74, f32[2,4]{1,0:T(2,128)S(1)} %get-tuple-element.75, f32[2,4]{1,0:T(2,128)S(1)} %get-tuple-element.76, ...), kind=kLoop, calls=%fused_computation | loop fusion | flops 4718592 | bytes 2359808 | tf_op jit(solution)/shard_map/jit(_where)/select_n | solution.py:1125
  7.6 1.1 dynamic_update_slice.3
  8.7 0.7 reshape.9826.s_ref
  9.4 0.1 copy.38
  9.5 0.9 pad_dynamic-slice_fusion.1.k_ref
  10.4 0.4 and_or_fusion
  10.8 1.1 fusion
  11.8 1.2 broadcast_in_dim.476.n_ref
  13.1 0.2 fusion.52
  13.6 0.9 pad_maximum_fusion.r_ref
  14.4 48.8 %gather.1 = (bf16[5408,256]{1,0:T(8,128)(2,1)}, bf16[2304,768]{1,0:T(8,128)(2,1)}, f32[8,8,128]{2,1,0:T(8,128)}, bf16[464,256]{1,0:T(8,128)(2,1)}, bf16[336,256]...) custom-call(bf16[192,256]{1,0:T(8,128)(2,1)} %reshape.9826.s_ref, bf16[288,384]{1,0:T(8,128)(2,1)} %pad_dynamic-slice_fusion.1.k_ref, ...), custom_call_target="tpu_custom_call" | custom-call | tf_op jit(solution)/shard_map/gather/pallas_call | solution.py:998
  63.3 13.8 %stem.1 = (f32[1536,512]{1,0:T(8,128)}, bf16[1536,512]{1,0:T(8,128)(2,1)}, bf16[2,3,2304,256]{3,2,1,0:T(8,128)(2,1)}, bf16[256,256]{1,0:T(8,128)(2,1)}) custom-call(bf16[2,16,18432]{2,1,0:T(8,128)(2,1)} %x_ref.3, bf16[2,16,9216]{2,1,0:T(8,128)(2,1)} %get-tuple-element.28.h_ref, bf16[464,256]{1,0:T(8,128)(2,1)} %get-tuple-element.29.head_ref), custom_call_target="tpu_custom_call" | custom-call | tf_op jit(solution)/shard_map/stem/pallas_call | solution.py:552
  77.0 3.2 %box_in.1.wb_ref = bf16[576,256]{1,0:T(8,128)(2,1)} custom-call(bf16[336,256]{1,0:T(8,128)(2,1)} %get-tuple-element.32.tail_ref), custom_call_target="tpu_custom_call" | custom-call | tf_op jit(solution)/shard_map/box_in/pallas_call | solution.py:670
  80.2 1.4 slice_reduce_fusion.18
  83.0 0.6 pad_maximum_fusion.1.scal_ref
  83.6 0.7 convert_bitcast_fusion
  84.2 0.6 copy.48
  84.9 0.4 compare_and_fusion.54
  85.2 0.4 compare_and_fusion.55
  85.7 0.6 compare_and_fusion.60
  86.4 0.6 compare_and_fusion.62
  87.0 0.2 compare_and_fusion.64
  87.3 0.3 stack.36
  87.5 0.7 pad_convert_fusion.mk_ref
  88.2 0.4 slice_reduce_fusion.34
  88.6 1.1 select_convert_fusion.lab_ref
  89.9 0.6 copy.51
  90.5 131.5 %heads.1 = (bf16[2304,768]{1,0:T(8,128)(2,1)}, bf16[4608,256]{1,0:T(8,128)(2,1)}, f32[576,256]{1,0:T(8,128)}, f32[1,512]{1,0:T(1,128)}, f32[2,2,1536,128]{3,2,1,0:T(8,128)}, /*index=5*/f32[16,256]{1,0:T(8,128)}) custom-call(f32[2]{0:T(128)} %pad_maximum_fusion.1.scal_ref, bf16[2,3,2304,256]{3,2,1,0:T(8,128)(2,1)} %get-tuple-element.30.f_ref, ...), custom_call_target="tpu_custom_call" | custom-call | tf_op jit(solution)/shard_map/heads/pallas_call | solution.py:694
  222.1 3.0 %box_out.1.tail_ref = bf16[336,256]{1,0:T(8,128)(2,1)} custom-call(f32[576,256]{1,0:T(8,128)} %get-tuple-element.39.w_ref, f32[1,512]{1,0:T(1,128)} %get-tuple-element.40.b_ref), custom_call_target="tpu_custom_call" | custom-call | tf_op jit(solution)/shard_map/box_out/pallas_call | solution.py:670
  225.1 9.4 %stem_back.1.head_ref = bf16[464,256]{1,0:T(8,128)(2,1)} custom-call(bf16[2,16,18432]{2,1,0:T(8,128)(2,1)} %x_ref.3, f32[2,2,1536,128]{3,2,1,0:T(8,128)} %get-tuple-element.34.fg_ref, bf16[1536,512]{1,0:T(8,128)(2,1)} %get-tuple-element.35.so_ref, f32[1536,512]{1,0:T(8,128)} %get-tuple-element.36.pre_ref, bf16[256,256]{1,0:T(8,128)(2,1)} %get-tuple-element.37.lw_ref), custom_call_target="tpu_custom_call" | custom-call | tf_op jit(solution)/shard_map/stem_back/pallas_call | solution.py:590
  234.5 48.8 %scatter.1 = (f32[192,256]{1,0:T(8,128)}, f32[288,384]{1,0:T(8,128)}, f32[16,256]{1,0:T(8,128)}) custom-call(bf16[464,256]{1,0:T(8,128)(2,1)} %stem_back.1.head_ref, bf16[4608,256]{1,0:T(8,128)(2,1)} %get-tuple-element.38.tower_ref, bf16[336,256]{1,0:T(8,128)(2,1)} %box_out.1.tail_ref, bf16[2304,768]{1,0:T(8,128)(2,1)} %get-tuple-element.41.k_ref, ...), custom_call_target="tpu_custom_call" | custom-call | tf_op jit(solution)/shard_map/scatter/pallas_call | solution.py:1035
  283.3 0.1 copy.40
  283.4 1.1 copy.41
  284.5 0.1 copy.43
  284.7 0.3 multiply_subtract_fusion
  285.0 0.9 copy.44
  285.9 0.9 copy.45
  286.7 0.9 copy.46
  287.6 0.1 copy.49
  287.7 1.0 multiply_subtract_fusion.1
  288.7 0.7 slice_reduce_fusion
  (44 shorter events, 0.6 us)
Async XLA Ops:
  3.4 0.7 copy-start.3
  4.3 3.3 %copy-start.4 = (f32[43072]{0:T(1024)S(1)}, f32[43072]{0:T(1024)}, u32[]{:S(2)}) copy-start(f32[43072]{0:T(1024)} %param.18) | copy-start | bytes 516868
  4.3 5.0 %copy-start.2 = (f32[288,180]{0,1:T(8,128)S(1)}, f32[288,180]{0,1:T(8,128)}, u32[]{:S(2)}) copy-start(f32[288,180]{0,1:T(8,128)} %param.21) | copy-start | bytes 622084
  7.6 3.2 %copy-start.1 = (s32[2,9,6144]{2,0,1:T(2,128)S(1)}, s32[2,9,6144]{2,0,1:T(2,128)}, u32[]{:S(2)}) copy-start(s32[2,9,6144]{2,0,1:T(2,128)} %param.14) | copy-start | bytes 1327108
  7.6 5.5 %copy-start = (bf16[2,16,18432]{2,1,0:T(8,128)(2,1)S(1)}, bf16[2,16,18432]{2,1,0:T(8,128)(2,1)}, u32[]{:S(2)}) copy-start(bf16[2,16,18432]{2,1,0:T(8,128)(2,1)} %x_ref.3) | copy-start | bytes 3538948
  77.0 11.2 %copy-start.6 = (s32[2,16]{1,0:T(2,128)S(1)}, s32[2,16]{1,0:T(2,128)}, u32[]{:S(2)}) copy-start(s32[2,16]{1,0:T(2,128)} %param.15) | copy-start | bytes 388
  234.5 48.8 %copy-start.5 = (f32[288,180]{0,1:T(8,128)S(1)}, f32[288,180]{0,1:T(8,128)}, u32[]{:S(2)}) copy-start(f32[288,180]{0,1:T(8,128)} %param.22) | copy-start | bytes 622084
  283.2 1.4 copy-start.7
  285.0 2.6 copy-start.8
  285.0 2.7 copy-start.9
  285.0 2.7 copy-start.10
  286.7 2.0 copy-start.11

commit v5 on v4

--- a/solution.py
+++ b/solution.py
@@ -696,7 +696,7 @@
         grid=(canvases,),
         in_specs=[
             pl.BlockSpec(memory_space=pltpu.SMEM),
-            pl.BlockSpec((1, 3, total, C), lambda c: (c, 0, 0, 0), pipeline_mode=pl.Buffered(1)),
+            per((3, total, C)),
             per((SLOT, total)),
             per((SLOT, total)),
             per((4, SLOT, total)),
@@ -788,7 +788,7 @@
     return pl.multiple_of((index * shard + LEAD * C) // (16 * C) * 16, 16)
 
 
-def gather_kernel(shard, s_ref, k_ref, n_ref, r_ref, full_ref, head_ref, count_ref, first_ref, last_ref, rim_ref, sh_ref, kx_ref, send_sems, recv_sems):
+def gather_kernel(shard, s_ref, k_ref, n_ref, r_ref, full_ref, head_ref, all_ref, first_ref, last_ref, rim_ref, count_ref, sh_ref, kx_ref, send_sems, recv_sems):
     z, y, x, c = place()
     block = k_ref.shape[0]
     win = s_ref.shape[0]
@@ -849,6 +849,7 @@
         got_c.append(mail.push(slot, slot, target(z, y, x, 1 - c)))
     for copy in got_c + got_kc + counts + rims:
         copy.wait_recv()
+    all_ref[...] = jnp.sum(count_ref[...], axis=0)
     full_ref[...] = jnp.zeros_like(full_ref)
 
     def merge(d, carry):
@@ -1002,12 +1003,13 @@
         out_shape=[
             shape_of((FULL_ROWS, C), BF),
             shape_of((img_parts * block, 2 * HALF), BF),
-            shape_of((img_parts, 8, LANE)),
+            shape_of((8, LANE)),
             shape_of((TOWER_ROW, C), BF),
             shape_of((FULL_ROWS - TAIL_ROW, C), BF),
             shape_of(edges.shape, BF),
         ],
         scratch_shapes=[
+            pltpu.VMEM((img_parts, 8, LANE), F32),
             pltpu.VMEM((img_parts * cls_parts, rows, C), BF),
             pltpu.VMEM((block, HALF), BF),
             pltpu.SemaphoreType.DMA((56,)),
@@ -1016,7 +1018,7 @@
         compiler_params=pltpu.CompilerParams(collective_id=0, has_side_effects=True, vmem_limit_bytes=VMEM_LIMIT),
         name="gather",
     )(window, wide, number, edges)
-    return full, first, last, head, jnp.sum(counts[:, 0, 0]), rim
+    return full, first, last, head, counts[0, 0], rim
 
 
 def scatter_all(head, tower, tail, class_grad, sums, shard, block, part):
@@ -1059,6 +1061,7 @@
     )(head, tower, tail, class_grad, sums)
     flat = lax.dynamic_slice_in_dim(window.reshape(-1), flat_place(img * cls_parts + cls, shard), shard)
     grad = lax.dynamic_slice_in_dim(wide, jnp.where(cls // 2 == 0, 0, part), part, 1)
+    grad = lax.optimization_barrier(grad.T).T
     return flat, grad, sums
 
 

time: 294 us -> 291 us (0.990)
  no operation moved by 1% of the time
where the time goes in v5:
time: 291 us
  Pallas kernels  256 us (88%)
  local copies, waits for them, and re-layouts  14.7 us (5%)
  other arithmetic  13.8 us (5%)
  between operations  5.95 us (2%)
    pallas_call x1, Pallas kernels, heads_call(): pl.pallas_call(functools.partial(head_kernel, cols, rows), grid=(canvases...  129 us
    pallas_call x1, Pallas kernels, gather_all(): pl.pallas_call(functools.partial(gather_kernel, shard), in_specs=[VM] * 4...  48.8 us
    pallas_call x1, Pallas kernels, scatter_all(): pl.pallas_call(functools.partial(scatter_kernel, shard), in_specs=[VM] *...  48.8 us
    pallas_call x1, Pallas kernels, stem_forward(): pl.pallas_call(functools.partial(stem_kernel, pairs, cols, rows), grid=(s...  13.8 us
    pallas_call x1, Pallas kernels, stem_backward(): pl.pallas_call(functools.partial(stem_back_kernel, pairs, cols, rows), gr...  9.42 us
    pallas_call x2, Pallas kernels, box_call(): pl.pallas_call(kernel, in_specs=[VM] * len(args), out_specs=VM, out_shape...  6.15 us

profile of v5, /device:TPU:0, one launch (start us, length us, event | category | flops | bytes accessed | tf_op | source)
XLA Modules:
  0.0 290.5 jit_solution(13731388013855288356)
XLA Ops:
  0.6 0.7 slice_bitcast_fusion.2
  1.3 0.3 slice_reduce_fusion.37
  1.7 0.2 slice_reduce_fusion.45
  1.9 0.1 fusion.43
  2.1 1.3 copy.39
  3.4 0.6 broadcast_compare_fusion.15
  4.1 0.2 slice_reduce_fusion.17
  4.3 3.2 %select_select_fusion.btt_ref = f32[2,4,16,2304]{3,2,1,0:T(8,128)} fusion(f32[2,4]{1,0:T(2,128)S(1)} %get-tuple-element.86, f32[2,4]{1,0:T(2,128)S(1)} %get-tuple-element.87, f32[2,4]{1,0:T(2,128)S(1)} %get-tuple-element.73, f32[2,4]{1,0:T(2,128)S(1)} %get-tuple-element.74, f32[2,4]{1,0:T(2,128)S(1)} %get-tuple-element.75, f32[2,4]{1,0:T(2,128)S(1)} %get-tuple-element.76, ...), kind=kLoop, calls=%fused_computation | loop fusion | flops 4718592 | bytes 2359808 | tf_op jit(solution)/shard_map/jit(_where)/select_n | solution.py:1128
  7.6 1.1 dynamic_update_slice.3
  8.7 0.7 reshape.9828.s_ref
  9.4 0.1 copy.38
  9.5 0.9 pad_dynamic-slice_fusion.1.k_ref
  10.4 0.4 and_or_fusion
  10.8 1.1 fusion
  11.8 1.2 broadcast_in_dim.476.n_ref
  13.1 0.2 fusion.52
  13.6 0.9 pad_maximum_fusion.r_ref
  14.4 48.8 %gather.1 = (bf16[5408,256]{1,0:T(8,128)(2,1)}, bf16[2304,768]{1,0:T(8,128)(2,1)}, f32[8,128]{1,0:T(8,128)}, bf16[464,256]{1,0:T(8,128)(2,1)}, bf16[336,256]{1,0:T(8,128)(2,1)}, /*index=5*/bf16[2,16,9216]{2,1,0:T(8,128)(2,1)}) custom-call(bf16[192,256]{1,0:T(8,128)(2,1)} %reshape.9828.s_ref, bf16[288,384]{1,0:T(8,128)(2,1)} %pad_dynamic-slice_fusion.1.k_ref, ...), custom_call_target="tpu_custom_call" | custom-call | tf_op jit(solution)/shard_map/gather/pallas_call | solution.py:999
  63.3 13.8 %stem.1 = (f32[1536,512]{1,0:T(8,128)}, bf16[1536,512]{1,0:T(8,128)(2,1)}, bf16[2,3,2304,256]{3,2,1,0:T(8,128)(2,1)}, bf16[256,256]{1,0:T(8,128)(2,1)}) custom-call(bf16[2,16,18432]{2,1,0:T(8,128)(2,1)} %x_ref.3, bf16[2,16,9216]{2,1,0:T(8,128)(2,1)} %get-tuple-element.28.h_ref, bf16[464,256]{1,0:T(8,128)(2,1)} %get-tuple-element.29.head_ref), custom_call_target="tpu_custom_call" | custom-call | tf_op jit(solution)/shard_map/stem/pallas_call | solution.py:552
  77.0 3.2 %box_in.1.wb_ref = bf16[576,256]{1,0:T(8,128)(2,1)} custom-call(bf16[336,256]{1,0:T(8,128)(2,1)} %get-tuple-element.32.tail_ref), custom_call_target="tpu_custom_call" | custom-call | tf_op jit(solution)/shard_map/box_in/pallas_call | solution.py:670
  80.2 1.2 slice.129
  82.8 0.6 pad_maximum_fusion.1.scal_ref
  83.4 0.7 convert_bitcast_fusion
  84.0 0.6 copy.48
  84.7 0.4 compare_and_fusion.54
  85.1 0.4 compare_and_fusion.55
  85.5 0.6 compare_and_fusion.60
  86.2 0.6 compare_and_fusion.62
  86.8 0.2 compare_and_fusion.64
  87.1 0.3 stack.36
  87.4 0.7 pad_convert_fusion.mk_ref
  88.0 0.4 slice_reduce_fusion.33
  88.5 1.1 select_convert_fusion.lab_ref
  89.7 0.6 copy.51
  90.3 129.2 %heads.1 = (bf16[2304,768]{1,0:T(8,128)(2,1)}, bf16[4608,256]{1,0:T(8,128)(2,1)}, f32[576,256]{1,0:T(8,128)}, f32[1,512]{1,0:T(1,128)}, f32[2,2,1536,128]{3,2,1,0:T(8,128)}, /*index=5*/f32[16,256]{1,0:T(8,128)}) custom-call(f32[2]{0:T(128)} %pad_maximum_fusion.1.scal_ref, bf16[2,3,2304,256]{3,2,1,0:T(8,128)(2,1)} %get-tuple-element.30.f_ref, ...), custom_call_target="tpu_custom_call" | custom-call | tf_op jit(solution)/shard_map/heads/pallas_call | solution.py:694
  219.5 3.0 %box_out.1.tail_ref = bf16[336,256]{1,0:T(8,128)(2,1)} custom-call(f32[576,256]{1,0:T(8,128)} %get-tuple-element.39.w_ref, f32[1,512]{1,0:T(1,128)} %get-tuple-element.40.b_ref), custom_call_target="tpu_custom_call" | custom-call | tf_op jit(solution)/shard_map/box_out/pallas_call | solution.py:670
  222.5 9.4 %stem_back.1.head_ref = bf16[464,256]{1,0:T(8,128)(2,1)} custom-call(bf16[2,16,18432]{2,1,0:T(8,128)(2,1)} %x_ref.3, f32[2,2,1536,128]{3,2,1,0:T(8,128)} %get-tuple-element.34.fg_ref, bf16[1536,512]{1,0:T(8,128)(2,1)} %get-tuple-element.35.so_ref, f32[1536,512]{1,0:T(8,128)} %get-tuple-element.36.pre_ref, bf16[256,256]{1,0:T(8,128)(2,1)} %get-tuple-element.37.lw_ref), custom_call_target="tpu_custom_call" | custom-call | tf_op jit(solution)/shard_map/stem_back/pallas_call | solution.py:590
  231.9 48.8 %scatter.1 = (f32[192,256]{1,0:T(8,128)}, f32[288,384]{1,0:T(8,128)}, f32[16,256]{1,0:T(8,128)}) custom-call(bf16[464,256]{1,0:T(8,128)(2,1)} %stem_back.1.head_ref, bf16[4608,256]{1,0:T(8,128)(2,1)} %get-tuple-element.38.tower_ref, bf16[336,256]{1,0:T(8,128)(2,1)} %box_out.1.tail_ref, bf16[2304,768]{1,0:T(8,128)(2,1)} %get-tuple-element.41.k_ref, ...), custom_call_target="tpu_custom_call" | custom-call | tf_op jit(solution)/shard_map/scatter/pallas_call | solution.py:1037
  280.7 1.2 dynamic-slice_bitcast_fusion
  281.9 0.1 copy.40
  282.1 0.1 copy.41
  282.2 0.1 copy.43
  282.4 0.2 multiply_subtract_fusion
  282.6 0.9 copy.44
  283.5 0.9 copy.45
  284.4 0.9 copy.46
  285.3 1.0 multiply_subtract_fusion.1
  286.3 0.7 slice_reduce_fusion
  (45 shorter events, 0.8 us)
Async XLA Ops:
  3.4 0.7 copy-start.3
  4.3 3.3 %copy-start.4 = (f32[43072]{0:T(1024)S(1)}, f32[43072]{0:T(1024)}, u32[]{:S(2)}) copy-start(f32[43072]{0:T(1024)} %param.18) | copy-start | bytes 516868
  4.3 5.0 %copy-start.2 = (f32[288,180]{0,1:T(8,128)S(1)}, f32[288,180]{0,1:T(8,128)}, u32[]{:S(2)}) copy-start(f32[288,180]{0,1:T(8,128)} %param.21) | copy-start | bytes 622084
  7.6 3.2 %copy-start.1 = (s32[2,9,6144]{2,0,1:T(2,128)S(1)}, s32[2,9,6144]{2,0,1:T(2,128)}, u32[]{:S(2)}) copy-start(s32[2,9,6144]{2,0,1:T(2,128)} %param.14) | copy-start | bytes 1327108
  7.6 5.5 %copy-start = (bf16[2,16,18432]{2,1,0:T(8,128)(2,1)S(1)}, bf16[2,16,18432]{2,1,0:T(8,128)(2,1)}, u32[]{:S(2)}) copy-start(bf16[2,16,18432]{2,1,0:T(8,128)(2,1)} %x_ref.3) | copy-start | bytes 3538948
  77.0 11.0 %copy-start.7 = (s32[2,16]{1,0:T(2,128)S(1)}, s32[2,16]{1,0:T(2,128)}, u32[]{:S(2)}) copy-start(s32[2,16]{1,0:T(2,128)} %param.15) | copy-start | bytes 388
  231.9 50.0 %copy-start.5 = (f32[288,180]{0,1:T(8,128)S(1)}, f32[288,180]{0,1:T(8,128)}, u32[]{:S(2)}) copy-start(f32[288,180]{0,1:T(8,128)} %param.22) | copy-start | bytes 622084
  280.7 1.4 copy-start.6
  282.6 2.6 copy-start.8
  282.6 2.7 copy-start.9
  282.6 2.7 copy-start.10
  284.4 2.0 copy-start.11

commit v6 on v5

--- a/solution.py
+++ b/solution.py
@@ -272,7 +272,7 @@
         zero = jnp.zeros((cols, C), BF)
         bt_ref[0:cols, :] = zero
         bt_ref[total - cols : total, :] = zero
-        piece = tower_rows // 3
+        piece = tower_rows // 2
 
         def towers(x_ref):
             def tower(i, carry):
@@ -286,7 +286,7 @@
                 bt_ref[pl.ds(at, piece), :] = out[:, C:].astype(BF)
                 return carry
 
-            lax.fori_loop(0, 3, tower, 0)
+            lax.fori_loop(0, 2, tower, 0)
 
         pl.run_scoped(towers, pltpu.VMEM((piece, 9 * C), BF))
 
@@ -429,7 +429,7 @@
     def class_back(z_ref):
         z_ref[:, 0:8, :] = jnp.zeros((3, 8, C), F32)
         z_ref[:, 8 + g_cells : 16 + g_cells, :] = jnp.zeros((3, 8, C), F32)
-        piece = g_cells // 4
+        piece = g_cells // 2
 
         def multiply(i, carry):
             row = pl.multiple_of(i * piece, 16)
@@ -445,7 +445,7 @@
                 z_ref[k, pl.ds(pl.multiple_of(8 + row, 8), piece), :] = acc
             return carry
 
-        lax.fori_loop(0, 4, multiply, 0)
+        lax.fori_loop(0, 2, multiply, 0)
 
         def collect(q, carry):
             row = pl.multiple_of(q * 256, 128)
@@ -544,7 +544,7 @@
 def stem_forward(patches, rim, head):
     canvases, rows, width = patches.shape
     cols = width // PATCH
-    pairs = 8
+    pairs = 12
     steps = cols // (2 * pairs)
     chunk = 2 * pairs * PATCH
     count = pairs * canvases * rows

time: 291 us -> 289 us (level)
  no operation moved by 1% of the time
where the time goes in v6:
time: 289 us
  Pallas kernels  254 us (88%)
  local copies, waits for them, and re-layouts  14.7 us (5%)
  other arithmetic  13.8 us (5%)
  between operations  5.95 us (2%)
    pallas_call x1, Pallas kernels, heads_call(): pl.pallas_call(functools.partial(head_kernel, cols, rows), grid=(canvases...  128 us
    pallas_call x1, Pallas kernels, gather_all(): pl.pallas_call(functools.partial(gather_kernel, shard), in_specs=[VM] * 4...  48.8 us
    pallas_call x1, Pallas kernels, scatter_all(): pl.pallas_call(functools.partial(scatter_kernel, shard), in_specs=[VM] *...  48.8 us
    pallas_call x1, Pallas kernels, stem_forward(): pl.pallas_call(functools.partial(stem_kernel, pairs, cols, rows), grid=(s...  13.2 us
    pallas_call x1, Pallas kernels, stem_backward(): pl.pallas_call(functools.partial(stem_back_kernel, pairs, cols, rows), gr...  9.42 us
    pallas_call x2, Pallas kernels, box_call(): pl.pallas_call(kernel, in_specs=[VM] * len(args), out_specs=VM, out_shape...  6.15 us

profile of v6, /device:TPU:0, one launch (start us, length us, event | category | flops | bytes accessed | tf_op | source)
XLA Modules:
  0.0 288.9 jit_solution(17367635308307011526)
XLA Ops:
  0.6 0.7 slice_bitcast_fusion.2
  1.3 0.3 slice_reduce_fusion.37
  1.7 0.2 slice_reduce_fusion.45
  1.9 0.1 fusion.43
  2.1 1.3 copy.39
  3.4 0.6 broadcast_compare_fusion.15
  4.1 0.2 slice_reduce_fusion.17
  4.3 3.2 %select_select_fusion.btt_ref = f32[2,4,16,2304]{3,2,1,0:T(8,128)} fusion(f32[2,4]{1,0:T(2,128)S(1)} %get-tuple-element.86, f32[2,4]{1,0:T(2,128)S(1)} %get-tuple-element.87, f32[2,4]{1,0:T(2,128)S(1)} %get-tuple-element.73, f32[2,4]{1,0:T(2,128)S(1)} %get-tuple-element.74, f32[2,4]{1,0:T(2,128)S(1)} %get-tuple-element.75, f32[2,4]{1,0:T(2,128)S(1)} %get-tuple-element.76, ...), kind=kLoop, calls=%fused_computation | loop fusion | flops 4718592 | bytes 2359808 | tf_op jit(solution)/shard_map/jit(_where)/select_n | solution.py:1128
  7.6 1.1 dynamic_update_slice.3
  8.7 0.7 reshape.9828.s_ref
  9.4 0.1 copy.38
  9.5 0.9 pad_dynamic-slice_fusion.1.k_ref
  10.4 0.4 and_or_fusion
  10.8 1.1 fusion
  11.8 1.2 broadcast_in_dim.476.n_ref
  13.1 0.2 fusion.52
  13.6 0.9 pad_maximum_fusion.r_ref
  14.4 48.8 %gather.1 = (bf16[5408,256]{1,0:T(8,128)(2,1)}, bf16[2304,768]{1,0:T(8,128)(2,1)}, f32[8,128]{1,0:T(8,128)}, bf16[464,256]{1,0:T(8,128)(2,1)}, bf16[336,256]{1,0:T(8,128)(2,1)}, /*index=5*/bf16[2,16,9216]{2,1,0:T(8,128)(2,1)}) custom-call(bf16[192,256]{1,0:T(8,128)(2,1)} %reshape.9828.s_ref, bf16[288,384]{1,0:T(8,128)(2,1)} %pad_dynamic-slice_fusion.1.k_ref, ...), custom_call_target="tpu_custom_call" | custom-call | tf_op jit(solution)/shard_map/gather/pallas_call | solution.py:999
  63.3 13.2 %stem.1 = (f32[1536,512]{1,0:T(8,128)}, bf16[1536,512]{1,0:T(8,128)(2,1)}, bf16[2,3,2304,256]{3,2,1,0:T(8,128)(2,1)}, bf16[256,256]{1,0:T(8,128)(2,1)}) custom-call(bf16[2,16,18432]{2,1,0:T(8,128)(2,1)} %x_ref.3, bf16[2,16,9216]{2,1,0:T(8,128)(2,1)} %get-tuple-element.28.h_ref, bf16[464,256]{1,0:T(8,128)(2,1)} %get-tuple-element.29.head_ref), custom_call_target="tpu_custom_call" | custom-call | tf_op jit(solution)/shard_map/stem/pallas_call | solution.py:552
  76.5 3.2 %box_in.1.wb_ref = bf16[576,256]{1,0:T(8,128)(2,1)} custom-call(bf16[336,256]{1,0:T(8,128)(2,1)} %get-tuple-element.32.tail_ref), custom_call_target="tpu_custom_call" | custom-call | tf_op jit(solution)/shard_map/box_in/pallas_call | solution.py:670
  79.7 1.2 slice.129
  82.2 0.6 pad_maximum_fusion.1.scal_ref
  82.8 0.7 convert_bitcast_fusion
  83.5 0.6 copy.48
  84.1 0.4 compare_and_fusion.54
  84.5 0.4 compare_and_fusion.55
  85.0 0.6 compare_and_fusion.60
  85.6 0.6 compare_and_fusion.62
  86.3 0.2 compare_and_fusion.64
  86.5 0.3 stack.36
  86.8 0.7 pad_convert_fusion.mk_ref
  87.5 0.4 slice_reduce_fusion.33
  87.9 1.1 select_convert_fusion.lab_ref
  89.2 0.6 copy.51
  89.8 128.0 %heads.1 = (bf16[2304,768]{1,0:T(8,128)(2,1)}, bf16[4608,256]{1,0:T(8,128)(2,1)}, f32[576,256]{1,0:T(8,128)}, f32[1,512]{1,0:T(1,128)}, f32[2,2,1536,128]{3,2,1,0:T(8,128)}, /*index=5*/f32[16,256]{1,0:T(8,128)}) custom-call(f32[2]{0:T(128)} %pad_maximum_fusion.1.scal_ref, bf16[2,3,2304,256]{3,2,1,0:T(8,128)(2,1)} %get-tuple-element.30.f_ref, ...), custom_call_target="tpu_custom_call" | custom-call | tf_op jit(solution)/shard_map/heads/pallas_call | solution.py:694
  217.9 3.0 %box_out.1.tail_ref = bf16[336,256]{1,0:T(8,128)(2,1)} custom-call(f32[576,256]{1,0:T(8,128)} %get-tuple-element.39.w_ref, f32[1,512]{1,0:T(1,128)} %get-tuple-element.40.b_ref), custom_call_target="tpu_custom_call" | custom-call | tf_op jit(solution)/shard_map/box_out/pallas_call | solution.py:670
  220.9 9.4 %stem_back.1.head_ref = bf16[464,256]{1,0:T(8,128)(2,1)} custom-call(bf16[2,16,18432]{2,1,0:T(8,128)(2,1)} %x_ref.3, f32[2,2,1536,128]{3,2,1,0:T(8,128)} %get-tuple-element.34.fg_ref, bf16[1536,512]{1,0:T(8,128)(2,1)} %get-tuple-element.35.so_ref, f32[1536,512]{1,0:T(8,128)} %get-tuple-element.36.pre_ref, bf16[256,256]{1,0:T(8,128)(2,1)} %get-tuple-element.37.lw_ref), custom_call_target="tpu_custom_call" | custom-call | tf_op jit(solution)/shard_map/stem_back/pallas_call | solution.py:590
  230.3 48.8 %scatter.1 = (f32[192,256]{1,0:T(8,128)}, f32[288,384]{1,0:T(8,128)}, f32[16,256]{1,0:T(8,128)}) custom-call(bf16[464,256]{1,0:T(8,128)(2,1)} %stem_back.1.head_ref, bf16[4608,256]{1,0:T(8,128)(2,1)} %get-tuple-element.38.tower_ref, bf16[336,256]{1,0:T(8,128)(2,1)} %box_out.1.tail_ref, bf16[2304,768]{1,0:T(8,128)(2,1)} %get-tuple-element.41.k_ref, ...), custom_call_target="tpu_custom_call" | custom-call | tf_op jit(solution)/shard_map/scatter/pallas_call | solution.py:1037
  279.1 1.2 dynamic-slice_bitcast_fusion
  280.3 0.1 copy.40
  280.4 0.1 copy.41
  280.6 0.1 copy.43
  280.7 0.2 multiply_subtract_fusion
  281.0 0.9 copy.44
  281.8 0.9 copy.45
  282.7 0.9 copy.46
  283.7 1.0 multiply_subtract_fusion.1
  284.7 0.7 slice_reduce_fusion
  (45 shorter events, 0.8 us)
Async XLA Ops:
  3.4 0.7 copy-start.3
  4.3 3.3 %copy-start.4 = (f32[43072]{0:T(1024)S(1)}, f32[43072]{0:T(1024)}, u32[]{:S(2)}) copy-start(f32[43072]{0:T(1024)} %param.18) | copy-start | bytes 516868
  4.3 5.0 %copy-start.2 = (f32[288,180]{0,1:T(8,128)S(1)}, f32[288,180]{0,1:T(8,128)}, u32[]{:S(2)}) copy-start(f32[288,180]{0,1:T(8,128)} %param.21) | copy-start | bytes 622084
  7.6 3.2 %copy-start.1 = (s32[2,9,6144]{2,0,1:T(2,128)S(1)}, s32[2,9,6144]{2,0,1:T(2,128)}, u32[]{:S(2)}) copy-start(s32[2,9,6144]{2,0,1:T(2,128)} %param.14) | copy-start | bytes 1327108
  7.6 5.5 %copy-start = (bf16[2,16,18432]{2,1,0:T(8,128)(2,1)S(1)}, bf16[2,16,18432]{2,1,0:T(8,128)(2,1)}, u32[]{:S(2)}) copy-start(bf16[2,16,18432]{2,1,0:T(8,128)(2,1)} %x_ref.3) | copy-start | bytes 3538948
  76.5 11.0 %copy-start.7 = (s32[2,16]{1,0:T(2,128)S(1)}, s32[2,16]{1,0:T(2,128)}, u32[]{:S(2)}) copy-start(s32[2,16]{1,0:T(2,128)} %param.15) | copy-start | bytes 388
  230.3 50.0 %copy-start.5 = (f32[288,180]{0,1:T(8,128)S(1)}, f32[288,180]{0,1:T(8,128)}, u32[]{:S(2)}) copy-start(f32[288,180]{0,1:T(8,128)} %param.22) | copy-start | bytes 622084
  279.0 1.4 copy-start.6
  280.9 2.6 copy-start.8
  281.0 2.7 copy-start.9
  281.0 2.7 copy-start.10
  282.7 2.0 copy-start.11

commit v7 on v6

--- a/solution.py
+++ b/solution.py
@@ -470,7 +470,7 @@
         lax.fori_loop(0, own // 256, flip, 0)
         weight_sums(pl.program_id(0), cols, edge, own, lambda: gt_ref[...], f_ref.at[0], mx_ref, dwt_ref)
         first_z = edge - 16
-        piece = (own + 32) // 2
+        piece = own + 32
 
         def multiply(i, carry):
             row = pl.multiple_of(i * piece, 16)
@@ -486,7 +486,7 @@
                 z_ref[k, pl.ds(row, piece), :] = acc
             return carry
 
-        lax.fori_loop(0, 2, multiply, 0)
+        lax.fori_loop(0, 1, multiply, 0)
 
         def collect(q, carry):
             row = pl.multiple_of(q * 256, 128)

time: 289 us -> 289 us (level)
  no operation moved by 1% of the time
where the time goes in v7:
time: 289 us; the launch traced here: 288 us
  Pallas kernels  254 us (88%)
  local copies, waits for them, and re-layouts  14.7 us (5%)
  other arithmetic  13.8 us (5%)
  between operations  5.95 us (2%)
    pallas_call x1, Pallas kernels, heads_call(): pl.pallas_call(functools.partial(head_kernel, cols, rows), grid=(canvases...  128 us
    pallas_call x1, Pallas kernels, gather_all(): pl.pallas_call(functools.partial(gather_kernel, shard), in_specs=[VM] * 4...  48.8 us
    pallas_call x1, Pallas kernels, scatter_all(): pl.pallas_call(functools.partial(scatter_kernel, shard), in_specs=[VM] *...  48.8 us
    pallas_call x1, Pallas kernels, stem_forward(): pl.pallas_call(functools.partial(stem_kernel, pairs, cols, rows), grid=(s...  13.2 us
    pallas_call x1, Pallas kernels, stem_backward(): pl.pallas_call(functools.partial(stem_back_kernel, pairs, cols, rows), gr...  9.42 us
    pallas_call x2, Pallas kernels, box_call(): pl.pallas_call(kernel, in_specs=[VM] * len(args), out_specs=VM, out_shape...  6.15 us

profile of v7, /device:TPU:0, one launch (start us, length us, event | category | flops | bytes accessed | tf_op | source)
XLA Modules:
  0.0 288.4 jit_solution(9009149071268958808)
XLA Ops:
  0.6 0.7 slice_bitcast_fusion.2
  1.3 0.3 slice_reduce_fusion.37
  1.7 0.2 slice_reduce_fusion.45
  1.9 0.1 fusion.43
  2.1 1.3 copy.39
  3.4 0.6 broadcast_compare_fusion.15
  4.1 0.2 slice_reduce_fusion.17
  4.3 3.2 %select_select_fusion.btt_ref = f32[2,4,16,2304]{3,2,1,0:T(8,128)} fusion(f32[2,4]{1,0:T(2,128)S(1)} %get-tuple-element.86, f32[2,4]{1,0:T(2,128)S(1)} %get-tuple-element.87, f32[2,4]{1,0:T(2,128)S(1)} %get-tuple-element.73, f32[2,4]{1,0:T(2,128)S(1)} %get-tuple-element.74, f32[2,4]{1,0:T(2,128)S(1)} %get-tuple-element.75, f32[2,4]{1,0:T(2,128)S(1)} %get-tuple-element.76, ...), kind=kLoop, calls=%fused_computation | loop fusion | flops 4718592 | bytes 2359808 | tf_op jit(solution)/shard_map/jit(_where)/select_n | solution.py:1128
  7.6 1.1 dynamic_update_slice.3
  8.7 0.7 reshape.9828.s_ref
  9.4 0.1 copy.38
  9.5 0.9 pad_dynamic-slice_fusion.1.k_ref
  10.4 0.4 and_or_fusion
  10.8 1.1 fusion
  11.8 1.2 broadcast_in_dim.476.n_ref
  13.1 0.2 fusion.52
  13.6 0.9 pad_maximum_fusion.r_ref
  14.4 48.8 %gather.1 = (bf16[5408,256]{1,0:T(8,128)(2,1)}, bf16[2304,768]{1,0:T(8,128)(2,1)}, f32[8,128]{1,0:T(8,128)}, bf16[464,256]{1,0:T(8,128)(2,1)}, bf16[336,256]{1,0:T(8,128)(2,1)}, /*index=5*/bf16[2,16,9216]{2,1,0:T(8,128)(2,1)}) custom-call(bf16[192,256]{1,0:T(8,128)(2,1)} %reshape.9828.s_ref, bf16[288,384]{1,0:T(8,128)(2,1)} %pad_dynamic-slice_fusion.1.k_ref, ...), custom_call_target="tpu_custom_call" | custom-call | tf_op jit(solution)/shard_map/gather/pallas_call | solution.py:999
  63.3 13.2 %stem.1 = (f32[1536,512]{1,0:T(8,128)}, bf16[1536,512]{1,0:T(8,128)(2,1)}, bf16[2,3,2304,256]{3,2,1,0:T(8,128)(2,1)}, bf16[256,256]{1,0:T(8,128)(2,1)}) custom-call(bf16[2,16,18432]{2,1,0:T(8,128)(2,1)} %x_ref.3, bf16[2,16,9216]{2,1,0:T(8,128)(2,1)} %get-tuple-element.28.h_ref, bf16[464,256]{1,0:T(8,128)(2,1)} %get-tuple-element.29.head_ref), custom_call_target="tpu_custom_call" | custom-call | tf_op jit(solution)/shard_map/stem/pallas_call | solution.py:552
  76.5 3.2 %box_in.1.wb_ref = bf16[576,256]{1,0:T(8,128)(2,1)} custom-call(bf16[336,256]{1,0:T(8,128)(2,1)} %get-tuple-element.32.tail_ref), custom_call_target="tpu_custom_call" | custom-call | tf_op jit(solution)/shard_map/box_in/pallas_call | solution.py:670
  79.7 1.2 slice.129
  82.2 0.6 pad_maximum_fusion.1.scal_ref
  82.8 0.7 convert_bitcast_fusion
  83.5 0.6 copy.48
  84.1 0.4 compare_and_fusion.54
  84.5 0.4 compare_and_fusion.55
  85.0 0.6 compare_and_fusion.60
  85.6 0.6 compare_and_fusion.62
  86.3 0.2 compare_and_fusion.64
  86.5 0.3 stack.36
  86.8 0.7 pad_convert_fusion.mk_ref
  87.5 0.4 slice_reduce_fusion.33
  87.9 1.1 select_convert_fusion.lab_ref
  89.2 0.6 copy.51
  89.8 127.6 %heads.1 = (bf16[2304,768]{1,0:T(8,128)(2,1)}, bf16[4608,256]{1,0:T(8,128)(2,1)}, f32[576,256]{1,0:T(8,128)}, f32[1,512]{1,0:T(1,128)}, f32[2,2,1536,128]{3,2,1,0:T(8,128)}, /*index=5*/f32[16,256]{1,0:T(8,128)}) custom-call(f32[2]{0:T(128)} %pad_maximum_fusion.1.scal_ref, bf16[2,3,2304,256]{3,2,1,0:T(8,128)(2,1)} %get-tuple-element.30.f_ref, ...), custom_call_target="tpu_custom_call" | custom-call | tf_op jit(solution)/shard_map/heads/pallas_call | solution.py:694
  217.4 3.0 %box_out.1.tail_ref = bf16[336,256]{1,0:T(8,128)(2,1)} custom-call(f32[576,256]{1,0:T(8,128)} %get-tuple-element.39.w_ref, f32[1,512]{1,0:T(1,128)} %get-tuple-element.40.b_ref), custom_call_target="tpu_custom_call" | custom-call | tf_op jit(solution)/shard_map/box_out/pallas_call | solution.py:670
  220.4 9.4 %stem_back.1.head_ref = bf16[464,256]{1,0:T(8,128)(2,1)} custom-call(bf16[2,16,18432]{2,1,0:T(8,128)(2,1)} %x_ref.3, f32[2,2,1536,128]{3,2,1,0:T(8,128)} %get-tuple-element.34.fg_ref, bf16[1536,512]{1,0:T(8,128)(2,1)} %get-tuple-element.35.so_ref, f32[1536,512]{1,0:T(8,128)} %get-tuple-element.36.pre_ref, bf16[256,256]{1,0:T(8,128)(2,1)} %get-tuple-element.37.lw_ref), custom_call_target="tpu_custom_call" | custom-call | tf_op jit(solution)/shard_map/stem_back/pallas_call | solution.py:590
  229.8 48.8 %scatter.1 = (f32[192,256]{1,0:T(8,128)}, f32[288,384]{1,0:T(8,128)}, f32[16,256]{1,0:T(8,128)}) custom-call(bf16[464,256]{1,0:T(8,128)(2,1)} %stem_back.1.head_ref, bf16[4608,256]{1,0:T(8,128)(2,1)} %get-tuple-element.38.tower_ref, bf16[336,256]{1,0:T(8,128)(2,1)} %box_out.1.tail_ref, bf16[2304,768]{1,0:T(8,128)(2,1)} %get-tuple-element.41.k_ref, ...), custom_call_target="tpu_custom_call" | custom-call | tf_op jit(solution)/shard_map/scatter/pallas_call | solution.py:1037
  278.6 1.2 dynamic-slice_bitcast_fusion
  279.8 0.1 copy.40
  280.0 0.1 copy.41
  280.1 0.1 copy.43
  280.2 0.2 multiply_subtract_fusion
  280.5 0.9 copy.44
  281.4 0.9 copy.45
  282.2 0.9 copy.46
  283.2 1.0 multiply_subtract_fusion.1
  284.2 0.7 slice_reduce_fusion
  (45 shorter events, 0.8 us)
Async XLA Ops:
  3.4 0.7 copy-start.3
  4.3 3.3 %copy-start.4 = (f32[43072]{0:T(1024)S(1)}, f32[43072]{0:T(1024)}, u32[]{:S(2)}) copy-start(f32[43072]{0:T(1024)} %param.18) | copy-start | bytes 516868
  4.3 5.0 %copy-start.2 = (f32[288,180]{0,1:T(8,128)S(1)}, f32[288,180]{0,1:T(8,128)}, u32[]{:S(2)}) copy-start(f32[288,180]{0,1:T(8,128)} %param.21) | copy-start | bytes 622084
  7.6 3.2 %copy-start.1 = (s32[2,9,6144]{2,0,1:T(2,128)S(1)}, s32[2,9,6144]{2,0,1:T(2,128)}, u32[]{:S(2)}) copy-start(s32[2,9,6144]{2,0,1:T(2,128)} %param.14) | copy-start | bytes 1327108
  7.6 5.5 %copy-start = (bf16[2,16,18432]{2,1,0:T(8,128)(2,1)S(1)}, bf16[2,16,18432]{2,1,0:T(8,128)(2,1)}, u32[]{:S(2)}) copy-start(bf16[2,16,18432]{2,1,0:T(8,128)(2,1)} %x_ref.3) | copy-start | bytes 3538948
  76.5 11.0 %copy-start.7 = (s32[2,16]{1,0:T(2,128)S(1)}, s32[2,16]{1,0:T(2,128)}, u32[]{:S(2)}) copy-start(s32[2,16]{1,0:T(2,128)} %param.15) | copy-start | bytes 388
  229.8 50.0 %copy-start.5 = (f32[288,180]{0,1:T(8,128)S(1)}, f32[288,180]{0,1:T(8,128)}, u32[]{:S(2)}) copy-start(f32[288,180]{0,1:T(8,128)} %param.22) | copy-start | bytes 622084
  278.6 1.4 copy-start.6
  280.5 2.6 copy-start.8
  280.5 2.7 copy-start.9
  280.5 2.7 copy-start.10
  282.2 2.0 copy-start.11
